TPU v7x, 128 devices: a whole 4x4x4 slice. The times are simulated.
128 devices in a mesh: seq: 32 (over x_hi, z, y), row: 4 (over x_lo, core).
Axes of the slice: x: 4 (x_hi: 2, x_lo: 2; x = x_hi * 2 + x_lo), y: 4, z: 4, core: 2. Of those that a mesh axis runs over, the one named last changes fastest.
Arguments:
- activations: bfloat16 [256, 256, 1024], P('seq', 'row'), may hold values from -6 to 6
- noise_embed: bfloat16 [256, 1024], P('seq'), may hold values from -6 to 6
- frame_position: int32 [256], P('seq'), may hold values from 0 to 7, as said below
- cotangent: bfloat16 [256, 256, 1024], P('seq', 'row'), may hold values from -6 to 6
- ada_weight: bfloat16 [1024, 6144], P('row'), may hold values from -0.1875 to 0.1875
- ada_bias: bfloat16 [6144], P('row'), may hold values from -3 to 3
- qkv_weight: bfloat16 [1024, 3072], P('row'), may hold values from -0.1875 to 0.1875
- qkv_bias: bfloat16 [3072], P('row'), may hold values from -3 to 3
- out_weight: bfloat16 [1024, 1024], P('row'), may hold values from -0.75 to 0.75
- out_bias: bfloat16 [1024], P('row'), may hold values from -3 to 3
- up_weight: bfloat16 [1024, 4096], P('row'), may hold values from -0.1875 to 0.1875
- up_bias: bfloat16 [4096], P('row'), may hold values from -3 to 3
- down_weight: bfloat16 [4096, 1024], P('row'), may hold values from -0.09375 to 0.09375
- down_bias: bfloat16 [1024], P('row'), may hold values from -3 to 3
Outputs:
- layer_output: bfloat16 [256, 256, 1024], P('seq', 'row')
- input_grad: float32 [256, 256, 1024], P('seq', 'row')
- embed_grad: float32 [256, 1024], P('seq')
- ada_weight_grad: float32 [1024, 6144], P('row')
- ada_bias_grad: float32 [6144], P('row')
- qkv_weight_grad: float32 [1024, 3072], P('row')
- qkv_bias_grad: float32 [3072], P('row')
- out_weight_grad: float32 [1024, 1024], P('row')
- out_bias_grad: float32 [1024], P('row')
- up_weight_grad: float32 [1024, 4096], P('row')
- up_bias_grad: float32 [4096], P('row')
- down_weight_grad: float32 [4096, 1024], P('row')
- down_bias_grad: float32 [1024], P('row')
Inputs may be any that keep to these rules, and one draw needn't show every extreme that they name: frame_position[f] is the place of frame f in its clip: 0 where a clip begins, else one more than at frame f - 1; a clip holds 1 to 8 frames, and frames 0 to 7 form one clip.
All inputs are finite; a program needn't handle non-finite values.
Results may differ from a plain program's by a relative error of at most 0.028.
The roundings to bfloat16 on the way count: a program that leaves them out, or rounds other values in their place, can miss the bound.
Values may be sent and summed in bfloat16 or wider, within the bound.
No kernel may reach another device: no remote copies, remote signals or barrier semaphores. Data moves between devices by JAX's collectives and lax.ppermute only.
A program may use at most 320 MiB of HBM per device.

v0:
```python
import math

import jax
import jax.numpy as jnp
from jax import lax
from jax.experimental import pallas as pl
from jax.experimental.pallas import tpu as pltpu
from jax.sharding import Mesh, PartitionSpec as P

F32 = jnp.float32
BF16 = jnp.bfloat16
HD = 64
GRID = 16
FPD = 8
PR = 64
D = 1024
FF = 4096
HC = 256
TOK = 256
PREV = 7
AXES = ("xh", "z", "y", "xl", "c")
CORE, DIRECT, OTHER, FAR = 1, 2, 66, 64
MB = 1024 * 1024


def swap(value, mask):
    return lax.ppermute(value, AXES, [(i, i ^ mask) for i in range(128)])


def shift(value, steps):
    return lax.ppermute(value, AXES, [(i, (i + 4 * steps) % 128) for i in range(128)])


def after(value, *others):
    return lax.optimization_barrier((value,) + others)[0]


def nt(left, right):
    return lax.dot_general(left, right, (((1,), (1,)), ((), ())), preferred_element_type=F32)


def tn(left, right):
    return lax.dot_general(left, right, (((0,), (0,)), ((), ())), preferred_element_type=F32)


def nn(left, right):
    return jnp.dot(left, right, preferred_element_type=F32)


def norm(values):
    center = values - jnp.mean(values, axis=-1, keepdims=True)
    spread = jnp.mean(center * center, axis=-1, keepdims=True)
    rate = lax.rsqrt(spread + 1e-06)
    return center * rate, rate


def norm_back(normal, rate, grad):
    mean_grad = jnp.mean(grad, axis=-1, keepdims=True)
    mean_both = jnp.mean(grad * normal, axis=-1, keepdims=True)
    return rate * (grad - mean_grad - normal * mean_both)


def turn(values, cosine, sine):
    lanes = lax.broadcasted_iota(jnp.int32, values.shape, 1)
    other = jnp.where(
        lanes % HD < HD // 2, pltpu.roll(values, HC - HD // 2, 1), pltpu.roll(values, HD // 2, 1)
    )
    return values * cosine + other * sine


def params(mib):
    return pltpu.CompilerParams(vmem_limit_bytes=mib * MB)


def cost(flops, moved, exps=0):
    return pl.CostEstimate(flops=int(flops), bytes_accessed=int(moved), transcendentals=int(exps))


def whole(shape):
    return pl.BlockSpec(shape, lambda i, *_: (0,) * len(shape))


def columns(row, j):
    return pl.ds(pl.multiple_of((row ^ j) * HC, HC), HC)


def shape(dims, kind=BF16):
    return jax.ShapeDtypeStruct(dims, kind)


UB, QB, OB, DB, WIDE = 6144, 6656, 7168, 7296, 7424


def put(ref, start, at, value):
    cols = slice(start, start + value.shape[1])
    number = lax.broadcasted_iota(jnp.int32, (8, value.shape[1]), 0)
    ref[:, cols] = jnp.where(number == at, value, ref[:, cols])


def take(value, at):
    number = lax.broadcasted_iota(jnp.int32, value.shape, 0)
    return jnp.sum(jnp.where(number == at, value, 0.0), axis=0, keepdims=True)


def put_half(ref, start, value):
    cols = slice(start, start + value.shape[1])
    number = lax.broadcasted_iota(jnp.int32, (8, value.shape[1]), 0)
    both = jnp.concatenate([value, value], axis=0)
    ref[:, cols] = jnp.where(number // 4 == pl.program_id(0), both, ref[:, cols])


def unfold(ref, start, width):
    return jnp.concatenate([ref[i : i + 1, start : start + width] for i in range(8)], axis=1)


def prepare_kernel(row_ref, pos_ref, noise, ada, ab, qb, ob, ub, db, pack, silu, cp, sp, frames):
    row = row_ref[0]
    embed = noise[...].astype(F32)
    value = (embed / (1.0 + jnp.exp(-embed))).astype(BF16)
    own = jnp.where(
        row < 2,
        jnp.where(row == 0, value[:, :HC], value[:, HC : 2 * HC]),
        jnp.where(row == 2, value[:, 2 * HC : 3 * HC], value[:, 3 * HC :]),
    )
    silu[...] = own
    pack[:, UB:] = jnp.zeros((FPD, WIDE - UB), F32)
    for segment in range(6):
        cols = slice(segment * D, (segment + 1) * D)
        pack[:, cols] = nn(own, ada[:, cols])
    bias = pl.ds(pl.multiple_of(row * 1536, 512), 1536)
    pack[:, bias] = pack[:, bias] + ab[...].astype(F32)
    for i in range(2):
        at = 2 * row + i
        put(pack, UB, at, ub[:, i * 512 : (i + 1) * 512].astype(F32))
        put(pack, OB, at, ob[:, i * 128 : (i + 1) * 128].astype(F32))
        put(pack, DB, at, db[:, i * 128 : (i + 1) * 128].astype(F32))
    for i in range(3):
        chunk = 3 * row + i
        at = jnp.where(chunk < 4, chunk, chunk - 4)
        second = (chunk >= 4) & (chunk < 8)
        value = qb[:, i * HC : (i + 1) * HC].astype(F32)
        put(pack, QB, jnp.where(second, -1, at), value)
        put(pack, QB + HC, jnp.where(second, at, -1), value)

    def parts(dims):
        lane = lax.broadcasted_iota(jnp.int32, dims, 1)
        index = lane % (HD // 2)
        quarter, eighth = HD // 4, HD // 8
        in_frame = index < quarter
        in_row = (index >= quarter) & (index < quarter + eighth)
        offset = jnp.where(
            in_frame, index, jnp.where(in_row, index - quarter, index - quarter - eighth)
        ).astype(F32)
        length = jnp.where(in_frame, 1.0 * quarter, 1.0 * eighth)
        frequency = jnp.exp(-math.log(10000.0) * offset / length)
        sign = jnp.where(lane % HD < HD // 2, -1.0, 1.0)
        return in_frame, in_row, frequency, sign

    in_frame, in_row, frequency, sign = parts((TOK, HC))
    slot = lax.broadcasted_iota(jnp.int32, (TOK, HC), 0)
    patch = ((slot // PR) ^ row) * PR + slot % PR
    angle = jnp.where(in_row, patch // GRID, patch % GRID).astype(F32) * frequency
    cp[...] = jnp.where(in_frame, 0.0, jnp.cos(angle))
    sp[...] = jnp.where(in_frame, 0.0, jnp.sin(angle) * sign)
    in_frame, _, frequency, sign = parts((16, HC))
    slot = lax.broadcasted_iota(jnp.int32, (16, HC), 0)
    place = pos_ref[0] - PREV + (slot - FPD)
    for f in range(FPD):
        place = jnp.where(slot == f, pos_ref[f], place)
    angle = place.astype(F32) * frequency
    frames[:, :HC] = jnp.where(in_frame, jnp.cos(angle), 0.0)
    frames[:, HC:] = jnp.where(in_frame, jnp.sin(angle) * sign, 0.0)


def prepare(row, places, noise, ada, biases):
    return pl.pallas_call(
        prepare_kernel,
        out_shape=[
            shape((FPD, WIDE), F32),
            shape((FPD, HC)),
            shape((TOK, HC), F32),
            shape((TOK, HC), F32),
            shape((16, 2 * HC), F32),
        ],
        grid_spec=pltpu.PrefetchScalarGridSpec(
            num_scalar_prefetch=2,
            grid=(1,),
            in_specs=[whole((FPD, D)), whole((HC, 6 * D))]
            + [whole((1, b.shape[0])) for b in biases],
            out_specs=[
                whole((FPD, WIDE)),
                whole((FPD, HC)),
                whole((TOK, HC)),
                whole((TOK, HC)),
                whole((16, 2 * HC)),
            ],
        ),
        compiler_params=params(24),
        cost_estimate=cost(2 * 8 * HC * 6 * D, 4 * MB, 4 * TOK * HC),
        name="prepare",
    )(row, places, noise, ada, *[b[None] for b in biases])


def split_heads_kernel(row_ref, q, k, v, p0, p1, p2, p3):
    for j, p in enumerate((p0, p1, p2, p3)):

        @pl.when(pl.program_id(0) == j)
        def _():
            p[:, :HC] = q[...]
            p[:, HC : 2 * HC] = k[...]
            p[:, 2 * HC :] = v[...]


def split_heads(row, weight):
    return pl.pallas_call(
        split_heads_kernel,
        out_shape=[shape((HC, 3 * HC))] * 4,
        grid_spec=pltpu.PrefetchScalarGridSpec(
            num_scalar_prefetch=1,
            grid=(4,),
            in_specs=[
                pl.BlockSpec((HC, HC), lambda j, row, s=s: (0, 4 * s + (row[0] ^ j)))
                for s in range(3)
            ],
            out_specs=[whole((HC, 3 * HC))] * 4,
        ),
        compiler_params=params(12),
        cost_estimate=cost(0, 3 * MB),
        name="split_heads",
    )(row, weight, weight, weight)


def cosines(cp, sp, frames, at):
    both = frames[pl.ds(at, 1), :]
    return cp[...] + both[:, :HC], sp[...] + both[:, HC:]


def project_kernel(own, row_ref, x0, x1, x2, x3, table, mods, w0, w1, w2, w3, cp, sp, fr, *outs):
    row = row_ref[0]
    f = pl.program_id(0)
    if own:
        h_ref, q_ref, k_ref, v_ref = outs
        first, at, angle = 0, f, f
    else:
        k_ref, v_ref, h_ref = outs
        first, at, angle = HC, f + FPD - PREV, f + FPD
    x = jnp.concatenate([r[0] for r in (x0, x1, x2, x3)], axis=0).astype(F32)
    normal, _ = norm(x)
    shift_row = mods[pl.ds(at, 1), :D]
    scale_row = mods[pl.ds(at, 1), D : 2 * D]
    hidden = (normal * (1.0 + scale_row) + shift_row).astype(BF16)
    where = (0,) if own else ()
    h_ref[where + (slice(None), slice(None))] = hidden
    low, high = table[pl.ds(row, 1), QB : QB + 2 * HC], table[pl.ds(row + 4, 1), QB : QB + HC]
    total = jnp.concatenate([low, high], axis=1)[:, first:]
    for j, w in enumerate((w0, w1, w2, w3)):
        total = total + nn(h_ref[where + (slice(None), columns(row, j))], w[:, first:])
    cosine, sine = cosines(cp, sp, fr, angle)
    if own:
        q_ref[0] = (turn(total[:, :HC], cosine, sine).astype(BF16).astype(F32) * 0.125).astype(BF16)
        total = total[:, HC:]
    k_ref[0] = turn(total[:, :HC], cosine, sine).astype(BF16)
    v_ref[0] = total[:, HC:].astype(BF16)


def project(own, row, xs, table, mods, weights, tables):
    frames = xs[0].shape[0]
    x_spec = pl.BlockSpec((1, PR, D), lambda f, *_: (f, 0, 0))
    out_spec = pl.BlockSpec((1, TOK, HC), lambda f, *_: (f, 0, 0))
    out = shape((frames, TOK, HC))
    if own:
        out_specs = [pl.BlockSpec((1, TOK, D), lambda f, *_: (f, 0, 0)), out_spec, out_spec, out_spec]
        out_shape = [shape((frames, TOK, D)), out, out, out]
        scratch = []
    else:
        out_specs = [out_spec, out_spec]
        out_shape = [out, out]
        scratch = [pltpu.VMEM((TOK, D), BF16)]
    return pl.pallas_call(
        lambda *refs: project_kernel(own, *refs),
        out_shape=out_shape,
        grid_spec=pltpu.PrefetchScalarGridSpec(
            num_scalar_prefetch=1,
            grid=(frames,),
            in_specs=[x_spec] * 4
            + [whole((FPD, WIDE)), whole(mods.shape)]
            + [whole((HC, 3 * HC))] * 4
            + [whole((TOK, HC)), whole((TOK, HC)), whole((16, 2 * HC))],
            out_specs=out_specs,
            scratch_shapes=scratch,
        ),
        compiler_params=params(20),
        cost_estimate=cost(2 * frames * TOK * D * 3 * HC, frames * TOK * D * 4 + 4 * MB),
        name="project_own" if own else "project_prev",
    )(row, *xs, table, mods, *weights, *tables)


def head_lanes():
    return lax.broadcasted_iota(jnp.int32, (TOK, HC), 1) // HD


def attend_kernel(pos_ref, q, k, v, kp, vp, o0, o1, o23, lse, qs, scores, acc, top, low):
    f = pl.program_id(0)
    place = pos_ref[f]
    lanes = head_lanes()
    query = q[0]
    for h in range(4):
        qs[pl.ds(h * TOK, TOK), :] = jnp.where(lanes == h, query, jnp.zeros_like(query))
    top[...] = jnp.full_like(top, -1e30)
    low[...] = jnp.zeros_like(low)
    acc[...] = jnp.zeros_like(acc)
    before = jnp.maximum(place - f, 0)
    start = jnp.maximum(f - place, 0)

    def score(keys, slot):
        for h in range(4):
            rows = pl.ds(h * TOK, TOK)
            s = nt(qs[rows, :], keys)
            scores[slot, rows, :] = s
            top[rows, :] = jnp.maximum(top[rows, :], jnp.maximum(s[:, :128], s[:, 128:]))

    def mix(values, slot):
        for h in range(4):
            rows = pl.ds(h * TOK, TOK)
            p = jnp.exp(scores[slot, rows, :] - jnp.concatenate([top[rows, :]] * 2, axis=1))
            low[rows, :] = low[rows, :] + (p[:, :128] + p[:, 128:])
            acc[rows, :] = acc[rows, :] + nn(p.astype(BF16), values)

    def run(step):
        def prev(i, _):
            at = PREV - before + i
            step(kp[at] if step is score else vp[at], i)
            return 0

        def own(g, _):
            step(k[g] if step is score else v[g], g - f + place)
            return 0

        lax.fori_loop(0, before, prev, 0)
        lax.fori_loop(start, f + 1, own, 0)

    run(score)
    for h in range(4):
        rows = pl.ds(h * TOK, TOK)
        top[rows, :] = jnp.broadcast_to(jnp.max(top[rows, :], axis=1, keepdims=True), (TOK, 128))
    run(mix)
    result = jnp.zeros((TOK, HC), F32)
    logs = jnp.zeros((TOK, 128), F32)
    narrow = lax.broadcasted_iota(jnp.int32, (TOK, 128), 1)
    for h in range(4):
        rows = pl.ds(h * TOK, TOK)
        total = jnp.sum(low[rows, :], axis=1, keepdims=True)
        result = jnp.where(lanes == h, acc[rows, :] / total, result)
        logs = jnp.where(narrow == h, top[rows, :] + jnp.log(total), logs)
    lse[0] = logs.T[:8]
    result = result.astype(BF16)
    o0[0] = result[:PR]
    o1[0] = result[PR : 2 * PR]
    o23[0, 0] = result[2 * PR : 3 * PR]
    o23[1, 0] = result[3 * PR :]


def attend(places, q, k, v, kp, vp):
    block = pl.BlockSpec((1, TOK, HC), lambda f, *_: (f, 0, 0))
    piece = pl.BlockSpec((1, PR, HC), lambda f, *_: (f, 0, 0))
    return pl.pallas_call(
        attend_kernel,
        out_shape=[shape((FPD, PR, HC))] * 2
        + [shape((2, FPD, PR, HC)), shape((FPD, 8, TOK), F32)],
        grid_spec=pltpu.PrefetchScalarGridSpec(
            num_scalar_prefetch=1,
            grid=(FPD,),
            in_specs=[block]
            + [whole((FPD, TOK, HC))] * 2
            + [whole((PREV, TOK, HC))] * 2,
            out_specs=[piece] * 2
            + [
                pl.BlockSpec((2, 1, PR, HC), lambda f, *_: (0, f, 0, 0)),
                pl.BlockSpec((1, 8, TOK), lambda f, *_: (f, 0, 0)),
            ],
            scratch_shapes=[
                pltpu.VMEM((4 * TOK, HC), BF16),
                pltpu.VMEM((8, 4 * TOK, TOK), F32),
                pltpu.VMEM((4 * TOK, HC), F32),
                pltpu.VMEM((4 * TOK, 128), F32),
                pltpu.VMEM((4 * TOK, 128), F32),
            ],
        ),
        compiler_params=params(58),
        cost_estimate=cost(36 * 4 * 2 * 2 * TOK**3, 6 * MB, 36 * 4 * TOK * TOK),
        name="attend",
    )(places, q, k, v, kp, vp)


def attend_back_kernel(own, pos_ref, q, k, v, g0, g1, g2, g3, o0, o1, o23, lse, *rest):
    if own:
        cp, sp, fr, before_ref, dq, dk, dv, qs, gs, ks, pl_scr, dl_scr, ds_scr, dq_acc = rest
        dk_acc, dv_acc = dk, dv
    else:
        dq, both_ref, qs, gs, ks, pl_scr, dl_scr, ds_scr, dq_acc, dk_acc, dv_acc = rest
    f = pl.program_id(0)
    place = pos_ref[f]
    lanes = head_lanes()

    @pl.when(f == 0)
    def _():
        for ref in (dk_acc, dv_acc):
            ref[...] = jnp.zeros_like(ref)

    def prelude():
        query = q[0]
        grad = jnp.concatenate([r[0] for r in (g0, g1, g2, g3)], axis=0)
        mixed = jnp.concatenate([o0[0], o1[0], o23[0, 0], o23[1, 0]], axis=0)
        for h in range(4):
            rows = pl.ds(h * TOK, TOK)
            qs[rows, :] = jnp.where(lanes == h, query, jnp.zeros_like(query))
            gs[rows, :] = jnp.where(lanes == h, grad, jnp.zeros_like(grad))
        both = grad.astype(F32) * mixed.astype(F32)
        pick = (
            lax.broadcasted_iota(jnp.int32, (8, HC), 1) // HD
            == lax.broadcasted_iota(jnp.int32, (8, HC), 0)
        ).astype(F32)
        return lax.dot_general(
            pick, both, (((1,), (1,)), ((), ())),
            preferred_element_type=F32, precision=lax.Precision.HIGHEST,
        )

    def step(delta, logs, at):
        keys, values = k[at], v[at]
        for h in range(4):
            rows = pl.ds(h * TOK, TOK)
            ks[rows, :] = jnp.where(lanes == h, keys, jnp.zeros_like(keys))
            p = jnp.exp(nt(keys, qs[rows, :]) - logs[h : h + 1])
            ds = (p * (nt(values, gs[rows, :]) - delta[h : h + 1])).astype(BF16)
            pl_scr[:, rows] = p.astype(BF16)
            dl_scr[:, rows] = ds
            ds_scr[rows, :] = ds
        dv_acc[at] = dv_acc[at] + nn(pl_scr[...], gs[...])
        dk_acc[at] = dk_acc[at] + nn(dl_scr[...], qs[...])
        dq_acc[...] = dq_acc[...] + tn(ds_scr[...], ks[...])

    def sweep(low, high):
        delta = prelude()
        logs = lse[0]
        dq_acc[...] = jnp.zeros_like(dq_acc)

        def one(at, _):
            step(delta, logs, at)
            return 0

        lax.fori_loop(low, high, one, 0)

    if own:
        sweep(jnp.maximum(f - place, 0), f + 1)
        cosine, sine = cosines(cp, sp, fr, f)
        dq[0] = turn((dq_acc[...] + before_ref[0]) * 0.125, cosine, -sine).astype(BF16)
    else:
        count = jnp.maximum(place - f, 0)

        @pl.when(count > 0)
        def _():
            sweep(PREV - count, PREV)
            dq[0] = dq_acc[...]

        @pl.when(count == 0)
        def _():
            dq[0] = jnp.zeros_like(dq_acc)

        @pl.when(f == FPD - 1)
        def _():
            both_ref[0] = dk_acc[...].astype(BF16)
            both_ref[1] = dv_acc[...].astype(BF16)


def attend_back(own, places, q, k, v, grads, mixed, lse, tables=None, before=None):
    block = pl.BlockSpec((1, TOK, HC), lambda f, *_: (f, 0, 0))
    piece = pl.BlockSpec((1, PR, HC), lambda f, *_: (f, 0, 0))
    count = FPD if own else PREV
    wide = pltpu.VMEM((4 * TOK, HC), BF16)
    tall = pltpu.VMEM((TOK, 4 * TOK), BF16)
    scratch = [wide, wide, wide, tall, tall, wide, pltpu.VMEM((TOK, HC), F32)]
    specs = []
    extra = ()
    if own:
        specs = [whole((TOK, HC)), whole((TOK, HC)), whole((16, 2 * HC)), block]
        extra = tuple(tables) + (before,)
    else:
        scratch += [pltpu.VMEM((PREV, TOK, HC), F32)] * 2
    return pl.pallas_call(
        lambda *refs: attend_back_kernel(own, *refs),
        out_shape=[shape((FPD, TOK, HC), BF16 if own else F32)]
        + ([shape((FPD, TOK, HC), F32)] * 2 if own else [shape((2, PREV, TOK, HC))]),
        grid_spec=pltpu.PrefetchScalarGridSpec(
            num_scalar_prefetch=1,
            grid=(FPD,),
            in_specs=[block]
            + [whole((count, TOK, HC))] * 2
            + [piece] * 6
            + [pl.BlockSpec((2, 1, PR, HC), lambda f, *_: (0, f, 0, 0))]
            + [pl.BlockSpec((1, 8, TOK), lambda f, *_: (f, 0, 0))]
            + specs,
            out_specs=[block]
            + ([whole((FPD, TOK, HC))] * 2 if own else [whole((2, PREV, TOK, HC))]),
            scratch_shapes=scratch,
        ),
        compiler_params=params(58),
        cost_estimate=cost(1000 if own else 12 * 4 * 5 * 2 * TOK**3, 1000 if own else 12 * MB),
        name="attend_back_own" if own else "attend_back_prev",
    )(places, q, k, v, *grads, *mixed, lse, *extra)


HALF = 4
RAW = HALF * PR


def flat(ref):
    return ref[...].reshape(RAW, ref.shape[-1])


def frames_of(value):
    return value.reshape(HALF, PR, value.shape[-1])


def segment(table, s):
    both = table[:, s * D : (s + 1) * D]
    return jnp.where(pl.program_id(0) == 0, both[:HALF], both[HALF:])[:, None, :]


def fold(out, start, width, row):
    @pl.when(pl.program_id(0) == 0)
    def _():
        out[:, start : start + width] = jnp.zeros((8, width), F32)

    for i in range(8):
        at = (slice(i, i + 1), slice(start, start + width))
        out[at] = out[at] + row[:, i * width : (i + 1) * width]


def mid_kernel(o0, o1, o2, o3, w0, w1, w2, w3, table, x, cot, branch, middle, hidden, down, dsum):
    total = unfold(table, OB, 128)
    for o, w in zip((o0, o1, o2, o3), (w0, w1, w2, w3)):
        total = total + nn(flat(o), w[...])
    branched = frames_of(total)
    branch[...] = branched
    mid_value = x[...].astype(F32) + segment(table, 2) * branched
    middle[...] = mid_value
    normal, _ = norm(mid_value)
    hidden[...] = (normal * (1.0 + segment(table, 4)) + segment(table, 3)).astype(BF16)
    grad = (segment(table, 5) * cot[...].astype(F32)).astype(BF16)
    down[...] = grad
    fold(dsum, 0, 128, jnp.sum(grad.astype(F32).reshape(RAW, D), axis=0, keepdims=True))


def half_spec(width):
    return pl.BlockSpec((HALF, PR, width), lambda i, *_: (i, 0, 0))


def mid(pieces, weights, table, x, cot):
    return pl.pallas_call(
        mid_kernel,
        out_shape=[
            shape((FPD, PR, D), F32),
            shape((FPD, PR, D), F32),
            shape((FPD, PR, D)),
            shape((FPD, PR, D)),
            shape((8, 128), F32),
        ],
        grid=(FPD // HALF,),
        in_specs=[half_spec(HC)] * 4
        + [whole((HC, D))] * 4
        + [whole((FPD, WIDE)), half_spec(D), half_spec(D)],
        out_specs=[half_spec(D)] * 4 + [whole((8, 128))],
        compiler_params=params(26),
        cost_estimate=cost(2 * 512 * D * D, 12 * MB),
        name="mid",
    )(*pieces, *weights, table, x, cot)


def mid_back_kernel(hg, middle, branch, cot, table, w0, w1, w2, w3, mg, bg, a0, a1, a23, sums):
    grad = hg[...]
    normal, rate = norm(middle[...])
    put_half(sums, D, jnp.sum(grad, axis=1))
    put_half(sums, 2 * D, jnp.sum(grad * normal, axis=1))
    total = cot[...].astype(F32) + norm_back(normal, rate, grad * (1.0 + segment(table, 4)))
    mg[...] = total
    put_half(sums, 0, jnp.sum(total * branch[...], axis=1))
    low = (segment(table, 2) * total).astype(BF16)
    bg[...] = low
    low = low.reshape(RAW, D)
    fold(sums, 3 * D, 128, jnp.sum(low.astype(F32), axis=0, keepdims=True))
    for j, w in enumerate((w0, w1, w2, w3)):
        value = frames_of(nt(low, w[...]).astype(BF16))
        if j < 2:
            (a0, a1)[j][...] = value
        else:
            a23[j - 2] = value


def mid_back(hg, middle, branch, cot, table, weights):
    return pl.pallas_call(
        mid_back_kernel,
        out_shape=[shape((FPD, PR, D), F32), shape((FPD, PR, D))]
        + [shape((FPD, PR, HC))] * 2
        + [shape((2, FPD, PR, HC)), shape((8, 3 * D + 128), F32)],
        grid=(FPD // HALF,),
        in_specs=[half_spec(D)] * 4
        + [whole((FPD, WIDE))]
        + [whole((HC, D))] * 4,
        out_specs=[half_spec(D)] * 2
        + [half_spec(HC)] * 2
        + [pl.BlockSpec((2, HALF, PR, HC), lambda i: (0, i, 0, 0)), whole((8, 3 * D + 128))],
        compiler_params=params(26),
        cost_estimate=cost(2 * 512 * D * D, 12 * MB),
        name="mid_back",
    )(hg, middle, branch, cot, table, *weights)


NB = 512
STEPS = FF // NB
PER = D // NB
TOKENS = FPD * PR


def block_of(t):
    phase = t // PER
    return ((phase % 2) * 2) ^ (phase // 2)


def up_column(t, row):
    return (row ^ block_of(t)) * PER + t % PER


def down_row(t):
    return block_of(t) * PER + t % PER


def down_spec(j):
    phase = (0, 2, 1, 3)[j]
    return pl.BlockSpec((NB, D), lambda t, row: (jnp.clip(t - phase * PER, 0, PER - 1), 0))


def pick_down(d0, d1, d2, d3):
    phase = pl.program_id(0) // PER
    return jnp.where(
        phase < 2,
        jnp.where(phase == 0, d0[...], d2[...]),
        jnp.where(phase == 2, d1[...], d3[...]),
    )


def feed_kernel(row_ref, h2, dg, u0, u1, u2, u3, table, d0, d1, d2, d3, act, upg, hg, usum):
    row = row_ref[0]
    ups = (u0, u1, u2, u3)
    down = pick_down(d0, d1, d2, d3)
    at = pl.ds(up_column(pl.program_id(0), row), 1)
    u = table[at, UB : UB + NB]
    for j, w in enumerate(ups):
        u = u + nn(h2[:, columns(row, j)], w[...])
    rate = math.sqrt(2.0 / math.pi)
    square = u * u
    half = 0.5 + 0.5 * jnp.tanh(u * (rate + (rate * 0.044715) * square))
    active = u * half
    act[...] = active.astype(BF16)
    slope = half + active * (1.0 - half) * (2.0 * rate + (6.0 * rate * 0.044715) * square)
    grad = (nt(dg[...], down) * slope).astype(BF16)
    upg[...] = grad
    put(usum, 0, up_column(pl.program_id(0), row), jnp.sum(grad.astype(F32), axis=0, keepdims=True))

    @pl.when(pl.program_id(0) == 0)
    def _():
        hg[...] = jnp.zeros_like(hg)

    for j, w in enumerate(ups):
        hg[:, columns(row, j)] = hg[:, columns(row, j)] + nt(grad, w[...])


def feed(row, h2, dg, ups, table, downs):
    tok = whole((TOKENS, D))
    block = pl.BlockSpec((TOKENS, NB), lambda t, row: (0, t))
    return pl.pallas_call(
        feed_kernel,
        out_shape=[
            shape((TOKENS, FF)),
            shape((TOKENS, FF)),
            shape((TOKENS, D), F32),
            shape((8, NB), F32),
        ],
        grid_spec=pltpu.PrefetchScalarGridSpec(
            num_scalar_prefetch=1,
            grid=(STEPS,),
            in_specs=[tok, tok]
            + [pl.BlockSpec((HC, NB), lambda t, row: (0, up_column(t, row[0])))] * 4
            + [whole((FPD, WIDE))]
            + [down_spec(j) for j in range(4)],
            out_specs=[block, block, tok, whole((8, NB))],
        ),
        compiler_params=params(58),
        cost_estimate=cost(3 * 2 * TOKENS * D * FF, 30 * MB, TOKENS * FF),
        name="feed",
    )(row, h2, dg, *ups, table, *downs)


def down_weight_kernel(row_ref, dg, act, d0, d1, d2, d3, table, middle, cot, dk, ds, out, gate, dn):
    t = pl.program_id(0)
    down = pick_down(d0, d1, d2, d3)
    active = act[...]

    @pl.when(t == 0)
    def _():
        dn[...] = jnp.zeros_like(dn)

    dn[...] = dn[...] + nn(active, down)
    part = tn(active, dg[...]).astype(BF16)

    @pl.when(t < STEPS // 2)
    def _():
        dk[0] = part

    @pl.when(t >= STEPS // 2)
    def _():
        ds[0] = part

    @pl.when(t == STEPS - 1)
    def _():
        bias = unfold(table, DB, 128)
        for f in range(FPD):
            rows = slice(f * PR, (f + 1) * PR)
            value = dn[rows, :] + bias
            out[f] = (middle[f] + table[f : f + 1, 5 * D : 6 * D] * value).astype(BF16)
            gate[f : f + 1, :] = jnp.sum(cot[f].astype(F32) * value, axis=0, keepdims=True)


def down_weight_grad(row, dg, act, downs, table, middle, cot):
    tok = whole((TOKENS, D))
    full = whole((FPD, PR, D))
    block = pl.BlockSpec((TOKENS, NB), lambda t, row: (0, t))

    def down_out(first):
        def index(t, row):
            at = jnp.clip(t - first, 0, STEPS // 2 - 1)
            return (at // PER, at % PER, 0)

        return pl.BlockSpec((1, NB, D), index)

    return pl.pallas_call(
        down_weight_kernel,
        out_shape=[shape((2, D, D))] * 2 + [shape((FPD, PR, D)), shape((8, D), F32)],
        grid_spec=pltpu.PrefetchScalarGridSpec(
            num_scalar_prefetch=1,
            grid=(STEPS,),
            in_specs=[tok, block]
            + [down_spec(j) for j in range(4)]
            + [whole((FPD, WIDE)), full, full],
            out_specs=[down_out(0), down_out(STEPS // 2), full, whole((8, D))],
            scratch_shapes=[pltpu.VMEM((TOKENS, D), F32)],
        ),
        compiler_params=params(58),
        cost_estimate=cost(2 * 2 * TOKENS * D * FF, 24 * MB),
        name="down_weight_grad",
    )(row, dg, act, *downs, table, middle, cot)


def up_weight_kernel(row_ref, h2, upg, uk, us):
    row = row_ref[0]
    grad = upg[...]
    for j, ref in enumerate((uk, us, uk, us)):
        ref[j // 2, 0] = tn(h2[:, columns(row, j)], grad).astype(BF16)


def up_weight_grad(row, h2, upg):
    up_out = pl.BlockSpec(
        (2, 1, HC, NB),
        lambda t, row: (0, up_column(t, row[0]) // PER, 0, up_column(t, row[0]) % PER),
    )
    return pl.pallas_call(
        up_weight_kernel,
        out_shape=[shape((2, 4, HC, D))] * 2,
        grid_spec=pltpu.PrefetchScalarGridSpec(
            num_scalar_prefetch=1,
            grid=(STEPS,),
            in_specs=[whole((TOKENS, D)), pl.BlockSpec((TOKENS, NB), lambda t, row: (0, t))],
            out_specs=[up_out, up_out],
        ),
        compiler_params=params(58),
        cost_estimate=cost(2 * TOKENS * D * FF, 14 * MB),
        name="up_weight_grad",
    )(row, h2, upg)


def out_weight_kernel(t0, t1, t2, t3, bg, keep, send):
    grad = bg[...].reshape(TOKENS, D)
    for j, t in enumerate((t0, t1, t2, t3)):
        ref = (keep, send)[j % 2]
        ref[j // 2] = tn(t[...].reshape(TOKENS, HC), grad).astype(BF16)


def out_weight_grad(pieces, bg):
    return pl.pallas_call(
        out_weight_kernel,
        out_shape=[shape((2, HC, D))] * 2,
        grid=(1,),
        in_specs=[whole((FPD, PR, HC))] * 4 + [whole((FPD, PR, D))],
        out_specs=[whole((2, HC, D))] * 2,
        compiler_params=params(14),
        cost_estimate=cost(2 * TOKENS * D * D, 4 * MB),
        name="out_weight_grad",
    )(*pieces, bg)


CHUNKS = 16
UP_ROWS, OUT_ROWS, DOWN_ROWS = D // CHUNKS, HC // CHUNKS, D // CHUNKS
FIRST = UP_ROWS + OUT_ROWS
ROWS = FIRST + DOWN_ROWS


def core_sum_kernel(ua, ub, da, db, oa, ob, out):
    def both(a, b):
        return (a.astype(F32) + b.astype(F32)).astype(BF16)

    for c in range(4):
        at = c * ROWS
        low, high = c * OUT_ROWS, (c + 1) * OUT_ROWS
        for i in range(4):
            to = at + i * OUT_ROWS
            out[0, to : to + OUT_ROWS] = both(ua[0, i, low:high], ub[0, i, low:high])
        out[0, at + UP_ROWS : at + FIRST] = both(oa[0, low:high], ob[0, low:high])
        low, high = c * DOWN_ROWS, (c + 1) * DOWN_ROWS
        out[0, at + FIRST : at + ROWS] = both(da[0, low:high], db[0, low:high])


def core_sum(up, down, out):
    ups = pl.BlockSpec((1, 4, 4 * OUT_ROWS, D), lambda j, c: (j, 0, c, 0))
    outs = pl.BlockSpec((1, 4 * OUT_ROWS, D), lambda j, c: (j, c, 0))
    downs = pl.BlockSpec((1, 4 * DOWN_ROWS, D), lambda j, c: (j, c, 0))
    return pl.pallas_call(
        core_sum_kernel,
        out_shape=shape((2, CHUNKS * ROWS, D)),
        grid=(2, CHUNKS // 4),
        in_specs=[ups, ups, downs, downs, outs, outs],
        out_specs=pl.BlockSpec((1, 4 * ROWS, D), lambda j, c: (j, c, 0)),
        compiler_params=params(20),
        cost_estimate=cost(1000, 1000),
        name="core_sum",
    )(*up, *down, *out)


def spread_first_kernel(index_ref, a0, a1, a2, a3, up, out):
    for m, a in enumerate((a0, a1, a2, a3)):

        @pl.when(pl.program_id(0) == m)
        def _():
            for k in range(4):
                at = index_ref[1] ^ k
                for i in range(4):
                    rows = slice(i * OUT_ROWS, (i + 1) * OUT_ROWS)
                    up[0, at, :, i * D : (i + 1) * D] = a[k, rows].astype(F32)
                out[0, at] = a[k, UP_ROWS:].astype(F32)


def spread_first(index, pieces):
    def at(i, index):
        return (index[0] ^ i, 0, 0, 0)

    up, out = pl.pallas_call(
        spread_first_kernel,
        out_shape=[shape((4, 4, OUT_ROWS, FF), F32), shape((4, 4, OUT_ROWS, D), F32)],
        grid_spec=pltpu.PrefetchScalarGridSpec(
            num_scalar_prefetch=1,
            grid=(4,),
            in_specs=[whole((4, FIRST, D))] * 4,
            out_specs=[
                pl.BlockSpec((1, 4, OUT_ROWS, FF), at),
                pl.BlockSpec((1, 4, OUT_ROWS, D), at),
            ],
        ),
        compiler_params=params(24),
        cost_estimate=cost(0, 8 * MB),
        name="spread_up_out",
    )(index, *pieces)
    return up.reshape(HC, FF), out.reshape(HC, D)


def spread_second_kernel(index_ref, a0, a1, a2, a3, down):
    for m, a in enumerate((a0, a1, a2, a3)):

        @pl.when(pl.program_id(0) == m)
        def _():
            for k in range(4):
                down[index_ref[0] ^ k, 0] = a[k].astype(F32)


def spread_second(index, pieces):
    return pl.pallas_call(
        spread_second_kernel,
        out_shape=shape((4, 4, DOWN_ROWS, D), F32),
        grid_spec=pltpu.PrefetchScalarGridSpec(
            num_scalar_prefetch=1,
            grid=(4,),
            in_specs=[whole((4, DOWN_ROWS, D))] * 4,
            out_specs=pl.BlockSpec(
                (4, 1, DOWN_ROWS, D), lambda i, index: (0, index[1] ^ i, 0, 0)
            ),
        ),
        compiler_params=params(24),
        cost_estimate=cost(0, 6 * MB),
        name="spread_down",
    )(index, *pieces).reshape(D, D)


def place_kernel(axis, index_ref, a0, a1, a2, a3, out):
    for m, a in enumerate((a0, a1, a2, a3)):

        @pl.when(pl.program_id(0) == m)
        def _():
            out[...] = a[...].astype(out.dtype)


def place(index, axis, pieces, kind):
    rows, width = pieces[0].shape
    return pl.pallas_call(
        lambda *refs: place_kernel(axis, *refs),
        out_shape=shape((4 * rows, width), kind),
        grid_spec=pltpu.PrefetchScalarGridSpec(
            num_scalar_prefetch=1,
            grid=(4,),
            in_specs=[whole((rows, width))] * 4,
            out_specs=pl.BlockSpec((rows, width), lambda i, index: (index[axis] ^ i, 0)),
        ),
        compiler_params=params(24),
        cost_estimate=cost(0, 24 * rows * width),
        name="place",
    )(index, *pieces)


def arrange_kernel(row_ref, a0, a1, a2, a3, out):
    row = row_ref[0]
    for j, a in enumerate((a0, a1, a2, a3)):
        for s in range(3):
            lanes = pl.ds(pl.multiple_of(s * D + (row ^ j) * HC, HC), HC)
            out[:, lanes] = a[:, s * HC : (s + 1) * HC]


def arrange(row, pieces):
    rows = pieces[0].shape[0]
    return pl.pallas_call(
        arrange_kernel,
        out_shape=shape((rows, 3 * D)),
        grid_spec=pltpu.PrefetchScalarGridSpec(
            num_scalar_prefetch=1,
            grid=(1,),
            in_specs=[whole((rows, 3 * HC))] * 4,
            out_specs=whole((rows, 3 * D)),
        ),
        compiler_params=params(16),
        cost_estimate=cost(0, 8 * rows * D),
        name="arrange",
    )(row, *pieces)


def project_back_kernel(row_ref, dq, dk, dv, rk, rv, w0, w1, w2, w3, cp, sp, fr, dp, h0, h2, hs, bsum):
    row = row_ref[0]
    f = pl.program_id(0)
    later = (f > 0).astype(F32)
    keys = dk[0] + later * rk[0, 0].astype(F32)
    values = dv[0] + later * rv[0, 0].astype(F32)
    cosine, sine = cosines(cp, sp, fr, f)
    dp[0, :, :HC] = dq[0]
    dp[0, :, HC : 2 * HC] = turn(keys, cosine, -sine).astype(BF16)
    dp[0, :, 2 * HC :] = values.astype(BF16)
    grad = dp[0]
    sums = jnp.sum(grad.astype(F32), axis=0, keepdims=True)

    @pl.when(f == 0)
    def _():
        bsum[...] = jnp.zeros_like(bsum)

    number = lax.broadcasted_iota(jnp.int32, (8, 2 * HC), 0)
    bsum[...] = bsum[...] + jnp.where(number == row, sums[:, : 2 * HC], 0.0)
    bsum[:, :HC] = bsum[:, :HC] + jnp.where(number[:, :HC] == row + 4, sums[:, 2 * HC :], 0.0)
    for j, w in enumerate((w0, w1, w2, w3)):
        part = nt(grad, w[...]).astype(BF16)
        at = (0, slice(None), columns(row, j))
        h0[at] = part[:PR]
        hs[(0,) + at] = part[PR : 2 * PR]
        h2[at] = part[2 * PR : 3 * PR]
        hs[(1,) + at] = part[3 * PR :]


def project_back(row, dq, dk, dv, returned, weights, tables):
    block = pl.BlockSpec((1, TOK, HC), lambda f, *_: (f, 0, 0))
    late = [
        pl.BlockSpec((1, 1, TOK, HC), lambda f, *_, i=i: (i, jnp.maximum(f - 1, 0), 0, 0))
        for i in range(2)
    ]
    piece = pl.BlockSpec((1, PR, D), lambda f, *_: (f, 0, 0))
    return pl.pallas_call(
        project_back_kernel,
        out_shape=[
            shape((FPD, TOK, 3 * HC)),
            shape((FPD, PR, D)),
            shape((FPD, PR, D)),
            shape((2, FPD, PR, D)),
            shape((8, 2 * HC), F32),
        ],
        grid_spec=pltpu.PrefetchScalarGridSpec(
            num_scalar_prefetch=1,
            grid=(FPD,),
            in_specs=[block] * 3
            + late
            + [whole((HC, 3 * HC))] * 4
            + [whole((TOK, HC)), whole((TOK, HC)), whole((16, 2 * HC))],
            out_specs=[
                pl.BlockSpec((1, TOK, 3 * HC), lambda f, *_: (f, 0, 0)),
                piece,
                piece,
                pl.BlockSpec((2, 1, PR, D), lambda f, *_: (0, f, 0, 0)),
                whole((8, 2 * HC)),
            ],
        ),
        compiler_params=params(20),
        cost_estimate=cost(2 * FPD * TOK * D * 3 * HC, 14 * MB),
        name="project_back",
    )(row, dq, dk, dv, returned, returned, *weights, *tables)


def weight_kernel(row_ref, h, dp, w):
    w[0] = tn(h[...], dp[...]).astype(BF16)


def project_weight(row, hidden, dproj):
    tokens = FPD * TOK
    return pl.pallas_call(
        weight_kernel,
        out_shape=shape((4, HC, 3 * HC)),
        grid_spec=pltpu.PrefetchScalarGridSpec(
            num_scalar_prefetch=1,
            grid=(4,),
            in_specs=[
                pl.BlockSpec((tokens, HC), lambda j, row: (0, row[0] ^ j)),
                whole((tokens, 3 * HC)),
            ],
            out_specs=pl.BlockSpec((1, HC, 3 * HC), lambda j, row: (j, 0, 0)),
        ),
        compiler_params=params(20),
        cost_estimate=cost(2 * tokens * D * 3 * HC, 9 * MB),
        name="project_weight",
    )(row, hidden.reshape(tokens, D), dproj.reshape(tokens, 3 * HC))


def input_back_kernel(x, h0, near, far, table, mg, bsum, gate, out, sums):
    grad = h0[...].astype(F32) + near[0].astype(F32) + far[...].astype(F32)
    normal, rate = norm(x[...].astype(F32))
    put_half(sums, 0, jnp.sum(grad, axis=1))
    put_half(sums, D, jnp.sum(grad * normal, axis=1))
    sums[:, 2 * D : 3 * D] = gate[...]
    sums[:, 3 * D :] = bsum[...]
    out[...] = mg[...] + norm_back(normal, rate, grad * (1.0 + segment(table, 1)))


LATE = 3 * D + 2 * HC
EARLY = 3 * D + NB + 256


def input_back(x, h0, near, far, table, mg, bsum, gate):
    return pl.pallas_call(
        input_back_kernel,
        out_shape=[shape((FPD, PR, D), F32), shape((8, LATE), F32)],
        grid=(FPD // HALF,),
        in_specs=[half_spec(D)] * 2
        + [pl.BlockSpec((1, HALF, PR, D), lambda i: (0, i, 0, 0))]
        + [half_spec(D), whole((FPD, WIDE)), half_spec(D), whole((8, 2 * HC)), whole((8, D))],
        out_specs=[half_spec(D), whole((8, LATE))],
        compiler_params=params(20),
        cost_estimate=cost(20 * 512 * D, 10 * MB),
        name="input_back",
    )(x, h0, near, far, table, mg, bsum, gate)


def early_kernel(m, u, d, out):
    out[:, : 3 * D] = m[:, : 3 * D]
    out[:, 3 * D : 3 * D + NB] = u[...]
    out[:, 3 * D + NB : 3 * D + NB + 128] = d[...]
    out[:, 3 * D + NB + 128 :] = m[:, 3 * D :]


def early_sums(sums, usum, dsum):
    return pl.pallas_call(
        early_kernel,
        out_shape=shape((8, EARLY), F32),
        grid=(1,),
        in_specs=[whole(a.shape) for a in (sums, usum, dsum)],
        out_specs=whole((8, EARLY)),
        cost_estimate=cost(0, MB),
        name="early_sums",
    )(sums, usum, dsum)


def final_kernel(row_ref, *refs):
    row = row_ref[0]
    late, early = refs[:4], refs[4:8]
    ada, ab, qb, ob, ub, db, asum = refs[8:]

    def rows(ref, cols):
        value = ref[:, :, cols].astype(F32)
        return value.reshape(64, value.shape[-1])

    left = [rows(s, slice(EARLY, EARLY + HC)).astype(BF16) for s in early]
    for segment in range(6):
        source, start = ((late, 0), (late, 1), (early, 0), (early, 1), (early, 2), (late, 2))[segment]
        cols = slice(start * D, (start + 1) * D)
        product, total = 0.0, 0.0
        for s, ref in zip(left, source):
            right = rows(ref, cols)
            total = total + jnp.sum(right, axis=0, keepdims=True)
            product = product + tn(s, right.astype(BF16))
        at = segment * D
        ada[:, at : at + D] = product
        asum[0:1, at : at + D] = total

    def bias(source, start, stop):
        return sum(
            jnp.sum(ref[:, :, start:stop].astype(F32), axis=0) for ref in source
        )

    ab[...] = asum[0:1, pl.ds(pl.multiple_of(row * 1536, 512), 1536)]
    folded = bias(late, 3 * D, LATE)
    for i in range(3):
        chunk = 3 * row + i
        at = jnp.where(chunk < 4, chunk, chunk - 4)
        second = (chunk >= 4) & (chunk < 8)
        value = jnp.where(second, folded[:, HC:], folded[:, :HC])
        qb[:, i * HC : (i + 1) * HC] = take(value, at)
    folded = bias(early, 3 * D, EARLY)
    for i in range(2):
        at = 2 * row + i
        ub[:, i * NB : (i + 1) * NB] = take(folded[:, :NB], at)
        db[:, i * 128 : (i + 1) * 128] = take(folded[:, NB : NB + 128], at)
        ob[:, i * 128 : (i + 1) * 128] = take(folded[:, NB + 128 :], at)


def final_sums(row, late, early):
    sizes = (1536, 768, 256, 1024, 256)
    return pl.pallas_call(
        final_kernel,
        out_shape=[shape((HC, 6 * D), F32)] + [shape((1, n), F32) for n in sizes],
        grid_spec=pltpu.PrefetchScalarGridSpec(
            num_scalar_prefetch=1,
            grid=(1,),
            in_specs=[whole((8, 8, LATE))] * 4
            + [whole((8, 8, EARLY + HC))] * 4,
            out_specs=[whole((HC, 6 * D))] + [whole((1, n)) for n in sizes],
            scratch_shapes=[pltpu.VMEM((8, 6 * D), F32)],
        ),
        compiler_params=params(28),
        cost_estimate=cost(2 * 256 * HC * 6 * D, 10 * MB),
        name="final_sums",
    )(row, *late, *early)


def row_sum(value):
    value = value + swap(value, CORE)
    return value + swap(value, DIRECT)


def row_pieces(value):
    return [value, swap(value, CORE), swap(value, DIRECT), swap(value, DIRECT ^ CORE)]


def seq_gather(value):
    value = jnp.stack([value, swap(value, FAR)])
    value = jnp.concatenate([value] + [swap(value, m) for m in (16, 32, 48)])
    return [value] + [swap(value, m) for m in (4, 8, 12)]


def by_row(pieces, row):
    a, b, c, d = pieces
    odd, high = row % 2 == 1, row >= 2
    a, b = jnp.where(odd, b, a), jnp.where(odd, a, b)
    c, d = jnp.where(odd, d, c), jnp.where(odd, c, d)
    return jnp.stack(
        [
            jnp.where(high, c, a),
            jnp.where(high, d, b),
            jnp.where(high, a, c),
            jnp.where(high, b, d),
        ]
    )


def exchange_rows(value, bit, index, axis):
    rows = value.shape[1] // 4
    at = lambda m: lax.dynamic_slice_in_dim(value, (index[axis] ^ m) * rows, rows, 1)
    parts = [at(0)] + [swap(at(m), bit * m) for m in (1, 2, 3)]
    return sum(part.astype(F32) for part in parts).astype(BF16)


def turn_heads(own, beside, across, order=lambda piece: piece):
    across = swap(across, DIRECT)
    return [own, swap(beside, CORE), across[0], swap(order(across)[1], CORE)]


def per_device(
    activations,
    noise_embed,
    frame_position,
    cotangent,
    ada_weight,
    ada_bias,
    qkv_weight,
    qkv_bias,
    out_weight,
    out_bias,
    up_weight,
    up_bias,
    down_weight,
    down_bias,
):
    row = lax.axis_index(("xl", "c")).astype(jnp.int32)
    row_arg = row.reshape(1)
    index = [lax.axis_index("y").astype(jnp.int32), lax.axis_index("z").astype(jnp.int32)]
    index_arg = jnp.stack(index)

    x0 = activations
    x2 = swap(x0, DIRECT)
    x1 = swap(x0, CORE)
    p0 = shift(activations[1:], 1)
    biases = (ada_bias, qkv_bias, out_bias, up_bias, down_bias)
    heads = list(split_heads(row_arg, qkv_weight))
    noise, heads[1] = lax.optimization_barrier((noise_embed, heads[1]))
    part, silu_own, *tables = prepare(row_arg, frame_position, noise, ada_weight, biases)
    qkv_pieces = [heads[0], swap(heads[1], CORE), swap(heads[2], OTHER), swap(heads[3], OTHER ^ CORE)]
    part = part + swap(part, CORE)
    table = part + swap(part, DIRECT)
    x2, p0, table, *qkv_pieces = lax.optimization_barrier((x2, p0, table, *qkv_pieces))

    x3 = swap(x2, CORE)
    p2 = swap(p0, DIRECT)
    p1 = swap(p0, CORE)
    before_mods = shift(table[:, : 2 * D], 1)

    out_own, up_own, _ = lax.optimization_barrier((out_weight, up_weight, table))
    outs2 = swap(out_own, OTHER)
    ups2 = swap(up_own, OTHER)

    hidden1, q, k, v = project(True, row_arg, (x0, x1, x2, x3), table, table, qkv_pieces, tables)
    p2, down_own, q, before_mods = lax.optimization_barrier((p2, down_weight, q, before_mods))
    p3 = swap(p2, CORE)
    downs2 = swap(down_own, DIRECT)
    kp, vp = project(
        False, row_arg, (p0, p1, p2, p3), table, before_mods, qkv_pieces, tables
    )
    *mixed, lse = attend(frame_position, q, k, v, kp, vp)
    outs2, ups2, downs2, lse = lax.optimization_barrier((outs2, ups2, downs2, lse))
    outs = [out_weight, swap(out_own, CORE), outs2, swap(outs2, CORE)]
    ups = [up_weight, swap(up_own, CORE), ups2, swap(ups2, CORE)]
    downs = [down_weight, swap(down_own, CORE), downs2, swap(downs2, CORE)]
    turned = turn_heads(*mixed)
    branch, middle, hidden2, down_grad, dsum = mid(turned, outs, table, x0, cotangent)
    h2 = hidden2.reshape(TOKENS, D)
    dg = down_grad.reshape(TOKENS, D)
    act, upg, hg, usum = feed(row_arg, h2, dg, ups, table, downs)
    mg, bg, *ag, sums = mid_back(hg.reshape(FPD, PR, D), middle, branch, cotangent, table, outs)
    late = []
    back = turn_heads(*ag[:2], ag[2], order=lambda piece: late.append(piece) or piece)[:2]

    early = early_sums(sums, usum, dsum)
    early = early + swap(early, CORE)
    dk_part, ds_part, layer_output, gate = down_weight_grad(
        row_arg, after(dg, bg), act, downs, table, middle, cotangent
    )
    upg, early, gate, far_back, *back = lax.optimization_barrier((upg, early, gate, *late, *back))
    back += [far_back[0], swap(far_back[1], CORE)]
    early = early + swap(early, DIRECT)
    uk, us = up_weight_grad(row_arg, h2, upg)
    ok, os = out_weight_grad(turned, bg)

    early = jnp.concatenate([early.astype(BF16), silu_own], axis=1)
    early, uk, ok, *back = lax.optimization_barrier((early, uk, ok, *back))
    dq_before, both = attend_back(False, frame_position, q, kp, vp, back, mixed, lse)
    returned = shift(both, -1)
    early = jnp.stack([early, swap(early, FAR)])
    uk, early, dq_before = lax.optimization_barrier((uk, early, dq_before))
    packed = core_sum(
        (uk, swap(us, CORE)), (dk_part, swap(ds_part, CORE)), (ok, swap(os, CORE))
    )
    early = jnp.concatenate([early] + [swap(early, m) for m in (16, 32, 48)])
    dq_before, packed, early = lax.optimization_barrier((dq_before, packed, early))
    scattered = lax.psum_scatter(packed, ("y", "z"), scatter_dimension=1, tiled=True)
    early_all = [early] + [swap(early, m) for m in (4, 8, 12)]
    dq, dk, dv = attend_back(
        True, frame_position, q, k, v, back, mixed, lse, tables, dq_before
    )
    dq, *early_all = lax.optimization_barrier((dq, *early_all))
    early = early_all[0][0].astype(F32)

    dproj, h0, h2_part, send, bsum = project_back(row_arg, dq, dk, dv, returned, qkv_pieces, tables)
    near = swap(send, CORE)
    far_part = (h2_part.astype(F32) + near[1].astype(F32)).astype(BF16)
    far = swap(far_part, DIRECT)
    qkv_parts = project_weight(row_arg, hidden1, dproj)
    input_grad, late = input_back(x0, h0, near, far, table, mg, bsum, gate)
    late = row_sum(late)
    late_all = seq_gather(late.astype(BF16))

    qkv_parts = after(qkv_parts, far_part)
    qkv_parts = exchange_rows(qkv_parts, 4, index, 0)
    qkv_parts = exchange_rows(qkv_parts, 16, index, 1)
    qkv_parts = (qkv_parts.astype(F32) + swap(qkv_parts, FAR).astype(F32)).astype(BF16)
    qkv_share = arrange(row_arg, turn_heads(qkv_parts[0], qkv_parts[1], qkv_parts[2:]))
    qkv_share = place(
        index_arg, 1, [qkv_share] + [swap(qkv_share, 16 * m) for m in (1, 2, 3)], BF16
    )
    qkv_total = place(
        index_arg, 0, [qkv_share] + [swap(qkv_share, 4 * m) for m in (1, 2, 3)], F32
    )

    share = scattered[0].astype(F32) + swap(scattered[1], DIRECT).astype(F32)
    share = (share + swap(share.astype(BF16), FAR).astype(F32)).astype(BF16)
    one, two = share[:FIRST], share[FIRST:]
    one = jnp.stack([one] + [swap(one, 16 * m) for m in (1, 2, 3)])
    two = jnp.stack([two] + [swap(two, 4 * m) for m in (1, 2, 3)])
    up_total, out_total = spread_first(index_arg, [one] + [swap(one, 4 * m) for m in (1, 2, 3)])
    down_total = spread_second(index_arg, [two] + [swap(two, 16 * m) for m in (1, 2, 3)])

    ada_total, *bias_sums = final_sums(row_arg, late_all, early_all)
    ada_sum, qkv_sum, out_sum, up_sum, down_sum = [b[0] for b in bias_sums]
    mod_own = jnp.concatenate(
        [late[:, : 2 * D], early[:, : 3 * D], late[:, 2 * D : 3 * D]], axis=1
    ).astype(BF16)
    silu_grad = nt(mod_own, ada_weight)
    silu_grad = by_row(row_pieces(silu_grad), row).transpose(1, 0, 2).reshape(FPD, D)
    embed = noise_embed.astype(F32)
    sigma = jax.nn.sigmoid(embed)
    embed_grad = silu_grad * (sigma * (1.0 + embed * (1.0 - sigma)))

    return (
        layer_output,
        input_grad,
        embed_grad,
        ada_total,
        ada_sum,
        qkv_total,
        qkv_sum,
        out_total,
        out_sum,
        up_total,
        up_sum,
        down_total,
        down_sum,
    )


def solution(mesh):
    fine = Mesh(mesh.devices.reshape(2, 4, 4, 2, 2), AXES)
    seq, row = ("xh", "z", "y"), ("xl", "c")
    token, weight, vector = P(seq, row, None), P(row, None), P(row)
    in_specs = (token, P(seq, None), P(seq), token) + (weight, vector) * 5
    out_specs = (token, token, P(seq, None)) + (weight, vector) * 5
    return jax.shard_map(
        per_device, mesh=fine, in_specs=in_specs, out_specs=out_specs, check_vma=False
    )
```

profile of v0, /device:TPU:6, one launch (start us, length us, event | category | flops | bytes accessed | tf_op | source)
XLA Modules:
  0.0 627.1 jit_solution(4838035148517123919)
XLA Ops:
  19.7 17.8 %collective-permute-done.3 = f32[8,7424]{1,0:T(8,128)S(1)} collective-permute-done((f32[8,7424]{1,0:T(8,128)S(1)}, f32[8,7424]{1,0:T(8,128)S(1)}, u32[]{:S(2)}, u32[]{:S(2)}) %collective-permute-start.3) | collective-permute-done | bytes 237600 | tf_op jit(solution)/shard_map/ppermute | solution.py:27
  38.0 11.3 %collective-permute-done.6.refs_10_.w3 = bf16[256,768]{1,0:T(8,128)(2,1)S(1)} collective-permute-done((bf16[256,768]{1,0:T(8,128)(2,1)S(1)}, bf16[256,768]{1,0:T(8,128)(2,1)S(1)}, u32[]{:S(2)}, u32[]{:S(2)}) %collective-permute-start.6) | collective-permute-done | bytes 393248 | tf_op jit(solution)/shard_map/ppermute | solution.py:27
  49.3 9.9 %collective-permute-done.1.refs_1_ = bf16[7,64,1024]{2,1,0:T(8,128)(2,1)} collective-permute-done((bf16[7,64,1024]{2,1,0:T(8,128)(2,1)}, bf16[7,64,1024]{2,1,0:T(8,128)(2,1)}, u32[]{:S(2)}, u32[]{:S(2)}) %collective-permute-start.1) | collective-permute-done | bytes 917536 | tf_op jit(solution)/shard_map/ppermute | solution.py:31
  62.3 11.0 %project_own.1 = (bf16[8,256,1024]{2,1,0:T(8,128)(2,1)S(1)}, bf16[8,256,256]{2,1,0:T(8,128)(2,1)S(1)}, bf16[8,256,256]{2,1,0:T(8,128)(2,1)S(1)}, bf16[8,256,256]{2,1,0:T(8,128)(2,1)S(1)}) custom-call(s32[1]{0:T(128)} %bitcast.row_ref.refs_0_, bf16[8,64,1024]{2,1,0:T(8,128)(2,1)S(1)} %copy-done.4, bf16[8,64,1024]{2,1,0:T(8,128)(2,1)S(1)} %collective-permute-done.8.refs_2_, ...), custom_call_target="tpu_custom_call" | custom-call | flops 3221225472 | bytes 12582912 | tf_op jit(solution)/shard_map/project_own/pallas_call | solution.py:279
  76.2 23.9 %collective-permute-done.10.refs_6_ = f32[8,2048]{1,0:T(8,128)S(1)} collective-permute-done((f32[8,2048]{1,0:T(8,128)S(1)}, f32[8,2048]{1,0:T(8,128)S(1)}, u32[]{:S(2)}, u32[]{:S(2)}) %collective-permute-start.10) | collective-permute-done | bytes 65568 | tf_op jit(solution)/shard_map/ppermute | solution.py:31
  105.3 8.1 %project_prev.1 = (bf16[7,256,256]{2,1,0:T(8,128)(2,1)S(1)}, bf16[7,256,256]{2,1,0:T(8,128)(2,1)S(1)}) custom-call(s32[1]{0:T(128)} %bitcast.row_ref.refs_0_, bf16[7,64,1024]{2,1,0:T(8,128)(2,1)} %collective-permute-done.1.refs_1_, bf16[7,64,1024]{2,1,0:T(8,128)(2,1)S(1)} %collective-permute-done.11.refs_2_, ...), custom_call_target="tpu_custom_call" | custom-call | flops 2818572288 | bytes 11534336 | tf_op jit(solution)/shard_map/project_prev/pallas_call | solution.py:279
  115.4 21.6 %attend.1 = (bf16[8,64,256]{2,1,0:T(8,128)(2,1)}, bf16[8,64,256]{2,1,0:T(8,128)(2,1)}, bf16[2,8,64,256]{3,2,1,0:T(8,128)(2,1)}, f32[8,8,256]{2,1,0:T(8,128)}) custom-call(s32[8]{0:T(128)} %refs_0_.3, bf16[8,256,256]{2,1,0:T(8,128)(2,1)} %copy-done.23, bf16[8,256,256]{2,1,0:T(8,128)(2,1)} %copy-done.24, bf16[8,256,256]{2,1,0:T(8,128)(2,1)} %copy-done.25, ...), custom_call_target="tpu_custom_call" | custom-call | flops 9663676416 | bytes 6291456 | tf_op jit(solution)/shard_map/attend/pallas_call | solution.py:366
  137.5 9.9 %collective-permute-done.19.d2 = bf16[1024,1024]{1,0:T(8,128)(2,1)} collective-permute-done((bf16[1024,1024]{1,0:T(8,128)(2,1)}, bf16[1024,1024]{1,0:T(8,128)(2,1)}, u32[]{:S(2)}, u32[]{:S(2)}) %collective-permute-start.19) | collective-permute-done | bytes 2097184 | tf_op jit(solution)/shard_map/ppermute | solution.py:27
  148.7 13.8 %collective-permute-done.14 = bf16[2,8,64,256]{3,2,1,0:T(8,128)(2,1)S(1)} collective-permute-done((bf16[2,8,64,256]{3,2,1,0:T(8,128)(2,1)}, bf16[2,8,64,256]{3,2,1,0:T(8,128)(2,1)S(1)}, u32[]{:S(2)}, u32[]{:S(2)}) %collective-permute-start.14) | collective-permute-done | bytes 524320 | tf_op jit(solution)/shard_map/ppermute | solution.py:27
  177.7 26.8 %feed.1 = (bf16[512,4096]{1,0:T(8,128)(2,1)}, bf16[512,4096]{1,0:T(8,128)(2,1)}, f32[512,1024]{1,0:T(8,128)}, f32[8,512]{1,0:T(8,128)}) custom-call(s32[1]{0:T(128)} %bitcast.row_ref.refs_0_, bf16[512,1024]{1,0:T(8,128)(2,1)} %bitcast.75, bf16[512,1024]{1,0:T(8,128)(2,1)} %bitcast.77, bf16[256,4096]{1,0:T(8,128)(2,1)} %u0.1, ...), custom_call_target="tpu_custom_call" | custom-call | flops 12884901888 | bytes 31457280 | tf_op jit(solution)/shard_map/feed/pallas_call | solution.py:680
  219.9 22.0 %down_weight_grad.1 = (bf16[2,1024,1024]{2,1,0:T(8,128)(2,1)}, bf16[2,1024,1024]{2,1,0:T(8,128)(2,1)}, bf16[8,64,1024]{2,1,0:T(8,128)(2,1)}, f32[8,1024]{1,0:T(8,128)}) custom-call(s32[1]{0:T(128)} %bitcast.row_ref.refs_0_, bf16[512,1024]{1,0:T(8,128)(2,1)} %bitcast.78, bf16[512,4096]{1,0:T(8,128)(2,1)} %get-tuple-element.162.act, bf16[1024,1024]{1,0:T(8,128)(2,1)} %d0.3, ...), custom_call_target="tpu_custom_call" | custom-call | flops 8589934592 | bytes 25165824 | tf_op jit(solution)/shard_map/down_weight_grad/pallas_call | solution.py:745
  242.6 11.1 %up_weight_grad.1 = (bf16[2,4,256,1024]{3,2,1,0:T(8,128)(2,1)}, bf16[2,4,256,1024]{3,2,1,0:T(8,128)(2,1)}) custom-call(s32[1]{0:T(128)} %bitcast.row_ref.refs_0_, bf16[512,1024]{1,0:T(8,128)(2,1)} %bitcast.76, bf16[512,4096]{1,0:T(8,128)(2,1)} %get-tuple-element.174.upg), custom_call_target="tpu_custom_call" | custom-call | flops 4294967296 | bytes 14680064 | tf_op jit(solution)/shard_map/up_weight_grad/pallas_call | solution.py:775
  263.0 4.4 collective-permute-start.30
  267.5 14.2 %attend_back_prev.1 = (f32[8,256,256]{2,1,0:T(8,128)}, bf16[2,7,256,256]{3,2,1,0:T(8,128)(2,1)}) custom-call(s32[8]{0:T(128)} %refs_0_.3, bf16[8,256,256]{2,1,0:T(8,128)(2,1)} %copy-done.23, bf16[7,256,256]{2,1,0:T(8,128)(2,1)} %copy-done.87, bf16[7,256,256]{2,1,0:T(8,128)(2,1)} %copy-done.88, bf16[8,64,256]{2,1,0:T(8,128)(2,1)} %copy-done.54, ...), custom_call_target="tpu_custom_call" | custom-call | flops 8053063680 | bytes 12582912 | tf_op jit(solution)/shard_map/attend_back_prev/pallas_call | solution.py:489
  281.9 9.2 %collective-permute-done.36 = bf16[2,8,4096]{2,1,0:T(8,128)(2,1)S(1)} collective-permute-done((bf16[2,8,4096]{2,1,0:T(8,128)(2,1)S(1)}, bf16[2,8,4096]{2,1,0:T(8,128)(2,1)S(1)}, u32[]{:S(2)}, u32[]{:S(2)}) %collective-permute-start.36) | collective-permute-done | bytes 131104 | tf_op jit(solution)/shard_map/ppermute | solution.py:27
  291.1 5.0 collective-permute-done.34
  300.7 6.7 %core_sum.1 = bf16[2,2304,1024]{2,1,0:T(8,128)(2,1)S(1)} custom-call(bf16[2,4,256,1024]{3,2,1,0:T(8,128)(2,1)S(1)} %copy-done.9, bf16[2,4,256,1024]{3,2,1,0:T(8,128)(2,1)} %collective-permute-done.31.ub, bf16[2,1024,1024]{2,1,0:T(8,128)(2,1)S(1)} %copy-done.8, bf16[2,1024,1024]{2,1,0:T(8,128)(2,1)} %collective-permute-done.32.db, ...), custom_call_target="tpu_custom_call" | custom-call | flops 1000 | bytes 1000 | tf_op jit(solution)/shard_map/core_sum/pallas_call | solution.py:835
  315.9 22.7 %attend_back_own.1 = (bf16[8,256,256]{2,1,0:T(8,128)(2,1)}, f32[8,256,256]{2,1,0:T(8,128)}, f32[8,256,256]{2,1,0:T(8,128)}) custom-call(s32[8]{0:T(128)} %refs_0_.3, bf16[8,256,256]{2,1,0:T(8,128)(2,1)} %copy-done.23, bf16[8,256,256]{2,1,0:T(8,128)(2,1)} %copy-done.24, bf16[8,256,256]{2,1,0:T(8,128)(2,1)} %copy-done.25, bf16[8,64,256]{2,1,0:T(8,128)(2,1)} %copy-done.54, ...), custom_call_target="tpu_custom_call" | custom-call | flops 1000 | bytes 1000 | tf_op jit(solution)/shard_map/attend_back_own/pallas_call | solution.py:489
  338.6 45.3 %collective-permute-done.37.refs_5_ = bf16[8,8,4096]{2,1,0:T(8,128)(2,1)S(1)} collective-permute-done((bf16[8,8,4096]{2,1,0:T(8,128)(2,1)S(1)}, bf16[8,8,4096]{2,1,0:T(8,128)(2,1)S(1)}, u32[]{:S(2)}, u32[]{:S(2)}) %collective-permute-start.37) | collective-permute-done | bytes 524320 | tf_op jit(solution)/shard_map/ppermute | solution.py:27
  393.2 8.0 %project_back.1 = (bf16[8,256,768]{2,1,0:T(8,128)(2,1)S(1)}, bf16[8,64,1024]{2,1,0:T(8,128)(2,1)S(1)}, bf16[8,64,1024]{2,1,0:T(8,128)(2,1)S(1)}, bf16[2,8,64,1024]{3,2,1,0:T(8,128)(2,1)}, f32[8,512]{1,0:T(8,128)S(1)}) custom-call(s32[1]{0:T(128)} %bitcast.row_ref.refs_0_, bf16[8,256,256]{2,1,0:T(8,128)(2,1)S(1)} %copy-done.72, ...), custom_call_target="tpu_custom_call" | custom-call | flops 3221225472 | bytes 14680064 | tf_op jit(solution)/shard_map/project_back/pallas_call | solution.py:996
  409.0 4.7 project_weight.1
  416.3 22.1 %collective-permute-start.57 = (bf16[4,64,768]{2,1,0:T(8,128)(2,1)}, bf16[4,64,768]{2,1,0:T(8,128)(2,1)}, u32[]{:S(2)}, u32[]{:S(2)}) collective-permute-start(bf16[4,64,768]{2,1,0:T(8,128)(2,1)} %get-tuple-element.230), channel_id=1, source_target_pairs={{0,12},{1,13},{2,14},{3,15},{4,8},{5,9},{6,10},{7,11},{8,4},{9,5},... | collective-permute-start | bytes 1179656 | tf_op jit(solution)/shard_map/ppermute | solution.py:27
  441.2 18.4 %collective-permute-done.57 = bf16[4,64,768]{2,1,0:T(8,128)(2,1)} collective-permute-done((bf16[4,64,768]{2,1,0:T(8,128)(2,1)}, bf16[4,64,768]{2,1,0:T(8,128)(2,1)}, u32[]{:S(2)}, u32[]{:S(2)}) %collective-permute-start.57) | collective-permute-done | bytes 393248 | tf_op jit(solution)/shard_map/ppermute | solution.py:27
  473.9 6.1 collective-permute-done.61
  516.7 6.9 %collective-permute-done.71 = bf16[144,1024]{1,0:T(8,128)(2,1)S(1)} collective-permute-done((bf16[144,1024]{1,0:T(8,128)(2,1)S(1)}, bf16[144,1024]{1,0:T(8,128)(2,1)S(1)}, u32[]{:S(2)}, u32[]{:S(2)}) %collective-permute-start.71) | collective-permute-done | bytes 294944 | tf_op jit(solution)/shard_map/ppermute | solution.py:27
  524.8 8.2 %collective-permute-done.72 = bf16[144,1024]{1,0:T(8,128)(2,1)S(1)} collective-permute-done((bf16[144,1024]{1,0:T(8,128)(2,1)S(1)}, bf16[144,1024]{1,0:T(8,128)(2,1)S(1)}, u32[]{:S(2)}, u32[]{:S(2)}) %collective-permute-start.72) | collective-permute-done | bytes 294944 | tf_op jit(solution)/shard_map/ppermute | solution.py:27
  537.3 4.5 collective-permute-done.81
  555.7 10.6 %collective-permute-done.74 = bf16[80,1024]{1,0:T(8,128)(2,1)S(1)} collective-permute-done((bf16[80,1024]{1,0:T(8,128)(2,1)S(1)}, bf16[80,1024]{1,0:T(8,128)(2,1)S(1)}, u32[]{:S(2)}, u32[]{:S(2)}) %collective-permute-start.74) | collective-permute-done | bytes 163872 | tf_op jit(solution)/shard_map/ppermute | solution.py:27
  566.6 5.4 collective-permute-done.73
  588.8 7.2 %final_sums.1 = (f32[256,6144]{1,0:T(8,128)}, f32[1,1536]{1,0:T(1,128)S(1)}, f32[1,768]{1,0:T(1,128)S(1)}, f32[1,256]{1,0:T(1,128)}, f32[1,1024]{1,0:T(1,128)}, /*index=5*/f32[1,256]{1,0:T(1,128)}) custom-call(s32[1]{0:T(128)} %bitcast.row_ref.refs_0_, bf16[8,8,3584]{2,1,0:T(8,128)(2,1)S(1)} %constant_dynamic-update-slice_fusion.refs_0_, ...), custom_call_target="tpu_custom_call" | custom-call | flops 805306368 | bytes 10485760 | tf_op jit(solution)/shard_map/final_sums/pallas_call | solution.py:1143
  600.0 11.1 %collective-permute-done.84.a3 = bf16[4,64,1024]{2,1,0:T(8,128)(2,1)} collective-permute-done((bf16[4,64,1024]{2,1,0:T(8,128)(2,1)S(1)}, bf16[4,64,1024]{2,1,0:T(8,128)(2,1)}, u32[]{:S(2)}, u32[]{:S(2)}) %collective-permute-start.84) | collective-permute-done | bytes 524320 | tf_op jit(solution)/shard_map/ppermute | solution.py:27
  615.5 4.4 spread_up_out.1
  (421 shorter events, 199.2 us)
Async XLA Ops:
  7.2 507.9 %reduce-scatter.2.cloned.1.call-start = ((), (), s32[]{:S(2)}) async-start(), calls=%async_computation.1 | async-start | bytes 10027008 | tf_op jit(solution)/shard_map/reduce_scatter | solution.py:1288
  7.2 51.9 %collective-permute-start = (bf16[8,64,1024]{2,1,0:T(8,128)(2,1)}, bf16[8,64,1024]{2,1,0:T(8,128)(2,1)}, u32[]{:S(2)}, u32[]{:S(2)}) collective-permute-start(bf16[8,64,1024]{2,1,0:T(8,128)(2,1)} %x.3), channel_id=1, source_target_pairs={{0,2},{1,3},{2,0},{3,1},{4,6},{5,7},{6,4},{7,5},{8,10},{9,11},{10,... | collective-permute-start | bytes 3145736 | tf_op jit(solution)/shard_map/ppermute | solution.py:27
  10.4 48.8 %collective-permute-start.1 = (bf16[7,64,1024]{2,1,0:T(8,128)(2,1)}, bf16[7,64,1024]{2,1,0:T(8,128)(2,1)}, u32[]{:S(2)}, u32[]{:S(2)}) collective-permute-start(bf16[7,64,1024]{2,1,0:T(8,128)(2,1)} %slice.63), channel_id=1, source_target_pairs={{0,4},{1,5},{2,6},{3,7},{4,8},{5,9},{6,10},{7,11},{8,12},{9,13},{1... | collective-permute-start | bytes 2752520 | tf_op jit(solution)/shard_map/ppermute | solution.py:31
  37.6 24.7 %collective-permute-start.8 = (bf16[8,64,1024]{2,1,0:T(8,128)(2,1)S(1)}, bf16[8,64,1024]{2,1,0:T(8,128)(2,1)S(1)}, u32[]{:S(2)}, u32[]{:S(2)}) collective-permute-start(bf16[8,64,1024]{2,1,0:T(8,128)(2,1)S(1)} %copy-done.4), channel_id=1, source_target_pairs={{0,1},{1,0},{2,3},{3,2},{4,5},{5,4},{6,7},{7,6},{8,9},{9,8},{10,11... | collective-permute-start | bytes 3145736 | tf_op jit(solution)/shard_map/ppermute | solution.py:27
  59.2 40.9 %collective-permute-start.7 = (bf16[7,64,1024]{2,1,0:T(8,128)(2,1)}, bf16[7,64,1024]{2,1,0:T(8,128)(2,1)S(1)}, u32[]{:S(2)}, u32[]{:S(2)}) collective-permute-start(bf16[7,64,1024]{2,1,0:T(8,128)(2,1)} %collective-permute-done.1.refs_1_), channel_id=1, source_target_pairs={{0,2},{1,3},{2,0},{3,1},{4,6},{5,7},{6,4},{7,5},{8,10},{9,11},{10,... | collective-permute-start | bytes 2752520 | tf_op jit(solution)/shard_map/ppermute | solution.py:27
  60.1 40.0 %collective-permute-start.10 = (f32[8,2048]{1,0:T(8,128)S(1)}, f32[8,2048]{1,0:T(8,128)S(1)}, u32[]{:S(2)}, u32[]{:S(2)}) collective-permute-start(f32[8,2048]{1,0:T(8,128)S(1)} %slice.64), channel_id=1, source_target_pairs={{0,4},{1,5},{2,6},{3,7},{4,8},{5,9},{6,10},{7,11},{8,12},{9,13},{1... | collective-permute-start | bytes 196616 | tf_op jit(solution)/shard_map/ppermute | solution.py:31
  60.1 77.4 %collective-permute-start.18 = (bf16[256,4096]{1,0:T(8,128)(2,1)}, bf16[256,4096]{1,0:T(8,128)(2,1)}, u32[]{:S(2)}, u32[]{:S(2)}) collective-permute-start(bf16[256,4096]{1,0:T(8,128)(2,1)} %u0.1), channel_id=1, source_target_pairs={{0,66},{1,67},{2,64},{3,65},{4,70},{5,71},{6,68},{7,69},{8,74},{9,... | collective-permute-start | bytes 6291464 | tf_op jit(solution)/shard_map/ppermute | solution.py:27
  100.1 47.3 %collective-permute-start.19 = (bf16[1024,1024]{1,0:T(8,128)(2,1)}, bf16[1024,1024]{1,0:T(8,128)(2,1)}, u32[]{:S(2)}, u32[]{:S(2)}) collective-permute-start(bf16[1024,1024]{1,0:T(8,128)(2,1)} %d0.3), channel_id=1, source_target_pairs={{0,2},{1,3},{2,0},{3,1},{4,6},{5,7},{6,4},{7,5},{8,10},{9,11},{10,... | collective-permute-start | bytes 6291464 | tf_op jit(solution)/shard_map/ppermute | solution.py:27
  100.6 47.7 %collective-permute-start.16 = (bf16[256,1024]{1,0:T(8,128)(2,1)S(1)}, bf16[256,1024]{1,0:T(8,128)(2,1)S(1)}, u32[]{:S(2)}, u32[]{:S(2)}) collective-permute-start(bf16[256,1024]{1,0:T(8,128)(2,1)S(1)} %copy-done.19), channel_id=1, source_target_pairs={{0,1},{1,0},{2,3},{3,2},{4,5},{5,4},{6,7},{7,6},{8,9},{9,8},{10,11... | collective-permute-start | bytes 1572872 | tf_op jit(solution)/shard_map/ppermute | solution.py:27
  103.2 33.7 %collective-permute-start.17 = (bf16[256,1024]{1,0:T(8,128)(2,1)S(1)}, bf16[256,1024]{1,0:T(8,128)(2,1)S(1)}, u32[]{:S(2)}, u32[]{:S(2)}) collective-permute-start(bf16[256,1024]{1,0:T(8,128)(2,1)S(1)} %copy-done.19), channel_id=1, source_target_pairs={{0,66},{1,67},{2,64},{3,65},{4,70},{5,71},{6,68},{7,69},{8,74},{9,... | collective-permute-start | bytes 1572872 | tf_op jit(solution)/shard_map/ppermute | solution.py:27
  105.3 69.7 %collective-permute-start.21 = (bf16[256,4096]{1,0:T(8,128)(2,1)}, bf16[256,4096]{1,0:T(8,128)(2,1)}, u32[]{:S(2)}, u32[]{:S(2)}) collective-permute-start(bf16[256,4096]{1,0:T(8,128)(2,1)} %u0.1), channel_id=1, source_target_pairs={{0,1},{1,0},{2,3},{3,2},{4,5},{5,4},{6,7},{7,6},{8,9},{9,8},{10,11... | collective-permute-start | bytes 6291464 | tf_op jit(solution)/shard_map/ppermute | solution.py:27
  137.0 38.0 %collective-permute-start.23 = (bf16[1024,1024]{1,0:T(8,128)(2,1)}, bf16[1024,1024]{1,0:T(8,128)(2,1)S(1)}, u32[]{:S(2)}, u32[]{:S(2)}) collective-permute-start(bf16[1024,1024]{1,0:T(8,128)(2,1)} %d0.3), channel_id=1, source_target_pairs={{0,1},{1,0},{2,3},{3,2},{4,5},{5,4},{6,7},{7,6},{8,9},{9,8},{10,11... | collective-permute-start | bytes 6291464 | tf_op jit(solution)/shard_map/ppermute | solution.py:27
  147.4 27.6 %collective-permute-start.22 = (bf16[256,4096]{1,0:T(8,128)(2,1)}, bf16[256,4096]{1,0:T(8,128)(2,1)S(1)}, u32[]{:S(2)}, u32[]{:S(2)}) collective-permute-start(bf16[256,4096]{1,0:T(8,128)(2,1)} %collective-permute-done.18.u2), channel_id=1, source_target_pairs={{0,1},{1,0},{2,3},{3,2},{4,5},{5,4},{6,7},{7,6},{8,9},{9,8},{10,11... | collective-permute-start | bytes 6291464 | tf_op jit(solution)/shard_map/ppermute | solution.py:27
  147.9 27.2 %collective-permute-start.24 = (bf16[1024,1024]{1,0:T(8,128)(2,1)}, bf16[1024,1024]{1,0:T(8,128)(2,1)S(1)}, u32[]{:S(2)}, u32[]{:S(2)}) collective-permute-start(bf16[1024,1024]{1,0:T(8,128)(2,1)} %collective-permute-done.19.d2), channel_id=1, source_target_pairs={{0,1},{1,0},{2,3},{3,2},{4,5},{5,4},{6,7},{7,6},{8,9},{9,8},{10,11... | collective-permute-start | bytes 6291464 | tf_op jit(solution)/shard_map/ppermute | solution.py:27
  241.9 54.3 %collective-permute-start.32 = (bf16[2,1024,1024]{2,1,0:T(8,128)(2,1)}, bf16[2,1024,1024]{2,1,0:T(8,128)(2,1)}, u32[]{:S(2)}, u32[]{:S(2)}) collective-permute-start(bf16[2,1024,1024]{2,1,0:T(8,128)(2,1)} %get-tuple-element.192), channel_id=1, source_target_pairs={{0,1},{1,0},{2,3},{3,2},{4,5},{5,4},{6,7},{7,6},{8,9},{9,8},{10,11... | collective-permute-start | bytes 12582920 | tf_op jit(solution)/shard_map/ppermute | solution.py:27
  253.8 42.4 %collective-permute-start.31 = (bf16[2,4,256,1024]{3,2,1,0:T(8,128)(2,1)}, bf16[2,4,256,1024]{3,2,1,0:T(8,128)(2,1)}, u32[]{:S(2)}, u32[]{:S(2)}) collective-permute-start(bf16[2,4,256,1024]{3,2,1,0:T(8,128)(2,1)} %get-tuple-element.190), channel_id=1, source_target_pairs={{0,1},{1,0},{2,3},{3,2},{4,5},{5,4},{6,7},{7,6},{8,9},{9,8},{10,11... | collective-permute-start | bytes 12582920 | tf_op jit(solution)/shard_map/ppermute | solution.py:27
  255.4 40.7 %collective-permute-start.33 = (bf16[2,256,1024]{2,1,0:T(8,128)(2,1)S(1)}, bf16[2,256,1024]{2,1,0:T(8,128)(2,1)S(1)}, u32[]{:S(2)}, u32[]{:S(2)}) collective-permute-start(bf16[2,256,1024]{2,1,0:T(8,128)(2,1)S(1)} %get-tuple-element.194), channel_id=1, source_target_pairs={{0,1},{1,0},{2,3},{3,2},{4,5},{5,4},{6,7},{7,6},{8,9},{9,8},{10,11... | collective-permute-start | bytes 3145736 | tf_op jit(solution)/shard_map/ppermute | solution.py:27
  311.0 72.9 %collective-permute-start.40 = (bf16[2,7,256,256]{3,2,1,0:T(8,128)(2,1)}, bf16[2,7,256,256]{3,2,1,0:T(8,128)(2,1)S(1)}, u32[]{:S(2)}, u32[]{:S(2)}) collective-permute-start(bf16[2,7,256,256]{3,2,1,0:T(8,128)(2,1)} %get-tuple-element.202), channel_id=1, source_target_pairs={{0,124},{1,125},{2,126},{3,127},{4,0},{5,1},{6,2},{7,3},{8,4},{9,5... | collective-permute-start | bytes 5505032 | tf_op jit(solution)/shard_map/ppermute | solution.py:31
  311.1 72.7 %collective-permute-start.37 = (bf16[8,8,4096]{2,1,0:T(8,128)(2,1)S(1)}, bf16[8,8,4096]{2,1,0:T(8,128)(2,1)S(1)}, u32[]{:S(2)}, u32[]{:S(2)}) collective-permute-start(bf16[8,8,4096]{2,1,0:T(8,128)(2,1)S(1)} %pad_maximum_fusion.1.refs_4_), channel_id=1, source_target_pairs={{0,4},{1,5},{2,6},{3,7},{4,0},{5,1},{6,2},{7,3},{8,12},{9,13},{10,... | collective-permute-start | bytes 1572872 | tf_op jit(solution)/shard_map/ppermute | solution.py:27
  313.1 70.7 %collective-permute-start.38 = (bf16[8,8,4096]{2,1,0:T(8,128)(2,1)S(1)}, bf16[8,8,4096]{2,1,0:T(8,128)(2,1)S(1)}, u32[]{:S(2)}, u32[]{:S(2)}) collective-permute-start(bf16[8,8,4096]{2,1,0:T(8,128)(2,1)S(1)} %pad_maximum_fusion.1.refs_4_), channel_id=1, source_target_pairs={{0,8},{1,9},{2,10},{3,11},{4,12},{5,13},{6,14},{7,15},{8,0},{9,1},... | collective-permute-start | bytes 1572872 | tf_op jit(solution)/shard_map/ppermute | solution.py:27
  313.1 70.7 %collective-permute-start.39 = (bf16[8,8,4096]{2,1,0:T(8,128)(2,1)S(1)}, bf16[8,8,4096]{2,1,0:T(8,128)(2,1)S(1)}, u32[]{:S(2)}, u32[]{:S(2)}) collective-permute-start(bf16[8,8,4096]{2,1,0:T(8,128)(2,1)S(1)} %pad_maximum_fusion.1.refs_4_), channel_id=1, source_target_pairs={{0,12},{1,13},{2,14},{3,15},{4,8},{5,9},{6,10},{7,11},{8,4},{9,5},... | collective-permute-start | bytes 1572872 | tf_op jit(solution)/shard_map/ppermute | solution.py:27
  416.3 43.4 %collective-permute-start.57 = (bf16[4,64,768]{2,1,0:T(8,128)(2,1)}, bf16[4,64,768]{2,1,0:T(8,128)(2,1)}, u32[]{:S(2)}, u32[]{:S(2)}) collective-permute-start(bf16[4,64,768]{2,1,0:T(8,128)(2,1)} %get-tuple-element.230), channel_id=1, source_target_pairs={{0,12},{1,13},{2,14},{3,15},{4,8},{5,9},{6,10},{7,11},{8,4},{9,5},... | collective-permute-start | bytes 1179656 | tf_op jit(solution)/shard_map/ppermute | solution.py:27
  439.3 42.6 %collective-permute-start.42 = (bf16[8,64,1024]{2,1,0:T(8,128)(2,1)}, bf16[8,64,1024]{2,1,0:T(8,128)(2,1)}, u32[]{:S(2)}, u32[]{:S(2)}) collective-permute-start(bf16[8,64,1024]{2,1,0:T(8,128)(2,1)} %fusion), channel_id=1, source_target_pairs={{0,2},{1,3},{2,0},{3,1},{4,6},{5,7},{6,4},{7,5},{8,10},{9,11},{10,... | collective-permute-start | bytes 3145736 | tf_op jit(solution)/shard_map/ppermute | solution.py:27
  501.1 42.3 %collective-permute-start.68 = (bf16[64,3072]{1,0:T(8,128)(2,1)S(1)}, bf16[64,3072]{1,0:T(8,128)(2,1)S(1)}, u32[]{:S(2)}, u32[]{:S(2)}) collective-permute-start(bf16[64,3072]{1,0:T(8,128)(2,1)S(1)} %place.2.refs_1_), channel_id=1, source_target_pairs={{0,4},{1,5},{2,6},{3,7},{4,0},{5,1},{6,2},{7,3},{8,12},{9,13},{10,... | collective-permute-start | bytes 1179656 | tf_op jit(solution)/shard_map/ppermute | solution.py:27
  502.2 41.9 %collective-permute-start.69 = (bf16[64,3072]{1,0:T(8,128)(2,1)S(1)}, bf16[64,3072]{1,0:T(8,128)(2,1)S(1)}, u32[]{:S(2)}, u32[]{:S(2)}) collective-permute-start(bf16[64,3072]{1,0:T(8,128)(2,1)S(1)} %place.2.refs_1_), channel_id=1, source_target_pairs={{0,8},{1,9},{2,10},{3,11},{4,12},{5,13},{6,14},{7,15},{8,0},{9,1},... | collective-permute-start | bytes 1179656 | tf_op jit(solution)/shard_map/ppermute | solution.py:27
  549.4 38.0 %collective-permute-start.82 = (bf16[4,64,1024]{2,1,0:T(8,128)(2,1)S(1)}, bf16[4,64,1024]{2,1,0:T(8,128)(2,1)}, u32[]{:S(2)}, u32[]{:S(2)}) collective-permute-start(bf16[4,64,1024]{2,1,0:T(8,128)(2,1)S(1)} %pad_maximum_fusion.2.a0), channel_id=1, source_target_pairs={{0,16},{1,17},{2,18},{3,19},{4,20},{5,21},{6,22},{7,23},{8,24},{9,... | collective-permute-start | bytes 1572872 | tf_op jit(solution)/shard_map/ppermute | solution.py:27
  550.8 26.5 %collective-permute-start.53 = (bf16[8,8,3584]{2,1,0:T(8,128)(2,1)S(1)}, bf16[8,8,3584]{2,1,0:T(8,128)(2,1)S(1)}, u32[]{:S(2)}, u32[]{:S(2)}) collective-permute-start(bf16[8,8,3584]{2,1,0:T(8,128)(2,1)S(1)} %constant_dynamic-update-slice_fusion.refs_0_), channel_id=1, source_target_pairs={{0,8},{1,9},{2,10},{3,11},{4,12},{5,13},{6,14},{7,15},{8,0},{9,1},... | collective-permute-start | bytes 1376264 | tf_op jit(solution)/shard_map/ppermute | solution.py:27
  555.0 30.0 %collective-permute-start.54 = (bf16[8,8,3584]{2,1,0:T(8,128)(2,1)S(1)}, bf16[8,8,3584]{2,1,0:T(8,128)(2,1)}, u32[]{:S(2)}, u32[]{:S(2)}) collective-permute-start(bf16[8,8,3584]{2,1,0:T(8,128)(2,1)S(1)} %constant_dynamic-update-slice_fusion.refs_0_), channel_id=1, source_target_pairs={{0,12},{1,13},{2,14},{3,15},{4,8},{5,9},{6,10},{7,11},{8,4},{9,5},... | collective-permute-start | bytes 1376264 | tf_op jit(solution)/shard_map/ppermute | solution.py:27
  573.1 42.4 %collective-permute-start.76 = (bf16[4,80,1024]{2,1,0:T(8,128)(2,1)S(1)}, bf16[4,80,1024]{2,1,0:T(8,128)(2,1)S(1)}, u32[]{:S(2)}, u32[]{:S(2)}) collective-permute-start(bf16[4,80,1024]{2,1,0:T(8,128)(2,1)S(1)} %pad_maximum_fusion.a0), channel_id=1, source_target_pairs={{0,4},{1,5},{2,6},{3,7},{4,0},{5,1},{6,2},{7,3},{8,12},{9,13},{10,... | collective-permute-start | bytes 1966088 | tf_op jit(solution)/shard_map/ppermute | solution.py:27
  573.9 41.6 %collective-permute-start.77 = (bf16[4,80,1024]{2,1,0:T(8,128)(2,1)S(1)}, bf16[4,80,1024]{2,1,0:T(8,128)(2,1)S(1)}, u32[]{:S(2)}, u32[]{:S(2)}) collective-permute-start(bf16[4,80,1024]{2,1,0:T(8,128)(2,1)S(1)} %pad_maximum_fusion.a0), channel_id=1, source_target_pairs={{0,8},{1,9},{2,10},{3,11},{4,12},{5,13},{6,14},{7,15},{8,0},{9,1},... | collective-permute-start | bytes 1966088 | tf_op jit(solution)/shard_map/ppermute | solution.py:27
  578.0 37.5 %collective-permute-start.78 = (bf16[4,80,1024]{2,1,0:T(8,128)(2,1)S(1)}, bf16[4,80,1024]{2,1,0:T(8,128)(2,1)}, u32[]{:S(2)}, u32[]{:S(2)}) collective-permute-start(bf16[4,80,1024]{2,1,0:T(8,128)(2,1)S(1)} %pad_maximum_fusion.a0), channel_id=1, source_target_pairs={{0,12},{1,13},{2,14},{3,15},{4,8},{5,9},{6,10},{7,11},{8,4},{9,5},... | collective-permute-start | bytes 1966088 | tf_op jit(solution)/shard_map/ppermute | solution.py:27
  587.4 23.6 %collective-permute-start.84 = (bf16[4,64,1024]{2,1,0:T(8,128)(2,1)S(1)}, bf16[4,64,1024]{2,1,0:T(8,128)(2,1)}, u32[]{:S(2)}, u32[]{:S(2)}) collective-permute-start(bf16[4,64,1024]{2,1,0:T(8,128)(2,1)S(1)} %pad_maximum_fusion.2.a0), channel_id=1, source_target_pairs={{0,48},{1,49},{2,50},{3,51},{4,52},{5,53},{6,54},{7,55},{8,56},{9,... | collective-permute-start | bytes 1572872 | tf_op jit(solution)/shard_map/ppermute | solution.py:27
  (157 other events, 2210.5 us)
Sparse Core Ops, SparseCore 0:
  311.1 144.6 reduce-scatter.1
where the time goes:
time: 636 us; the launch traced here: 627 us
  waiting for transfers between devices  252 us (40%)
  Pallas kernels  193 us (30%)
  starting transfers between devices  92.6 us (15%)
  local copies, waits for them, and re-layouts  64.6 us (10%)
  between operations  15.7 us (2%)
  other arithmetic  9.01 us (1%)
    ppermute x82, waiting for transfers between devices, swap(): return lax.ppermute(value, AXES, [(i, i ^ mask) for i in range(128)])  218 us
    ppermute x82, starting transfers between devices, swap(): return lax.ppermute(value, AXES, [(i, i ^ mask) for i in range(128)])  90.9 us
    unnamed x209, local copies, waits for them, and re-layouts  56.8 us
    pallas_call x2, Pallas kernels, attend_back(): pl.pallas_call(lambda *refs: attend_back_kernel(own, *refs), out_shape=[s...  36.8 us
    ppermute x3, waiting for transfers between devices, shift(): lax.ppermute(value, AXES, [(i, (i + 4 * steps) % 128) for i in range(128)])  33.8 us
    pallas_call x1, Pallas kernels, feed(): pl.pallas_call(feed_kernel, out_shape=[shape((TOKENS, FF)), shape((TOKENS...  26.8 us
    pallas_call x1, Pallas kernels, down_weight_grad(): pl.pallas_call(down_weight_kernel, out_shape=[shape((2, D, D))] * 2 + [sh...  22 us
    pallas_call x1, Pallas kernels, attend(): pl.pallas_call(attend_kernel, out_shape=[shape((FPD, PR, HC))] * 2 + [sha...  21.6 us
  transfers between devices with their start and end apart: 86, of which 34 were waited for; matrix products, arithmetic and copies ran while one was open for 3% of the time, Pallas kernels for 24%

commit v1 on v0

--- a/solution.py
+++ b/solution.py
@@ -201,8 +201,8 @@
     )(row, places, noise, ada, *[b[None] for b in biases])
 
 
-def split_heads_kernel(row_ref, q, k, v, p0, p1, p2, p3):
-    for j, p in enumerate((p0, p1, p2, p3)):
+def split_heads_kernel(row_ref, q, k, v, p0, p1, p23):
+    for j, p in enumerate((p0, p1, p23.at[0], p23.at[1])):
 
         @pl.when(pl.program_id(0) == j)
         def _():
@@ -212,9 +212,10 @@
 
 
 def split_heads(row, weight):
+    piece = (HC, 3 * HC)
     return pl.pallas_call(
         split_heads_kernel,
-        out_shape=[shape((HC, 3 * HC))] * 4,
+        out_shape=[shape(piece), shape(piece), shape((2,) + piece)],
         grid_spec=pltpu.PrefetchScalarGridSpec(
             num_scalar_prefetch=1,
             grid=(4,),
@@ -222,7 +223,7 @@
                 pl.BlockSpec((HC, HC), lambda j, row, s=s: (0, 4 * s + (row[0] ^ j)))
                 for s in range(3)
             ],
-            out_specs=[whole((HC, 3 * HC))] * 4,
+            out_specs=[whole(piece), whole(piece), whole((2,) + piece)],
         ),
         compiler_params=params(12),
         cost_estimate=cost(0, 3 * MB),
@@ -838,123 +839,95 @@
         grid=(2, CHUNKS // 4),
         in_specs=[ups, ups, downs, downs, outs, outs],
         out_specs=pl.BlockSpec((1, 4 * ROWS, D), lambda j, c: (j, c, 0)),
-        compiler_params=params(20),
+        compiler_params=params(58),
         cost_estimate=cost(1000, 1000),
         name="core_sum",
     )(*up, *down, *out)
 
 
-def spread_first_kernel(index_ref, a0, a1, a2, a3, up, out):
-    for m, a in enumerate((a0, a1, a2, a3)):
-
-        @pl.when(pl.program_id(0) == m)
-        def _():
-            for k in range(4):
-                at = index_ref[1] ^ k
-                for i in range(4):
-                    rows = slice(i * OUT_ROWS, (i + 1) * OUT_ROWS)
-                    up[0, at, :, i * D : (i + 1) * D] = a[k, rows].astype(F32)
-                out[0, at] = a[k, UP_ROWS:].astype(F32)
-
-
-def spread_first(index, pieces):
-    def at(i, index):
-        return (index[0] ^ i, 0, 0, 0)
-
-    up, out = pl.pallas_call(
-        spread_first_kernel,
-        out_shape=[shape((4, 4, OUT_ROWS, FF), F32), shape((4, 4, OUT_ROWS, D), F32)],
-        grid_spec=pltpu.PrefetchScalarGridSpec(
-            num_scalar_prefetch=1,
-            grid=(4,),
-            in_specs=[whole((4, FIRST, D))] * 4,
-            out_specs=[
-                pl.BlockSpec((1, 4, OUT_ROWS, FF), at),
-                pl.BlockSpec((1, 4, OUT_ROWS, D), at),
-            ],
-        ),
+def unpack_kernel(total, up, out, down):
+    for k in range(4):
+        at = k * ROWS
+        for i in range(4):
+            rows = slice(at + i * OUT_ROWS, at + (i + 1) * OUT_ROWS)
+            up[k * OUT_ROWS : (k + 1) * OUT_ROWS, i * D : (i + 1) * D] = total[rows].astype(F32)
+        out[k * OUT_ROWS : (k + 1) * OUT_ROWS] = total[at + UP_ROWS : at + FIRST].astype(F32)
+        down[k * DOWN_ROWS : (k + 1) * DOWN_ROWS] = total[at + FIRST : at + ROWS].astype(F32)
+
+
+def unpack(total):
+    block = lambda i: (i, 0)
+    return pl.pallas_call(
+        unpack_kernel,
+        out_shape=[shape((HC, FF), F32), shape((HC, D), F32), shape((D, D), F32)],
+        grid=(4,),
+        in_specs=[pl.BlockSpec((4 * ROWS, D), block)],
+        out_specs=[
+            pl.BlockSpec((4 * OUT_ROWS, FF), block),
+            pl.BlockSpec((4 * OUT_ROWS, D), block),
+            pl.BlockSpec((4 * DOWN_ROWS, D), block),
+        ],
         compiler_params=params(24),
-        cost_estimate=cost(0, 8 * MB),
-        name="spread_up_out",
-    )(index, *pieces)
-    return up.reshape(HC, FF), out.reshape(HC, D)
-
-
-def spread_second_kernel(index_ref, a0, a1, a2, a3, down):
-    for m, a in enumerate((a0, a1, a2, a3)):
-
-        @pl.when(pl.program_id(0) == m)
-        def _():
-            for k in range(4):
-                down[index_ref[0] ^ k, 0] = a[k].astype(F32)
-
-
-def spread_second(index, pieces):
-    return pl.pallas_call(
-        spread_second_kernel,
-        out_shape=shape((4, 4, DOWN_ROWS, D), F32),
-        grid_spec=pltpu.PrefetchScalarGridSpec(
-            num_scalar_prefetch=1,
-            grid=(4,),
-            in_specs=[whole((4, DOWN_ROWS, D))] * 4,
-            out_specs=pl.BlockSpec(
-                (4, 1, DOWN_ROWS, D), lambda i, index: (0, index[1] ^ i, 0, 0)
-            ),
-        ),
-        compiler_params=params(24),
-        cost_estimate=cost(0, 6 * MB),
-        name="spread_down",
-    )(index, *pieces).reshape(D, D)
-
-
-def place_kernel(axis, index_ref, a0, a1, a2, a3, out):
-    for m, a in enumerate((a0, a1, a2, a3)):
-
-        @pl.when(pl.program_id(0) == m)
-        def _():
-            out[...] = a[...].astype(out.dtype)
-
-
-def place(index, axis, pieces, kind):
-    rows, width = pieces[0].shape
-    return pl.pallas_call(
-        lambda *refs: place_kernel(axis, *refs),
-        out_shape=shape((4 * rows, width), kind),
-        grid_spec=pltpu.PrefetchScalarGridSpec(
-            num_scalar_prefetch=1,
-            grid=(4,),
-            in_specs=[whole((rows, width))] * 4,
-            out_specs=pl.BlockSpec((rows, width), lambda i, index: (index[axis] ^ i, 0)),
-        ),
-        compiler_params=params(24),
-        cost_estimate=cost(0, 24 * rows * width),
-        name="place",
-    )(index, *pieces)
-
-
-def arrange_kernel(row_ref, a0, a1, a2, a3, out):
+        cost_estimate=cost(0, 14 * MB),
+        name="unpack",
+    )(total)
+
+
+LATE = 3 * D + 2 * HC
+EARLY = 3 * D + NB + 256
+
+
+def arrange_kernel(row_ref, a0, a1, a2, a3, late, far, out):
     row = row_ref[0]
     for j, a in enumerate((a0, a1, a2, a3)):
         for s in range(3):
             lanes = pl.ds(pl.multiple_of(s * D + (row ^ j) * HC, HC), HC)
             out[:, lanes] = a[:, s * HC : (s + 1) * HC]
-
-
-def arrange(row, pieces):
+    both = jnp.concatenate([late[...].astype(F32), far[...].astype(F32)], axis=0)
+    out[:, 3 * D :] = both.astype(BF16)
+
+
+def arrange(row, pieces, late, far):
     rows = pieces[0].shape[0]
     return pl.pallas_call(
         arrange_kernel,
-        out_shape=shape((rows, 3 * D)),
+        out_shape=shape((rows, 3 * D + LATE)),
         grid_spec=pltpu.PrefetchScalarGridSpec(
             num_scalar_prefetch=1,
             grid=(1,),
-            in_specs=[whole((rows, 3 * HC))] * 4,
-            out_specs=whole((rows, 3 * D)),
+            in_specs=[whole((rows, 3 * HC))] * 4 + [whole((8, LATE))] * 2,
+            out_specs=whole((rows, 3 * D + LATE)),
         ),
         compiler_params=params(16),
         cost_estimate=cost(0, 8 * rows * D),
         name="arrange",
-    )(row, *pieces)
+    )(row, *pieces, late, far)
+
+
+def place_kernel(index_ref, a0, a1, a2, a3, out):
+    for m, a in enumerate((a0, a1, a2, a3)):
+
+        @pl.when(pl.program_id(0) == m)
+        def _():
+            for k in range(4):
+                out[0, index_ref[1] ^ k] = a[k, :, : 3 * D].astype(F32)
+
+
+def place(index, pieces):
+    rows = pieces[0].shape[1]
+    return pl.pallas_call(
+        place_kernel,
+        out_shape=shape((4, 4, rows, 3 * D), F32),
+        grid_spec=pltpu.PrefetchScalarGridSpec(
+            num_scalar_prefetch=1,
+            grid=(4,),
+            in_specs=[whole(a.shape) for a in pieces],
+            out_specs=pl.BlockSpec((1, 4, rows, 3 * D), lambda i, index: (index[0] ^ i, 0, 0, 0)),
+        ),
+        compiler_params=params(24),
+        cost_estimate=cost(0, 24 * rows * D),
+        name="place",
+    )(index, *pieces).reshape(HC, 3 * D)
 
 
 def project_back_kernel(row_ref, dq, dk, dv, rk, rv, w0, w1, w2, w3, cp, sp, fr, dp, h0, h2, hs, bsum):
@@ -1057,10 +1030,6 @@
     out[...] = mg[...] + norm_back(normal, rate, grad * (1.0 + segment(table, 1)))
 
 
-LATE = 3 * D + 2 * HC
-EARLY = 3 * D + NB + 256
-
-
 def input_back(x, h0, near, far, table, mg, bsum, gate):
     return pl.pallas_call(
         input_back_kernel,
@@ -1104,6 +1073,7 @@
         value = ref[:, :, cols].astype(F32)
         return value.reshape(64, value.shape[-1])
 
+    late = [ref.at[:, :, 3 * D :] for ref in late]
     left = [rows(s, slice(EARLY, EARLY + HC)).astype(BF16) for s in early]
     for segment in range(6):
         source, start = ((late, 0), (late, 1), (early, 0), (early, 1), (early, 2), (late, 2))[segment]
@@ -1117,9 +1087,13 @@
         ada[:, at : at + D] = product
         asum[0:1, at : at + D] = total
 
+    def fold8(value):
+        value = jnp.sum(value, axis=0)
+        return value if value.shape[0] == 8 else value[:8] + value[8:]
+
     def bias(source, start, stop):
         return sum(
-            jnp.sum(ref[:, :, start:stop].astype(F32), axis=0) for ref in source
+            fold8(ref[:, :, start:stop].astype(F32)) for ref in source
         )
 
     ab[...] = asum[0:1, pl.ds(pl.multiple_of(row * 1536, 512), 1536)]
@@ -1146,7 +1120,7 @@
         grid_spec=pltpu.PrefetchScalarGridSpec(
             num_scalar_prefetch=1,
             grid=(1,),
-            in_specs=[whole((8, 8, LATE))] * 4
+            in_specs=[whole((4, 16, 3 * D + LATE))] * 4
             + [whole((8, 8, EARLY + HC))] * 4,
             out_specs=[whole((HC, 6 * D))] + [whole((1, n)) for n in sizes],
             scratch_shapes=[pltpu.VMEM((8, 6 * D), F32)],
@@ -1164,12 +1138,6 @@
 
 def row_pieces(value):
     return [value, swap(value, CORE), swap(value, DIRECT), swap(value, DIRECT ^ CORE)]
-
-
-def seq_gather(value):
-    value = jnp.stack([value, swap(value, FAR)])
-    value = jnp.concatenate([value] + [swap(value, m) for m in (16, 32, 48)])
-    return [value] + [swap(value, m) for m in (4, 8, 12)]
 
 
 def by_row(pieces, row):
@@ -1187,11 +1155,18 @@
     )
 
 
-def exchange_rows(value, bit, index, axis):
+def quarter_rows(value, bit, index, axis):
     rows = value.shape[1] // 4
     at = lambda m: lax.dynamic_slice_in_dim(value, (index[axis] ^ m) * rows, rows, 1)
-    parts = [at(0)] + [swap(at(m), bit * m) for m in (1, 2, 3)]
+    return [at(0)] + [swap(at(m), bit * m) for m in (1, 2, 3)]
+
+
+def add_all(parts):
     return sum(part.astype(F32) for part in parts).astype(BF16)
+
+
+def exchange_rows(value, bit, index, axis):
+    return add_all(quarter_rows(value, bit, index, axis))
 
 
 def turn_heads(own, beside, across, order=lambda piece: piece):
@@ -1228,11 +1203,13 @@
     heads = list(split_heads(row_arg, qkv_weight))
     noise, heads[1] = lax.optimization_barrier((noise_embed, heads[1]))
     part, silu_own, *tables = prepare(row_arg, frame_position, noise, ada_weight, biases)
-    qkv_pieces = [heads[0], swap(heads[1], CORE), swap(heads[2], OTHER), swap(heads[3], OTHER ^ CORE)]
+    across = swap(heads[2], OTHER)
+    qkv_pieces = [heads[0], swap(heads[1], CORE), across]
     part = part + swap(part, CORE)
     table = part + swap(part, DIRECT)
     x2, p0, table, *qkv_pieces = lax.optimization_barrier((x2, p0, table, *qkv_pieces))
 
+    qkv_pieces = qkv_pieces[:2] + [qkv_pieces[2][0], swap(qkv_pieces[2][1], CORE)]
     x3 = swap(x2, CORE)
     p2 = swap(p0, DIRECT)
     p1 = swap(p0, CORE)
@@ -1275,54 +1252,63 @@
     ok, os = out_weight_grad(turned, bg)
 
     early = jnp.concatenate([early.astype(BF16), silu_own], axis=1)
+    early, uk = lax.optimization_barrier((early, uk))
+    early = jnp.stack([early, swap(early, FAR)])
     early, uk, ok, *back = lax.optimization_barrier((early, uk, ok, *back))
+    early_parts = [early] + [swap(early, m) for m in (16, 32, 48)]
     dq_before, both = attend_back(False, frame_position, q, kp, vp, back, mixed, lse)
     returned = shift(both, -1)
-    early = jnp.stack([early, swap(early, FAR)])
-    uk, early, dq_before = lax.optimization_barrier((uk, early, dq_before))
+    uk, dq_before = lax.optimization_barrier((uk, dq_before))
     packed = core_sum(
         (uk, swap(us, CORE)), (dk_part, swap(ds_part, CORE)), (ok, swap(os, CORE))
     )
-    early = jnp.concatenate([early] + [swap(early, m) for m in (16, 32, 48)])
-    dq_before, packed, early = lax.optimization_barrier((dq_before, packed, early))
+    dq_before, packed = lax.optimization_barrier((dq_before, packed))
     scattered = lax.psum_scatter(packed, ("y", "z"), scatter_dimension=1, tiled=True)
-    early_all = [early] + [swap(early, m) for m in (4, 8, 12)]
     dq, dk, dv = attend_back(
         True, frame_position, q, k, v, back, mixed, lse, tables, dq_before
     )
-    dq, *early_all = lax.optimization_barrier((dq, *early_all))
-    early = early_all[0][0].astype(F32)
+    dq, *early_parts = lax.optimization_barrier((dq, *early_parts))
+    early = jnp.concatenate(early_parts)
+    early_high = early
+    early = early[0].astype(F32)
 
     dproj, h0, h2_part, send, bsum = project_back(row_arg, dq, dk, dv, returned, qkv_pieces, tables)
     near = swap(send, CORE)
-    far_part = (h2_part.astype(F32) + near[1].astype(F32)).astype(BF16)
-    far = swap(far_part, DIRECT)
     qkv_parts = project_weight(row_arg, hidden1, dproj)
+    far = swap((h2_part.astype(F32) + near[1].astype(F32)).astype(BF16), DIRECT)
+    qkv_parts = exchange_rows(qkv_parts, 4, index, 0)
+    far, qkv_parts, early_high = lax.optimization_barrier((far, qkv_parts, early_high))
+    early_all = [early_high] + [swap(early_high, m) for m in (4, 8, 12)]
+    quarters = quarter_rows(qkv_parts, 16, index, 1)
     input_grad, late = input_back(x0, h0, near, far, table, mg, bsum, gate)
-    late = row_sum(late)
-    late_all = seq_gather(late.astype(BF16))
-
-    qkv_parts = after(qkv_parts, far_part)
-    qkv_parts = exchange_rows(qkv_parts, 4, index, 0)
-    qkv_parts = exchange_rows(qkv_parts, 16, index, 1)
-    qkv_parts = (qkv_parts.astype(F32) + swap(qkv_parts, FAR).astype(F32)).astype(BF16)
-    qkv_share = arrange(row_arg, turn_heads(qkv_parts[0], qkv_parts[1], qkv_parts[2:]))
-    qkv_share = place(
-        index_arg, 1, [qkv_share] + [swap(qkv_share, 16 * m) for m in (1, 2, 3)], BF16
+    late, *quarters = lax.optimization_barrier((late, *quarters))
+    qkv_parts = add_all(quarters)
+    late_near = swap(late, CORE)
+    late, late_near, qkv_parts = lax.optimization_barrier((late, late_near, qkv_parts))
+    late = late + late_near
+    late_far = swap(late, DIRECT)
+    qkv_far = swap(qkv_parts, FAR)
+    late, late_far, qkv_parts, qkv_far = lax.optimization_barrier(
+        (late, late_far, qkv_parts, qkv_far)
     )
-    qkv_total = place(
-        index_arg, 0, [qkv_share] + [swap(qkv_share, 4 * m) for m in (1, 2, 3)], F32
-    )
-
+    late = late + late_far
+    qkv_parts = add_all([qkv_parts, qkv_far])
+    late_low = late.astype(BF16)
+    late_far = swap(late_low, FAR)
+    turned = turn_heads(qkv_parts[0], qkv_parts[1], qkv_parts[2:])
+    last = arrange(row_arg, turned, late_low, late_far)
+
+    scattered, last, *early_all = lax.optimization_barrier((scattered, last, *early_all))
+    last = jnp.stack([last] + [swap(last, m) for m in (16, 32, 48)])
     share = scattered[0].astype(F32) + swap(scattered[1], DIRECT).astype(F32)
     share = (share + swap(share.astype(BF16), FAR).astype(F32)).astype(BF16)
-    one, two = share[:FIRST], share[FIRST:]
-    one = jnp.stack([one] + [swap(one, 16 * m) for m in (1, 2, 3)])
-    two = jnp.stack([two] + [swap(two, 4 * m) for m in (1, 2, 3)])
-    up_total, out_total = spread_first(index_arg, [one] + [swap(one, 4 * m) for m in (1, 2, 3)])
-    down_total = spread_second(index_arg, [two] + [swap(two, 16 * m) for m in (1, 2, 3)])
-
-    ada_total, *bias_sums = final_sums(row_arg, late_all, early_all)
+    share, last = lax.optimization_barrier((share, last))
+    last_all = [last] + [swap(last, m) for m in (4, 8, 12)]
+    totals = lax.all_gather(share, ("y", "z"), axis=0, tiled=True)
+    up_total, out_total, down_total = unpack(totals)
+    qkv_total = place(index_arg, last_all)
+
+    ada_total, *bias_sums = final_sums(row_arg, last_all, early_all)
     ada_sum, qkv_sum, out_sum, up_sum, down_sum = [b[0] for b in bias_sums]
     mod_own = jnp.concatenate(
         [late[:, : 2 * D], early[:, : 3 * D], late[:, 2 * D : 3 * D]], axis=1

time: 636 us -> 573 us (0.901)
  waiting for transfers between devices: 252 us -> 220 us
  starting transfers between devices: 92.6 us -> 70.2 us
  local copies, waits for them, and re-layouts: 64.6 us -> 51.1 us
  Pallas kernels: 193 us -> 200 us
    ppermute x82 -> x64, waiting for transfers between devices: 218 us -> 170 us  [swap(): return lax.ppermute(value, AXES, [(i, i ^ mask) for i in range(128)])]
    ppermute x82 -> x64, starting transfers between devices: 90.9 us -> 68.5 us  [swap(): return lax.ppermute(value, AXES, [(i, i ^ mask) for i in range(128)])]
    ppermute x3, waiting for transfers between devices: 33.8 us -> 50.2 us  [shift(): lax.ppermute(value, AXES, [(i, (i + 4 * steps) % 128) for i in range(128)])]
    unnamed x209 -> x196, local copies, waits for them, and re-layouts: 56.8 us -> 46 us
    pallas_call x6 -> x4, Pallas kernels: 12.8 us -> 8.73 us  [the longest x1 4.38 us: place(): pl.pallas_call(place_kernel, out_shape=shape((4, 4, rows, 3 * D), F32), g...]
  transfers between devices with their start and end apart: 86 -> 69, of which waited for: 34 -> 34; matrix products, arithmetic and copies ran while one was open for 3% -> 2% of each run, Pallas kernels for 24% -> 27%
where the time goes in v1:
time: 573 us; the launch traced here: 566 us
  waiting for transfers between devices  220 us (38%)
  Pallas kernels  200 us (35%)
  starting transfers between devices  70.2 us (12%)
  local copies, waits for them, and re-layouts  51.1 us (9%)
  between operations  15.7 us (3%)
  other arithmetic  7.63 us (1%)
    ppermute x64, waiting for transfers between devices, swap(): return lax.ppermute(value, AXES, [(i, i ^ mask) for i in range(128)])  170 us
    ppermute x64, starting transfers between devices, swap(): return lax.ppermute(value, AXES, [(i, i ^ mask) for i in range(128)])  68.5 us
    ppermute x3, waiting for transfers between devices, shift(): lax.ppermute(value, AXES, [(i, (i + 4 * steps) % 128) for i in range(128)])  50.2 us
    unnamed x196, local copies, waits for them, and re-layouts  46 us
    pallas_call x2, Pallas kernels, attend_back(): pl.pallas_call(lambda *refs: attend_back_kernel(own, *refs), out_shape=[s...  41.3 us
    pallas_call x1, Pallas kernels, feed(): pl.pallas_call(feed_kernel, out_shape=[shape((TOKENS, FF)), shape((TOKENS...  26.8 us
    pallas_call x1, Pallas kernels, attend(): pl.pallas_call(attend_kernel, out_shape=[shape((FPD, PR, HC))] * 2 + [sha...  24.9 us
    pallas_call x1, Pallas kernels, down_weight_grad(): pl.pallas_call(down_weight_kernel, out_shape=[shape((2, D, D))] * 2 + [sh...  21.9 us
  transfers between devices with their start and end apart: 69, of which 34 were waited for; matrix products, arithmetic and copies ran while one was open for 2% of the time, Pallas kernels for 27%

profile of v1, /device:TPU:6, one launch (start us, length us, event | category | flops | bytes accessed | tf_op | source)
XLA Modules:
  0.0 565.9 jit_solution(4148960081142271723)
XLA Ops:
  19.2 18.3 %collective-permute-done.3 = f32[8,7424]{1,0:T(8,128)S(1)} collective-permute-done((f32[8,7424]{1,0:T(8,128)S(1)}, f32[8,7424]{1,0:T(8,128)S(1)}, u32[]{:S(2)}, u32[]{:S(2)}) %collective-permute-start.3) | collective-permute-done | bytes 237600 | tf_op jit(solution)/shard_map/ppermute | solution.py:27
  37.6 21.6 %collective-permute-done.1.refs_1_ = bf16[7,64,1024]{2,1,0:T(8,128)(2,1)} collective-permute-done((bf16[7,64,1024]{2,1,0:T(8,128)(2,1)}, bf16[7,64,1024]{2,1,0:T(8,128)(2,1)}, u32[]{:S(2)}, u32[]{:S(2)}) %collective-permute-start.1) | collective-permute-done | bytes 917536 | tf_op jit(solution)/shard_map/ppermute | solution.py:31
  62.7 10.0 %project_own.1 = (bf16[8,256,1024]{2,1,0:T(8,128)(2,1)S(1)}, bf16[8,256,256]{2,1,0:T(8,128)(2,1)S(1)}, bf16[8,256,256]{2,1,0:T(8,128)(2,1)S(1)}, bf16[8,256,256]{2,1,0:T(8,128)(2,1)S(1)}) custom-call(s32[1]{0:T(128)} %bitcast.row_ref.refs_0_, bf16[8,64,1024]{2,1,0:T(8,128)(2,1)S(1)} %copy-done.3, bf16[8,64,1024]{2,1,0:T(8,128)(2,1)S(1)} %collective-permute-done.7.refs_2_, ...), custom_call_target="tpu_custom_call" | custom-call | flops 3221225472 | bytes 12582912 | tf_op jit(solution)/shard_map/project_own/pallas_call | solution.py:280
  75.7 12.1 %collective-permute-done.10.refs_6_ = f32[8,2048]{1,0:T(8,128)S(1)} collective-permute-done((f32[8,2048]{1,0:T(8,128)S(1)}, f32[8,2048]{1,0:T(8,128)S(1)}, u32[]{:S(2)}, u32[]{:S(2)}) %collective-permute-start.10) | collective-permute-done | bytes 65568 | tf_op jit(solution)/shard_map/ppermute | solution.py:31
  94.8 8.1 %project_prev.1 = (bf16[7,256,256]{2,1,0:T(8,128)(2,1)S(1)}, bf16[7,256,256]{2,1,0:T(8,128)(2,1)S(1)}) custom-call(s32[1]{0:T(128)} %bitcast.row_ref.refs_0_, bf16[7,64,1024]{2,1,0:T(8,128)(2,1)} %collective-permute-done.1.refs_1_, bf16[7,64,1024]{2,1,0:T(8,128)(2,1)S(1)} %collective-permute-done.11.refs_2_, ...), custom_call_target="tpu_custom_call" | custom-call | flops 2818572288 | bytes 11534336 | tf_op jit(solution)/shard_map/project_prev/pallas_call | solution.py:280
  104.9 24.9 %attend.1 = (bf16[8,64,256]{2,1,0:T(8,128)(2,1)}, bf16[8,64,256]{2,1,0:T(8,128)(2,1)}, bf16[2,8,64,256]{3,2,1,0:T(8,128)(2,1)}, f32[8,8,256]{2,1,0:T(8,128)}) custom-call(s32[8]{0:T(128)} %refs_0_.3, bf16[8,256,256]{2,1,0:T(8,128)(2,1)} %copy-done.23, bf16[8,256,256]{2,1,0:T(8,128)(2,1)} %copy-done.24, bf16[8,256,256]{2,1,0:T(8,128)(2,1)} %copy-done.25, ...), custom_call_target="tpu_custom_call" | custom-call | flops 9663676416 | bytes 6291456 | tf_op jit(solution)/shard_map/attend/pallas_call | solution.py:367
  130.4 4.1 collective-permute-done.19.d2
  136.0 13.2 %collective-permute-done.14 = bf16[2,8,64,256]{3,2,1,0:T(8,128)(2,1)S(1)} collective-permute-done((bf16[2,8,64,256]{3,2,1,0:T(8,128)(2,1)}, bf16[2,8,64,256]{3,2,1,0:T(8,128)(2,1)S(1)}, u32[]{:S(2)}, u32[]{:S(2)}) %collective-permute-start.14) | collective-permute-done | bytes 524320 | tf_op jit(solution)/shard_map/ppermute | solution.py:27
  164.3 26.8 %feed.1 = (bf16[512,4096]{1,0:T(8,128)(2,1)}, bf16[512,4096]{1,0:T(8,128)(2,1)}, f32[512,1024]{1,0:T(8,128)}, f32[8,512]{1,0:T(8,128)}) custom-call(s32[1]{0:T(128)} %bitcast.row_ref.refs_0_, bf16[512,1024]{1,0:T(8,128)(2,1)} %bitcast.65, bf16[512,1024]{1,0:T(8,128)(2,1)} %bitcast.67, bf16[256,4096]{1,0:T(8,128)(2,1)} %u0.1, ...), custom_call_target="tpu_custom_call" | custom-call | flops 12884901888 | bytes 31457280 | tf_op jit(solution)/shard_map/feed/pallas_call | solution.py:681
  195.3 3.8 mid_back.1
  207.3 21.9 %down_weight_grad.1 = (bf16[2,1024,1024]{2,1,0:T(8,128)(2,1)}, bf16[2,1024,1024]{2,1,0:T(8,128)(2,1)}, bf16[8,64,1024]{2,1,0:T(8,128)(2,1)}, f32[8,1024]{1,0:T(8,128)}) custom-call(s32[1]{0:T(128)} %bitcast.row_ref.refs_0_, bf16[512,1024]{1,0:T(8,128)(2,1)} %bitcast.68, bf16[512,4096]{1,0:T(8,128)(2,1)} %get-tuple-element.181.act, bf16[1024,1024]{1,0:T(8,128)(2,1)} %d0.3, ...), custom_call_target="tpu_custom_call" | custom-call | flops 8589934592 | bytes 25165824 | tf_op jit(solution)/shard_map/down_weight_grad/pallas_call | solution.py:746
  230.5 11.0 %up_weight_grad.1 = (bf16[2,4,256,1024]{3,2,1,0:T(8,128)(2,1)}, bf16[2,4,256,1024]{3,2,1,0:T(8,128)(2,1)}) custom-call(s32[1]{0:T(128)} %bitcast.row_ref.refs_0_, bf16[512,1024]{1,0:T(8,128)(2,1)} %bitcast.66, bf16[512,4096]{1,0:T(8,128)(2,1)} %get-tuple-element.193.upg), custom_call_target="tpu_custom_call" | custom-call | flops 4294967296 | bytes 14680064 | tf_op jit(solution)/shard_map/up_weight_grad/pallas_call | solution.py:776
  247.5 5.8 %collective-permute-start.29 = (bf16[8,4096]{1,0:T(8,128)(2,1)S(1)}, bf16[8,4096]{1,0:T(8,128)(2,1)S(1)}, u32[]{:S(2)}, u32[]{:S(2)}) collective-permute-start(bf16[8,4096]{1,0:T(8,128)(2,1)S(1)} %pad_maximum_fusion.3), channel_id=1, source_target_pairs={{0,64},{1,65},{2,66},{3,67},{4,68},{5,69},{6,70},{7,71},{8,72},{9,... | collective-permute-start | bytes 196616 | tf_op jit(solution)/shard_map/ppermute | solution.py:27
  256.9 12.2 %attend_back_prev.1 = (f32[8,256,256]{2,1,0:T(8,128)}, bf16[2,7,256,256]{3,2,1,0:T(8,128)(2,1)}) custom-call(s32[8]{0:T(128)} %refs_0_.3, bf16[8,256,256]{2,1,0:T(8,128)(2,1)} %copy-done.23, bf16[7,256,256]{2,1,0:T(8,128)(2,1)} %copy-done.76, bf16[7,256,256]{2,1,0:T(8,128)(2,1)} %copy-done.77, bf16[8,64,256]{2,1,0:T(8,128)(2,1)} %copy-done.45, ...), custom_call_target="tpu_custom_call" | custom-call | flops 8053063680 | bytes 12582912 | tf_op jit(solution)/shard_map/attend_back_prev/pallas_call | solution.py:490
  270.1 12.0 %core_sum.1 = bf16[2,2304,1024]{2,1,0:T(8,128)(2,1)} custom-call(bf16[2,4,256,1024]{3,2,1,0:T(8,128)(2,1)} %get-tuple-element.209.ua, bf16[2,4,256,1024]{3,2,1,0:T(8,128)(2,1)} %collective-permute-done.31.ub, bf16[2,1024,1024]{2,1,0:T(8,128)(2,1)} %get-tuple-element.211.da, bf16[2,1024,1024]{2,1,0:T(8,128)(2,1)} %collective-permute-done.32.db, ...), custom_call_target="tpu_custom_call" | custom-call | flops 1000 | bytes 1000 | tf_op jit(solution)/shard_map/core_sum/pallas_call | solution.py:836
  283.0 4.7 collective-permute-start.36
  287.7 29.1 %attend_back_own.1 = (bf16[8,256,256]{2,1,0:T(8,128)(2,1)}, f32[8,256,256]{2,1,0:T(8,128)}, f32[8,256,256]{2,1,0:T(8,128)}) custom-call(s32[8]{0:T(128)} %refs_0_.3, bf16[8,256,256]{2,1,0:T(8,128)(2,1)} %copy-done.23, bf16[8,256,256]{2,1,0:T(8,128)(2,1)} %copy-done.24, bf16[8,256,256]{2,1,0:T(8,128)(2,1)} %copy-done.25, bf16[8,64,256]{2,1,0:T(8,128)(2,1)} %copy-done.45, ...), custom_call_target="tpu_custom_call" | custom-call | flops 1000 | bytes 1000 | tf_op jit(solution)/shard_map/attend_back_own/pallas_call | solution.py:490
  316.9 16.5 %collective-permute-done.37.rk.rv = bf16[2,7,256,256]{3,2,1,0:T(8,128)(2,1)S(1)} collective-permute-done((bf16[2,7,256,256]{3,2,1,0:T(8,128)(2,1)}, bf16[2,7,256,256]{3,2,1,0:T(8,128)(2,1)S(1)}, u32[]{:S(2)}, u32[]{:S(2)}) %collective-permute-start.37) | collective-permute-done | bytes 1835040 | tf_op jit(solution)/shard_map/ppermute | solution.py:31
  337.9 8.1 %project_back.1 = (bf16[8,256,768]{2,1,0:T(8,128)(2,1)S(1)}, bf16[8,64,1024]{2,1,0:T(8,128)(2,1)S(1)}, bf16[8,64,1024]{2,1,0:T(8,128)(2,1)S(1)}, bf16[2,8,64,1024]{3,2,1,0:T(8,128)(2,1)}, f32[8,512]{1,0:T(8,128)S(1)}) custom-call(s32[1]{0:T(128)} %bitcast.row_ref.refs_0_, bf16[8,256,256]{2,1,0:T(8,128)(2,1)S(1)} %copy-done.63, ...), custom_call_target="tpu_custom_call" | custom-call | flops 3221225472 | bytes 14680064 | tf_op jit(solution)/shard_map/project_back/pallas_call | solution.py:969
  349.7 4.4 collective-permute-done.38.near
  358.0 4.8 project_weight.1
  363.0 11.8 %collective-permute-start.42 = (bf16[4,64,768]{2,1,0:T(8,128)(2,1)S(1)}, bf16[4,64,768]{2,1,0:T(8,128)(2,1)S(1)}, u32[]{:S(2)}, u32[]{:S(2)}) collective-permute-start(bf16[4,64,768]{2,1,0:T(8,128)(2,1)S(1)} %get-tuple-element.270), channel_id=1, source_target_pairs={{0,12},{1,13},{2,14},{3,15},{4,8},{5,9},{6,10},{7,11},{8,4},{9,5},... | collective-permute-start | bytes 1179656 | tf_op jit(solution)/shard_map/ppermute | solution.py:27
  375.8 23.4 %collective-permute-done.42 = bf16[4,64,768]{2,1,0:T(8,128)(2,1)S(1)} collective-permute-done((bf16[4,64,768]{2,1,0:T(8,128)(2,1)S(1)}, bf16[4,64,768]{2,1,0:T(8,128)(2,1)S(1)}, u32[]{:S(2)}, u32[]{:S(2)}) %collective-permute-start.42) | collective-permute-done | bytes 393248 | tf_op jit(solution)/shard_map/ppermute | solution.py:27
  401.6 4.9 collective-permute-start.44
  433.2 5.4 collective-permute-done.56.refs_5_
  439.4 14.2 %collective-permute-done.57.refs_6_ = bf16[8,8,4096]{2,1,0:T(8,128)(2,1)S(1)} collective-permute-done((bf16[8,8,4096]{2,1,0:T(8,128)(2,1)S(1)}, bf16[8,8,4096]{2,1,0:T(8,128)(2,1)S(1)}, u32[]{:S(2)}, u32[]{:S(2)}) %collective-permute-start.57) | collective-permute-done | bytes 524320 | tf_op jit(solution)/shard_map/ppermute | solution.py:27
  473.6 4.4 collective-permute-done.60
  490.4 16.4 %collective-permute-done.64.refs_1_.a1 = bf16[4,16,6656]{2,1,0:T(8,128)(2,1)} collective-permute-done((bf16[4,16,6656]{2,1,0:T(8,128)(2,1)}, bf16[4,16,6656]{2,1,0:T(8,128)(2,1)}, u32[]{:S(2)}, u32[]{:S(2)}) %collective-permute-start.64) | collective-permute-done | bytes 852000 | tf_op jit(solution)/shard_map/ppermute | solution.py:27
  506.8 26.8 %collective-permute-done.65.refs_2_.a2 = bf16[4,16,6656]{2,1,0:T(8,128)(2,1)} collective-permute-done((bf16[4,16,6656]{2,1,0:T(8,128)(2,1)}, bf16[4,16,6656]{2,1,0:T(8,128)(2,1)}, u32[]{:S(2)}, u32[]{:S(2)}) %collective-permute-start.65) | collective-permute-done | bytes 852000 | tf_op jit(solution)/shard_map/ppermute | solution.py:27
  539.0 7.9 %final_sums.1 = (f32[256,6144]{1,0:T(8,128)}, f32[1,1536]{1,0:T(1,128)S(1)}, f32[1,768]{1,0:T(1,128)S(1)}, f32[1,256]{1,0:T(1,128)}, f32[1,1024]{1,0:T(1,128)}, /*index=5*/f32[1,256]{1,0:T(1,128)}) custom-call(s32[1]{0:T(128)} %bitcast.row_ref.refs_0_, bf16[4,16,6656]{2,1,0:T(8,128)(2,1)S(1)} %copy-done.4, ...), custom_call_target="tpu_custom_call" | custom-call | flops 805306368 | bytes 10485760 | tf_op jit(solution)/shard_map/final_sums/pallas_call | solution.py:1117
  548.1 4.4 place.1
  554.8 3.7 unpack.1
  (369 shorter events, 153.4 us)
Async XLA Ops:
  7.2 449.9 %reduce-scatter.2.cloned.1.call-start = ((), (), s32[]{:S(2)}) async-start(), calls=%async_computation.1 | async-start | bytes 10027008 | tf_op jit(solution)/shard_map/reduce_scatter | solution.py:1266
  7.2 51.9 %collective-permute-start = (bf16[8,64,1024]{2,1,0:T(8,128)(2,1)}, bf16[8,64,1024]{2,1,0:T(8,128)(2,1)S(1)}, u32[]{:S(2)}, u32[]{:S(2)}) collective-permute-start(bf16[8,64,1024]{2,1,0:T(8,128)(2,1)} %x.3), channel_id=1, source_target_pairs={{0,2},{1,3},{2,0},{3,1},{4,6},{5,7},{6,4},{7,5},{8,10},{9,11},{10,... | collective-permute-start | bytes 3145736 | tf_op jit(solution)/shard_map/ppermute | solution.py:27
  10.4 48.8 %collective-permute-start.1 = (bf16[7,64,1024]{2,1,0:T(8,128)(2,1)}, bf16[7,64,1024]{2,1,0:T(8,128)(2,1)}, u32[]{:S(2)}, u32[]{:S(2)}) collective-permute-start(bf16[7,64,1024]{2,1,0:T(8,128)(2,1)} %slice.63), channel_id=1, source_target_pairs={{0,4},{1,5},{2,6},{3,7},{4,8},{5,9},{6,10},{7,11},{8,12},{9,13},{1... | collective-permute-start | bytes 2752520 | tf_op jit(solution)/shard_map/ppermute | solution.py:31
  12.6 25.0 %collective-permute-start.5 = (bf16[2,256,768]{2,1,0:T(8,128)(2,1)S(1)}, bf16[2,256,768]{2,1,0:T(8,128)(2,1)S(1)}, u32[]{:S(2)}, u32[]{:S(2)}) collective-permute-start(bf16[2,256,768]{2,1,0:T(8,128)(2,1)S(1)} %get-tuple-element.146), channel_id=1, source_target_pairs={{0,66},{1,67},{2,64},{3,65},{4,70},{5,71},{6,68},{7,69},{8,74},{9,... | collective-permute-start | bytes 2359304 | tf_op jit(solution)/shard_map/ppermute | solution.py:27
  59.2 28.6 %collective-permute-start.6 = (bf16[7,64,1024]{2,1,0:T(8,128)(2,1)}, bf16[7,64,1024]{2,1,0:T(8,128)(2,1)S(1)}, u32[]{:S(2)}, u32[]{:S(2)}) collective-permute-start(bf16[7,64,1024]{2,1,0:T(8,128)(2,1)} %collective-permute-done.1.refs_1_), channel_id=1, source_target_pairs={{0,2},{1,3},{2,0},{3,1},{4,6},{5,7},{6,4},{7,5},{8,10},{9,11},{10,... | collective-permute-start | bytes 2752520 | tf_op jit(solution)/shard_map/ppermute | solution.py:27
  60.4 27.3 %collective-permute-start.10 = (f32[8,2048]{1,0:T(8,128)S(1)}, f32[8,2048]{1,0:T(8,128)S(1)}, u32[]{:S(2)}, u32[]{:S(2)}) collective-permute-start(f32[8,2048]{1,0:T(8,128)S(1)} %slice.66), channel_id=1, source_target_pairs={{0,4},{1,5},{2,6},{3,7},{4,8},{5,9},{6,10},{7,11},{8,12},{9,13},{1... | collective-permute-start | bytes 196616 | tf_op jit(solution)/shard_map/ppermute | solution.py:31
  60.5 70.0 %collective-permute-start.18 = (bf16[256,4096]{1,0:T(8,128)(2,1)}, bf16[256,4096]{1,0:T(8,128)(2,1)}, u32[]{:S(2)}, u32[]{:S(2)}) collective-permute-start(bf16[256,4096]{1,0:T(8,128)(2,1)} %u0.1), channel_id=1, source_target_pairs={{0,66},{1,67},{2,64},{3,65},{4,70},{5,71},{6,68},{7,69},{8,74},{9,... | collective-permute-start | bytes 6291464 | tf_op jit(solution)/shard_map/ppermute | solution.py:27
  87.8 46.7 %collective-permute-start.19 = (bf16[1024,1024]{1,0:T(8,128)(2,1)}, bf16[1024,1024]{1,0:T(8,128)(2,1)}, u32[]{:S(2)}, u32[]{:S(2)}) collective-permute-start(bf16[1024,1024]{1,0:T(8,128)(2,1)} %d0.3), channel_id=1, source_target_pairs={{0,2},{1,3},{2,0},{3,1},{4,6},{5,7},{6,4},{7,5},{8,10},{9,11},{10,... | collective-permute-start | bytes 6291464 | tf_op jit(solution)/shard_map/ppermute | solution.py:27
  89.2 46.0 %collective-permute-start.16 = (bf16[256,1024]{1,0:T(8,128)(2,1)S(1)}, bf16[256,1024]{1,0:T(8,128)(2,1)S(1)}, u32[]{:S(2)}, u32[]{:S(2)}) collective-permute-start(bf16[256,1024]{1,0:T(8,128)(2,1)S(1)} %copy-done.17), channel_id=1, source_target_pairs={{0,1},{1,0},{2,3},{3,2},{4,5},{5,4},{6,7},{7,6},{8,9},{9,8},{10,11... | collective-permute-start | bytes 1572872 | tf_op jit(solution)/shard_map/ppermute | solution.py:27
  92.6 37.2 %collective-permute-start.17 = (bf16[256,1024]{1,0:T(8,128)(2,1)S(1)}, bf16[256,1024]{1,0:T(8,128)(2,1)S(1)}, u32[]{:S(2)}, u32[]{:S(2)}) collective-permute-start(bf16[256,1024]{1,0:T(8,128)(2,1)S(1)} %copy-done.17), channel_id=1, source_target_pairs={{0,66},{1,67},{2,64},{3,65},{4,70},{5,71},{6,68},{7,69},{8,74},{9,... | collective-permute-start | bytes 1572872 | tf_op jit(solution)/shard_map/ppermute | solution.py:27
  94.7 66.9 %collective-permute-start.21 = (bf16[256,4096]{1,0:T(8,128)(2,1)}, bf16[256,4096]{1,0:T(8,128)(2,1)}, u32[]{:S(2)}, u32[]{:S(2)}) collective-permute-start(bf16[256,4096]{1,0:T(8,128)(2,1)} %u0.1), channel_id=1, source_target_pairs={{0,1},{1,0},{2,3},{3,2},{4,5},{5,4},{6,7},{7,6},{8,9},{9,8},{10,11... | collective-permute-start | bytes 6291464 | tf_op jit(solution)/shard_map/ppermute | solution.py:27
  129.8 31.9 %collective-permute-start.23 = (bf16[1024,1024]{1,0:T(8,128)(2,1)}, bf16[1024,1024]{1,0:T(8,128)(2,1)S(1)}, u32[]{:S(2)}, u32[]{:S(2)}) collective-permute-start(bf16[1024,1024]{1,0:T(8,128)(2,1)} %d0.3), channel_id=1, source_target_pairs={{0,1},{1,0},{2,3},{3,2},{4,5},{5,4},{6,7},{7,6},{8,9},{9,8},{10,11... | collective-permute-start | bytes 6291464 | tf_op jit(solution)/shard_map/ppermute | solution.py:27
  134.5 27.2 %collective-permute-start.22 = (bf16[256,4096]{1,0:T(8,128)(2,1)}, bf16[256,4096]{1,0:T(8,128)(2,1)S(1)}, u32[]{:S(2)}, u32[]{:S(2)}) collective-permute-start(bf16[256,4096]{1,0:T(8,128)(2,1)} %collective-permute-done.18.u2), channel_id=1, source_target_pairs={{0,1},{1,0},{2,3},{3,2},{4,5},{5,4},{6,7},{7,6},{8,9},{9,8},{10,11... | collective-permute-start | bytes 6291464 | tf_op jit(solution)/shard_map/ppermute | solution.py:27
  134.7 27.1 %collective-permute-start.24 = (bf16[1024,1024]{1,0:T(8,128)(2,1)}, bf16[1024,1024]{1,0:T(8,128)(2,1)S(1)}, u32[]{:S(2)}, u32[]{:S(2)}) collective-permute-start(bf16[1024,1024]{1,0:T(8,128)(2,1)} %collective-permute-done.19.d2), channel_id=1, source_target_pairs={{0,1},{1,0},{2,3},{3,2},{4,5},{5,4},{6,7},{7,6},{8,9},{9,8},{10,11... | collective-permute-start | bytes 6291464 | tf_op jit(solution)/shard_map/ppermute | solution.py:27
  205.9 23.9 %collective-permute-start.25 = (f32[8,3840]{1,0:T(8,128)}, f32[8,3840]{1,0:T(8,128)S(1)}, u32[]{:S(2)}, u32[]{:S(2)}) collective-permute-start(f32[8,3840]{1,0:T(8,128)} %early_sums.1), channel_id=1, source_target_pairs={{0,1},{1,0},{2,3},{3,2},{4,5},{5,4},{6,7},{7,6},{8,9},{9,8},{10,11... | collective-permute-start | bytes 368648 | tf_op jit(solution)/shard_map/ppermute | solution.py:27
  229.2 39.9 %collective-permute-start.32 = (bf16[2,1024,1024]{2,1,0:T(8,128)(2,1)}, bf16[2,1024,1024]{2,1,0:T(8,128)(2,1)}, u32[]{:S(2)}, u32[]{:S(2)}) collective-permute-start(bf16[2,1024,1024]{2,1,0:T(8,128)(2,1)} %get-tuple-element.212), channel_id=1, source_target_pairs={{0,1},{1,0},{2,3},{3,2},{4,5},{5,4},{6,7},{7,6},{8,9},{9,8},{10,11... | collective-permute-start | bytes 12582920 | tf_op jit(solution)/shard_map/ppermute | solution.py:27
  241.5 27.6 %collective-permute-start.31 = (bf16[2,4,256,1024]{3,2,1,0:T(8,128)(2,1)}, bf16[2,4,256,1024]{3,2,1,0:T(8,128)(2,1)}, u32[]{:S(2)}, u32[]{:S(2)}) collective-permute-start(bf16[2,4,256,1024]{3,2,1,0:T(8,128)(2,1)} %get-tuple-element.210), channel_id=1, source_target_pairs={{0,1},{1,0},{2,3},{3,2},{4,5},{5,4},{6,7},{7,6},{8,9},{9,8},{10,11... | collective-permute-start | bytes 12582920 | tf_op jit(solution)/shard_map/ppermute | solution.py:27
  245.0 24.1 %collective-permute-start.33 = (bf16[2,256,1024]{2,1,0:T(8,128)(2,1)S(1)}, bf16[2,256,1024]{2,1,0:T(8,128)(2,1)S(1)}, u32[]{:S(2)}, u32[]{:S(2)}) collective-permute-start(bf16[2,256,1024]{2,1,0:T(8,128)(2,1)S(1)} %get-tuple-element.214), channel_id=1, source_target_pairs={{0,1},{1,0},{2,3},{3,2},{4,5},{5,4},{6,7},{7,6},{8,9},{9,8},{10,11... | collective-permute-start | bytes 3145736 | tf_op jit(solution)/shard_map/ppermute | solution.py:27
  282.1 270.4 %all-gather.2.cloned.1.call-start = ((), (), s32[]{:S(2)}) async-start(), calls=%async_computation.2 | async-start | bytes 5013504 | tf_op jit(solution)/shard_map/all_gather | solution.py:1307
  282.3 51.2 %collective-permute-start.37 = (bf16[2,7,256,256]{3,2,1,0:T(8,128)(2,1)}, bf16[2,7,256,256]{3,2,1,0:T(8,128)(2,1)S(1)}, u32[]{:S(2)}, u32[]{:S(2)}) collective-permute-start(bf16[2,7,256,256]{3,2,1,0:T(8,128)(2,1)} %get-tuple-element.221), channel_id=1, source_target_pairs={{0,124},{1,125},{2,126},{3,127},{4,0},{5,1},{6,2},{7,3},{8,4},{9,5... | collective-permute-start | bytes 5505032 | tf_op jit(solution)/shard_map/ppermute | solution.py:31
  283.0 33.8 %collective-permute-start.34 = (bf16[2,8,4096]{2,1,0:T(8,128)(2,1)S(1)}, bf16[2,8,4096]{2,1,0:T(8,128)(2,1)S(1)}, u32[]{:S(2)}, u32[]{:S(2)}) collective-permute-start(bf16[2,8,4096]{2,1,0:T(8,128)(2,1)S(1)} %copy-done.80), channel_id=1, source_target_pairs={{0,16},{1,17},{2,18},{3,19},{4,20},{5,21},{6,22},{7,23},{8,24},{9,... | collective-permute-start | bytes 393224 | tf_op jit(solution)/shard_map/ppermute | solution.py:27
  283.0 33.8 %collective-permute-start.35 = (bf16[2,8,4096]{2,1,0:T(8,128)(2,1)S(1)}, bf16[2,8,4096]{2,1,0:T(8,128)(2,1)S(1)}, u32[]{:S(2)}, u32[]{:S(2)}) collective-permute-start(bf16[2,8,4096]{2,1,0:T(8,128)(2,1)S(1)} %copy-done.80), channel_id=1, source_target_pairs={{0,32},{1,33},{2,34},{3,35},{4,36},{5,37},{6,38},{7,39},{8,40},{9,... | collective-permute-start | bytes 393224 | tf_op jit(solution)/shard_map/ppermute | solution.py:27
  283.0 33.9 %collective-permute-start.36 = (bf16[2,8,4096]{2,1,0:T(8,128)(2,1)S(1)}, bf16[2,8,4096]{2,1,0:T(8,128)(2,1)S(1)}, u32[]{:S(2)}, u32[]{:S(2)}) collective-permute-start(bf16[2,8,4096]{2,1,0:T(8,128)(2,1)S(1)} %copy-done.80), channel_id=1, source_target_pairs={{0,48},{1,49},{2,50},{3,51},{4,52},{5,53},{6,54},{7,55},{8,56},{9,... | collective-permute-start | bytes 393224 | tf_op jit(solution)/shard_map/ppermute | solution.py:27
  355.7 45.8 %collective-permute-start.39 = (bf16[8,64,1024]{2,1,0:T(8,128)(2,1)S(1)}, bf16[8,64,1024]{2,1,0:T(8,128)(2,1)S(1)}, u32[]{:S(2)}, u32[]{:S(2)}) collective-permute-start(bf16[8,64,1024]{2,1,0:T(8,128)(2,1)S(1)} %fusion), channel_id=1, source_target_pairs={{0,2},{1,3},{2,0},{3,1},{4,6},{5,7},{6,4},{7,5},{8,10},{9,11},{10,... | collective-permute-start | bytes 3145736 | tf_op jit(solution)/shard_map/ppermute | solution.py:27
  363.0 36.3 %collective-permute-start.42 = (bf16[4,64,768]{2,1,0:T(8,128)(2,1)S(1)}, bf16[4,64,768]{2,1,0:T(8,128)(2,1)S(1)}, u32[]{:S(2)}, u32[]{:S(2)}) collective-permute-start(bf16[4,64,768]{2,1,0:T(8,128)(2,1)S(1)} %get-tuple-element.270), channel_id=1, source_target_pairs={{0,12},{1,13},{2,14},{3,15},{4,8},{5,9},{6,10},{7,11},{8,4},{9,5},... | collective-permute-start | bytes 1179656 | tf_op jit(solution)/shard_map/ppermute | solution.py:27
  374.8 24.5 %collective-permute-start.41 = (bf16[4,64,768]{2,1,0:T(8,128)(2,1)S(1)}, bf16[4,64,768]{2,1,0:T(8,128)(2,1)S(1)}, u32[]{:S(2)}, u32[]{:S(2)}) collective-permute-start(bf16[4,64,768]{2,1,0:T(8,128)(2,1)S(1)} %get-tuple-element.271), channel_id=1, source_target_pairs={{0,8},{1,9},{2,10},{3,11},{4,12},{5,13},{6,14},{7,15},{8,0},{9,1},... | collective-permute-start | bytes 1179656 | tf_op jit(solution)/shard_map/ppermute | solution.py:27
  374.8 26.5 %collective-permute-start.40 = (bf16[4,64,768]{2,1,0:T(8,128)(2,1)S(1)}, bf16[4,64,768]{2,1,0:T(8,128)(2,1)S(1)}, u32[]{:S(2)}, u32[]{:S(2)}) collective-permute-start(bf16[4,64,768]{2,1,0:T(8,128)(2,1)S(1)} %get-tuple-element.269), channel_id=1, source_target_pairs={{0,4},{1,5},{2,6},{3,7},{4,0},{5,1},{6,2},{7,3},{8,12},{9,13},{10,... | collective-permute-start | bytes 1179656 | tf_op jit(solution)/shard_map/ppermute | solution.py:27
  419.0 34.6 %collective-permute-start.57 = (bf16[8,8,4096]{2,1,0:T(8,128)(2,1)S(1)}, bf16[8,8,4096]{2,1,0:T(8,128)(2,1)S(1)}, u32[]{:S(2)}, u32[]{:S(2)}) collective-permute-start(bf16[8,8,4096]{2,1,0:T(8,128)(2,1)S(1)} %pad_maximum_fusion.1.refs_4_), channel_id=1, source_target_pairs={{0,8},{1,9},{2,10},{3,11},{4,12},{5,13},{6,14},{7,15},{8,0},{9,1},... | collective-permute-start | bytes 1572872 | tf_op jit(solution)/shard_map/ppermute | solution.py:27
  421.2 35.1 %collective-permute-start.58 = (bf16[8,8,4096]{2,1,0:T(8,128)(2,1)S(1)}, bf16[8,8,4096]{2,1,0:T(8,128)(2,1)S(1)}, u32[]{:S(2)}, u32[]{:S(2)}) collective-permute-start(bf16[8,8,4096]{2,1,0:T(8,128)(2,1)S(1)} %pad_maximum_fusion.1.refs_4_), channel_id=1, source_target_pairs={{0,12},{1,13},{2,14},{3,15},{4,8},{5,9},{6,10},{7,11},{8,4},{9,5},... | collective-permute-start | bytes 1572872 | tf_op jit(solution)/shard_map/ppermute | solution.py:27
  479.8 27.0 %collective-permute-start.64 = (bf16[4,16,6656]{2,1,0:T(8,128)(2,1)}, bf16[4,16,6656]{2,1,0:T(8,128)(2,1)}, u32[]{:S(2)}, u32[]{:S(2)}) collective-permute-start(bf16[4,16,6656]{2,1,0:T(8,128)(2,1)} %pad_maximum_fusion.refs_0_.a0), channel_id=1, source_target_pairs={{0,4},{1,5},{2,6},{3,7},{4,0},{5,1},{6,2},{7,3},{8,12},{9,13},{10,... | collective-permute-start | bytes 2555912 | tf_op jit(solution)/shard_map/ppermute | solution.py:27
  479.9 53.7 %collective-permute-start.65 = (bf16[4,16,6656]{2,1,0:T(8,128)(2,1)}, bf16[4,16,6656]{2,1,0:T(8,128)(2,1)}, u32[]{:S(2)}, u32[]{:S(2)}) collective-permute-start(bf16[4,16,6656]{2,1,0:T(8,128)(2,1)} %pad_maximum_fusion.refs_0_.a0), channel_id=1, source_target_pairs={{0,8},{1,9},{2,10},{3,11},{4,12},{5,13},{6,14},{7,15},{8,0},{9,1},... | collective-permute-start | bytes 2555912 | tf_op jit(solution)/shard_map/ppermute | solution.py:27
  482.0 51.6 %collective-permute-start.66 = (bf16[4,16,6656]{2,1,0:T(8,128)(2,1)}, bf16[4,16,6656]{2,1,0:T(8,128)(2,1)}, u32[]{:S(2)}, u32[]{:S(2)}) collective-permute-start(bf16[4,16,6656]{2,1,0:T(8,128)(2,1)} %pad_maximum_fusion.refs_0_.a0), channel_id=1, source_target_pairs={{0,12},{1,13},{2,14},{3,15},{4,8},{5,9},{6,10},{7,11},{8,4},{9,5},... | collective-permute-start | bytes 2555912 | tf_op jit(solution)/shard_map/ppermute | solution.py:27
  (135 other events, 2059.2 us)
Sparse Core Ops, SparseCore 0:
  282.3 174.7 reduce-scatter.1
  479.0 65.3 all-gather.1

commit v2 on v1

--- a/solution.py
+++ b/solution.py
@@ -814,63 +814,69 @@
 ROWS = FIRST + DOWN_ROWS
 
 
-def core_sum_kernel(ua, ub, da, db, oa, ob, out):
+def core_sum_kernel(ua, ub, oa, ob, out):
     def both(a, b):
         return (a.astype(F32) + b.astype(F32)).astype(BF16)
 
     for c in range(4):
-        at = c * ROWS
+        at = c * FIRST
         low, high = c * OUT_ROWS, (c + 1) * OUT_ROWS
         for i in range(4):
             to = at + i * OUT_ROWS
             out[0, to : to + OUT_ROWS] = both(ua[0, i, low:high], ub[0, i, low:high])
         out[0, at + UP_ROWS : at + FIRST] = both(oa[0, low:high], ob[0, low:high])
-        low, high = c * DOWN_ROWS, (c + 1) * DOWN_ROWS
-        out[0, at + FIRST : at + ROWS] = both(da[0, low:high], db[0, low:high])
-
-
-def core_sum(up, down, out):
+
+
+def core_sum(up, out):
     ups = pl.BlockSpec((1, 4, 4 * OUT_ROWS, D), lambda j, c: (j, 0, c, 0))
     outs = pl.BlockSpec((1, 4 * OUT_ROWS, D), lambda j, c: (j, c, 0))
-    downs = pl.BlockSpec((1, 4 * DOWN_ROWS, D), lambda j, c: (j, c, 0))
     return pl.pallas_call(
         core_sum_kernel,
-        out_shape=shape((2, CHUNKS * ROWS, D)),
+        out_shape=shape((2, CHUNKS * FIRST, D)),
         grid=(2, CHUNKS // 4),
-        in_specs=[ups, ups, downs, downs, outs, outs],
-        out_specs=pl.BlockSpec((1, 4 * ROWS, D), lambda j, c: (j, c, 0)),
+        in_specs=[ups, ups, outs, outs],
+        out_specs=pl.BlockSpec((1, 4 * FIRST, D), lambda j, c: (j, c, 0)),
         compiler_params=params(58),
         cost_estimate=cost(1000, 1000),
         name="core_sum",
-    )(*up, *down, *out)
-
-
-def unpack_kernel(total, up, out, down):
-    for k in range(4):
-        at = k * ROWS
-        for i in range(4):
-            rows = slice(at + i * OUT_ROWS, at + (i + 1) * OUT_ROWS)
-            up[k * OUT_ROWS : (k + 1) * OUT_ROWS, i * D : (i + 1) * D] = total[rows].astype(F32)
-        out[k * OUT_ROWS : (k + 1) * OUT_ROWS] = total[at + UP_ROWS : at + FIRST].astype(F32)
-        down[k * DOWN_ROWS : (k + 1) * DOWN_ROWS] = total[at + FIRST : at + ROWS].astype(F32)
-
-
-def unpack(total):
-    block = lambda i: (i, 0)
-    return pl.pallas_call(
-        unpack_kernel,
-        out_shape=[shape((HC, FF), F32), shape((HC, D), F32), shape((D, D), F32)],
-        grid=(4,),
-        in_specs=[pl.BlockSpec((4 * ROWS, D), block)],
-        out_specs=[
-            pl.BlockSpec((4 * OUT_ROWS, FF), block),
-            pl.BlockSpec((4 * OUT_ROWS, D), block),
-            pl.BlockSpec((4 * DOWN_ROWS, D), block),
-        ],
+    )(*up, *out)
+
+
+def spread_kernel(index_ref, *refs):
+    pieces, (up, out) = refs[:4], refs[4:]
+    for m, a in enumerate(pieces):
+
+        @pl.when(pl.program_id(0) == m)
+        def _():
+            for k in range(4):
+                at = index_ref[0] ^ k
+                for i in range(4):
+                    rows = slice(i * OUT_ROWS, (i + 1) * OUT_ROWS)
+                    up[at, 0, :, i * D : (i + 1) * D] = a[k, rows].astype(F32)
+                out[at, 0] = a[k, UP_ROWS:].astype(F32)
+
+
+def spread(index, pieces):
+    def at(i, index):
+        return (0, index[1] ^ i, 0, 0)
+
+    up, out = pl.pallas_call(
+        spread_kernel,
+        out_shape=[shape((4, 4, OUT_ROWS, FF), F32), shape((4, 4, OUT_ROWS, D), F32)],
+        grid_spec=pltpu.PrefetchScalarGridSpec(
+            num_scalar_prefetch=1,
+            grid=(4,),
+            in_specs=[whole((4, FIRST, D))] * 4,
+            out_specs=[
+                pl.BlockSpec((4, 1, OUT_ROWS, FF), at),
+                pl.BlockSpec((4, 1, OUT_ROWS, D), at),
+            ],
+        ),
         compiler_params=params(24),
-        cost_estimate=cost(0, 14 * MB),
-        name="unpack",
-    )(total)
+        cost_estimate=cost(0, 8 * MB),
+        name="spread",
+    )(index, *pieces)
+    return up.reshape(HC, FF), out.reshape(HC, D)
 
 
 LATE = 3 * D + 2 * HC
@@ -904,30 +910,50 @@
     )(row, *pieces, late, far)
 
 
-def place_kernel(index_ref, a0, a1, a2, a3, out):
-    for m, a in enumerate((a0, a1, a2, a3)):
+def stack_kernel(a0, a1, a2, a3, weights, sums):
+    for k, a in enumerate((a0, a1, a2, a3)):
+        weights[k] = a[:, : 3 * D]
+        sums[k] = a[:, 3 * D :]
+
+
+def stack(pieces):
+    rows, width = pieces[0].shape
+    return pl.pallas_call(
+        stack_kernel,
+        out_shape=[shape((4, rows, 3 * D)), shape((4, rows, LATE))],
+        grid=(1,),
+        in_specs=[whole((rows, width))] * 4,
+        out_specs=[whole((4, rows, 3 * D)), whole((4, rows, LATE))],
+        compiler_params=params(16),
+        cost_estimate=cost(0, 2 * MB),
+        name="stack",
+    )(*pieces)
+
+
+def place_kernel(index_ref, low, high, out):
+    for m, a in enumerate((low.at[0], low.at[1], high.at[1], high.at[0])):
 
         @pl.when(pl.program_id(0) == m)
         def _():
             for k in range(4):
-                out[0, index_ref[1] ^ k] = a[k, :, : 3 * D].astype(F32)
-
-
-def place(index, pieces):
-    rows = pieces[0].shape[1]
+                out[0, index_ref[1] ^ k] = a[k].astype(F32)
+
+
+def place(index, low, high):
+    rows = low.shape[2]
     return pl.pallas_call(
         place_kernel,
         out_shape=shape((4, 4, rows, 3 * D), F32),
         grid_spec=pltpu.PrefetchScalarGridSpec(
             num_scalar_prefetch=1,
             grid=(4,),
-            in_specs=[whole(a.shape) for a in pieces],
+            in_specs=[whole(low.shape)] * 2,
             out_specs=pl.BlockSpec((1, 4, rows, 3 * D), lambda i, index: (index[0] ^ i, 0, 0, 0)),
         ),
         compiler_params=params(24),
         cost_estimate=cost(0, 24 * rows * D),
         name="place",
-    )(index, *pieces).reshape(HC, 3 * D)
+    )(index, low, high).reshape(HC, 3 * D)
 
 
 def project_back_kernel(row_ref, dq, dk, dv, rk, rv, w0, w1, w2, w3, cp, sp, fr, dp, h0, h2, hs, bsum):
@@ -1066,14 +1092,15 @@
 
 def final_kernel(row_ref, *refs):
     row = row_ref[0]
-    late, early = refs[:4], refs[4:8]
-    ada, ab, qb, ob, ub, db, asum = refs[8:]
+    low, high, *early = refs[:6]
+    ada, ab, qb, ob, ub, db, asum = refs[6:]
+    late = [low.at[0], low.at[1], high.at[0], high.at[1]]
+    early = [early[0], early[3], early[1], early[2]]
 
     def rows(ref, cols):
         value = ref[:, :, cols].astype(F32)
         return value.reshape(64, value.shape[-1])
 
-    late = [ref.at[:, :, 3 * D :] for ref in late]
     left = [rows(s, slice(EARLY, EARLY + HC)).astype(BF16) for s in early]
     for segment in range(6):
         source, start = ((late, 0), (late, 1), (early, 0), (early, 1), (early, 2), (late, 2))[segment]
@@ -1120,7 +1147,7 @@
         grid_spec=pltpu.PrefetchScalarGridSpec(
             num_scalar_prefetch=1,
             grid=(1,),
-            in_specs=[whole((4, 16, 3 * D + LATE))] * 4
+            in_specs=[whole((2, 4, 16, LATE))] * 2
             + [whole((8, 8, EARLY + HC))] * 4,
             out_specs=[whole((HC, 6 * D))] + [whole((1, n)) for n in sizes],
             scratch_shapes=[pltpu.VMEM((8, 6 * D), F32)],
@@ -1242,49 +1269,65 @@
 
     early = early_sums(sums, usum, dsum)
     early = early + swap(early, CORE)
+    early, dg_later = lax.optimization_barrier((early, dg))
+    early_far = swap(early, DIRECT)
     dk_part, ds_part, layer_output, gate = down_weight_grad(
-        row_arg, after(dg, bg), act, downs, table, middle, cotangent
-    )
-    upg, early, gate, far_back, *back = lax.optimization_barrier((upg, early, gate, *late, *back))
+        row_arg, after(dg_later, bg), act, downs, table, middle, cotangent
+    )
+    ds_part = swap(ds_part, CORE)
+    upg, early_far, gate, far_back, *back = lax.optimization_barrier(
+        (upg, early_far, gate, *late, *back)
+    )
     back += [far_back[0], swap(far_back[1], CORE)]
-    early = early + swap(early, DIRECT)
+    early = jnp.concatenate([(early + early_far).astype(BF16), silu_own], axis=1)
+    early_far = swap(early, FAR)
     uk, us = up_weight_grad(row_arg, h2, upg)
+    us = swap(us, CORE)
+    uk, early, early_far, ds_part = lax.optimization_barrier((uk, early, early_far, ds_part))
+    early = jnp.stack([early, early_far])
+    early_parts = [early] + [swap(early, m) for m in (16, 32, 48)]
     ok, os = out_weight_grad(turned, bg)
-
-    early = jnp.concatenate([early.astype(BF16), silu_own], axis=1)
-    early, uk = lax.optimization_barrier((early, uk))
-    early = jnp.stack([early, swap(early, FAR)])
-    early, uk, ok, *back = lax.optimization_barrier((early, uk, ok, *back))
-    early_parts = [early] + [swap(early, m) for m in (16, 32, 48)]
+    packed_down = (dk_part.astype(F32) + ds_part.astype(F32)).astype(BF16)
+
+    ok, packed_down, early_parts, back = lax.optimization_barrier(
+        (ok, packed_down, early_parts, back)
+    )
+    scattered_down = lax.psum_scatter(packed_down, ("y", "z"), scatter_dimension=1, tiled=True)
     dq_before, both = attend_back(False, frame_position, q, kp, vp, back, mixed, lse)
     returned = shift(both, -1)
     uk, dq_before = lax.optimization_barrier((uk, dq_before))
-    packed = core_sum(
-        (uk, swap(us, CORE)), (dk_part, swap(ds_part, CORE)), (ok, swap(os, CORE))
-    )
+    packed = core_sum((uk, us), (ok, swap(os, CORE)))
     dq_before, packed = lax.optimization_barrier((dq_before, packed))
     scattered = lax.psum_scatter(packed, ("y", "z"), scatter_dimension=1, tiled=True)
     dq, dk, dv = attend_back(
         True, frame_position, q, k, v, back, mixed, lse, tables, dq_before
     )
-    dq, *early_parts = lax.optimization_barrier((dq, *early_parts))
+    early_parts, dq_before = lax.optimization_barrier((early_parts, dq))[0], None
     early = jnp.concatenate(early_parts)
-    early_high = early
+    early_all = [early] + [swap(early, m) for m in (4, 8, 12)]
     early = early[0].astype(F32)
 
     dproj, h0, h2_part, send, bsum = project_back(row_arg, dq, dk, dv, returned, qkv_pieces, tables)
     near = swap(send, CORE)
     qkv_parts = project_weight(row_arg, hidden1, dproj)
     far = swap((h2_part.astype(F32) + near[1].astype(F32)).astype(BF16), DIRECT)
+    qkv_parts, early_all, scattered_down = lax.optimization_barrier(
+        (qkv_parts, early_all, scattered_down)
+    )
+    down_far = swap(scattered_down[1], DIRECT)
     qkv_parts = exchange_rows(qkv_parts, 4, index, 0)
-    far, qkv_parts, early_high = lax.optimization_barrier((far, qkv_parts, early_high))
-    early_all = [early_high] + [swap(early_high, m) for m in (4, 8, 12)]
+    far, qkv_parts, down_far = lax.optimization_barrier((far, qkv_parts, down_far))
+    down_share = scattered_down[0].astype(F32) + down_far.astype(F32)
+    down_far = swap(down_share.astype(BF16), FAR)
     quarters = quarter_rows(qkv_parts, 16, index, 1)
     input_grad, late = input_back(x0, h0, near, far, table, mg, bsum, gate)
     late, *quarters = lax.optimization_barrier((late, *quarters))
     qkv_parts = add_all(quarters)
     late_near = swap(late, CORE)
-    late, late_near, qkv_parts = lax.optimization_barrier((late, late_near, qkv_parts))
+    late, late_near, qkv_parts, down_far = lax.optimization_barrier(
+        (late, late_near, qkv_parts, down_far)
+    )
+    down_share = (down_share + down_far.astype(F32)).astype(BF16)
     late = late + late_near
     late_far = swap(late, DIRECT)
     qkv_far = swap(qkv_parts, FAR)
@@ -1298,17 +1341,25 @@
     turned = turn_heads(qkv_parts[0], qkv_parts[1], qkv_parts[2:])
     last = arrange(row_arg, turned, late_low, late_far)
 
-    scattered, last, *early_all = lax.optimization_barrier((scattered, last, *early_all))
-    last = jnp.stack([last] + [swap(last, m) for m in (16, 32, 48)])
+    down_total = lax.all_gather(down_share, ("y", "z"), axis=0, tiled=True).astype(F32)
+    scattered, last = lax.optimization_barrier((scattered, last))
+    last = [last] + [swap(last, m) for m in (16, 32, 48)]
     share = scattered[0].astype(F32) + swap(scattered[1], DIRECT).astype(F32)
-    share = (share + swap(share.astype(BF16), FAR).astype(F32)).astype(BF16)
     share, last = lax.optimization_barrier((share, last))
-    last_all = [last] + [swap(last, m) for m in (4, 8, 12)]
-    totals = lax.all_gather(share, ("y", "z"), axis=0, tiled=True)
-    up_total, out_total, down_total = unpack(totals)
-    qkv_total = place(index_arg, last_all)
-
-    ada_total, *bias_sums = final_sums(row_arg, last_all, early_all)
+    share_far = swap(share.astype(BF16), FAR)
+    weights, sums_late = stack(last)
+    weights = jnp.stack([weights, swap(weights, 4)])
+    sums_late = jnp.stack([sums_late, swap(sums_late, 12)])
+    share_far, weights, sums_late = lax.optimization_barrier((share_far, weights, sums_late))
+    share = (share + share_far.astype(F32)).astype(BF16)
+    share = jnp.stack([share] + [swap(share, m) for m in (4, 8, 12)])
+    weights_far, sums_far = swap(weights, 12), swap(sums_late, 4)
+    share, sums_far = lax.optimization_barrier((share, sums_far))
+    share_all = [share] + [swap(share, m) for m in (16, 32, 48)]
+    up_total, out_total = spread(index_arg, share_all)
+    qkv_total = place(index_arg, weights, weights_far)
+
+    ada_total, *bias_sums = final_sums(row_arg, (sums_late, sums_far), early_all)
     ada_sum, qkv_sum, out_sum, up_sum, down_sum = [b[0] for b in bias_sums]
     mod_own = jnp.concatenate(
         [late[:, : 2 * D], early[:, : 3 * D], late[:, 2 * D : 3 * D]], axis=1

time: 573 us -> 624 us (1.089)
  waiting for transfers between devices: 220 us -> 249 us
  other arithmetic: 7.63 us -> 23.5 us
  starting transfers between devices: 70.2 us -> 76.8 us
    reduce_scatter x1, waiting for transfers between devices: 0.01 us -> 28.7 us  [per_device(): lax.psum_scatter(packed, ('y', 'z'), scatter_dimension=1, tiled=True)]
    convert_element_type x3 -> x7, other arithmetic: 1.92 us -> 14.3 us  [the longest x1 7.63 us: per_device(): packed_down = (dk_part.astype(F32) + ds_part.astype(F32)).astype(BF16)]
    ppermute x64 -> x73, starting transfers between devices: 68.5 us -> 75.1 us  [swap(): return lax.ppermute(value, AXES, [(i, i ^ mask) for i in range(128)])]
    unnamed x196 -> x199, local copies, waits for them, and re-layouts: 46 us -> 41 us
    pallas_call x2 -> x3, Pallas kernels: 15.7 us -> 13.5 us  [the longest x1 8.65 us: core_sum(): pl.pallas_call(core_sum_kernel, out_shape=shape((2, CHUNKS * FIRST, D)),...]
    ppermute x64 -> x73, waiting for transfers between devices: 170 us -> 169 us  [swap(): return lax.ppermute(value, AXES, [(i, i ^ mask) for i in range(128)])]
  transfers between devices with their start and end apart: 69 -> 79, of which waited for: 34 -> 32; matrix products, arithmetic and copies ran while one was open for 2% -> 6% of each run, Pallas kernels for 27% -> 23%
where the time goes in v2:
time: 624 us; the launch traced here: 614 us
  waiting for transfers between devices  249 us (40%)
  Pallas kernels  198 us (32%)
  starting transfers between devices  76.8 us (12%)
  local copies, waits for them, and re-layouts  49.3 us (8%)
  other arithmetic  23.5 us (4%)
  between operations  15.5 us (2%)
    ppermute x73, waiting for transfers between devices, swap(): return lax.ppermute(value, AXES, [(i, i ^ mask) for i in range(128)])  169 us
    ppermute x73, starting transfers between devices, swap(): return lax.ppermute(value, AXES, [(i, i ^ mask) for i in range(128)])  75.1 us
    ppermute x3, waiting for transfers between devices, shift(): lax.ppermute(value, AXES, [(i, (i + 4 * steps) % 128) for i in range(128)])  51.2 us
    pallas_call x2, Pallas kernels, attend_back(): pl.pallas_call(lambda *refs: attend_back_kernel(own, *refs), out_shape=[s...  41.8 us
    unnamed x199, local copies, waits for them, and re-layouts  41 us
    reduce_scatter x1, waiting for transfers between devices, per_device(): lax.psum_scatter(packed, ('y', 'z'), scatter_dimension=1, tiled=True)  28.7 us
    pallas_call x1, Pallas kernels, feed(): pl.pallas_call(feed_kernel, out_shape=[shape((TOKENS, FF)), shape((TOKENS...  26.9 us
    pallas_call x1, Pallas kernels, attend(): pl.pallas_call(attend_kernel, out_shape=[shape((FPD, PR, HC))] * 2 + [sha...  24.9 us
  transfers between devices with their start and end apart: 79, of which 32 were waited for; matrix products, arithmetic and copies ran while one was open for 6% of the time, Pallas kernels for 23%

profile of v2, /device:TPU:6, one launch (start us, length us, event | category | flops | bytes accessed | tf_op | source)
XLA Modules:
  0.0 614.0 jit_solution(10117685359087918889)
XLA Ops:
  19.2 18.3 %collective-permute-done.3 = f32[8,7424]{1,0:T(8,128)S(1)} collective-permute-done((f32[8,7424]{1,0:T(8,128)S(1)}, f32[8,7424]{1,0:T(8,128)S(1)}, u32[]{:S(2)}, u32[]{:S(2)}) %collective-permute-start.3) | collective-permute-done | bytes 237600 | tf_op jit(solution)/shard_map/ppermute | solution.py:27
  37.6 21.6 %collective-permute-done.1.refs_1_ = bf16[7,64,1024]{2,1,0:T(8,128)(2,1)} collective-permute-done((bf16[7,64,1024]{2,1,0:T(8,128)(2,1)}, bf16[7,64,1024]{2,1,0:T(8,128)(2,1)}, u32[]{:S(2)}, u32[]{:S(2)}) %collective-permute-start.1) | collective-permute-done | bytes 917536 | tf_op jit(solution)/shard_map/ppermute | solution.py:31
  62.7 11.0 %project_own.1 = (bf16[8,256,1024]{2,1,0:T(8,128)(2,1)S(1)}, bf16[8,256,256]{2,1,0:T(8,128)(2,1)S(1)}, bf16[8,256,256]{2,1,0:T(8,128)(2,1)S(1)}, bf16[8,256,256]{2,1,0:T(8,128)(2,1)S(1)}) custom-call(s32[1]{0:T(128)} %bitcast.row_ref.refs_0_, bf16[8,64,1024]{2,1,0:T(8,128)(2,1)S(1)} %copy-done.3, bf16[8,64,1024]{2,1,0:T(8,128)(2,1)S(1)} %collective-permute-done.7.refs_2_, ...), custom_call_target="tpu_custom_call" | custom-call | flops 3221225472 | bytes 12582912 | tf_op jit(solution)/shard_map/project_own/pallas_call | solution.py:280
  76.7 11.1 %collective-permute-done.10.refs_6_ = f32[8,2048]{1,0:T(8,128)S(1)} collective-permute-done((f32[8,2048]{1,0:T(8,128)S(1)}, f32[8,2048]{1,0:T(8,128)S(1)}, u32[]{:S(2)}, u32[]{:S(2)}) %collective-permute-start.10) | collective-permute-done | bytes 65568 | tf_op jit(solution)/shard_map/ppermute | solution.py:31
  93.2 8.1 %project_prev.1 = (bf16[7,256,256]{2,1,0:T(8,128)(2,1)S(1)}, bf16[7,256,256]{2,1,0:T(8,128)(2,1)S(1)}) custom-call(s32[1]{0:T(128)} %bitcast.row_ref.refs_0_, bf16[7,64,1024]{2,1,0:T(8,128)(2,1)} %collective-permute-done.1.refs_1_, bf16[7,64,1024]{2,1,0:T(8,128)(2,1)S(1)} %collective-permute-done.11.refs_2_, ...), custom_call_target="tpu_custom_call" | custom-call | flops 2818572288 | bytes 11534336 | tf_op jit(solution)/shard_map/project_prev/pallas_call | solution.py:280
  103.2 24.9 %attend.1 = (bf16[8,64,256]{2,1,0:T(8,128)(2,1)}, bf16[8,64,256]{2,1,0:T(8,128)(2,1)}, bf16[2,8,64,256]{3,2,1,0:T(8,128)(2,1)}, f32[8,8,256]{2,1,0:T(8,128)}) custom-call(s32[8]{0:T(128)} %refs_0_.3, bf16[8,256,256]{2,1,0:T(8,128)(2,1)} %copy-done.18, bf16[8,256,256]{2,1,0:T(8,128)(2,1)} %copy-done.19, bf16[8,256,256]{2,1,0:T(8,128)(2,1)} %copy-done.20, ...), custom_call_target="tpu_custom_call" | custom-call | flops 9663676416 | bytes 6291456 | tf_op jit(solution)/shard_map/attend/pallas_call | solution.py:367
  128.4 6.1 collective-permute-done.19.d2
  136.3 13.2 %collective-permute-done.14 = bf16[2,8,64,256]{3,2,1,0:T(8,128)(2,1)S(1)} collective-permute-done((bf16[2,8,64,256]{3,2,1,0:T(8,128)(2,1)}, bf16[2,8,64,256]{3,2,1,0:T(8,128)(2,1)S(1)}, u32[]{:S(2)}, u32[]{:S(2)}) %collective-permute-start.14) | collective-permute-done | bytes 524320 | tf_op jit(solution)/shard_map/ppermute | solution.py:27
  164.7 26.9 %feed.1 = (bf16[512,4096]{1,0:T(8,128)(2,1)}, bf16[512,4096]{1,0:T(8,128)(2,1)}, f32[512,1024]{1,0:T(8,128)}, f32[8,512]{1,0:T(8,128)}) custom-call(s32[1]{0:T(128)} %bitcast.row_ref.refs_0_, bf16[512,1024]{1,0:T(8,128)(2,1)} %bitcast.77, bf16[512,1024]{1,0:T(8,128)(2,1)} %bitcast.79, bf16[256,4096]{1,0:T(8,128)(2,1)} %u0.1, ...), custom_call_target="tpu_custom_call" | custom-call | flops 12884901888 | bytes 31457280 | tf_op jit(solution)/shard_map/feed/pallas_call | solution.py:681
  208.8 22.1 %down_weight_grad.1 = (bf16[2,1024,1024]{2,1,0:T(8,128)(2,1)}, bf16[2,1024,1024]{2,1,0:T(8,128)(2,1)}, bf16[8,64,1024]{2,1,0:T(8,128)(2,1)}, f32[8,1024]{1,0:T(8,128)}) custom-call(s32[1]{0:T(128)} %bitcast.row_ref.refs_0_, bf16[512,1024]{1,0:T(8,128)(2,1)} %bitcast.80, bf16[512,4096]{1,0:T(8,128)(2,1)} %get-tuple-element.203.act, bf16[1024,1024]{1,0:T(8,128)(2,1)} %d0.3, ...), custom_call_target="tpu_custom_call" | custom-call | flops 8589934592 | bytes 25165824 | tf_op jit(solution)/shard_map/down_weight_grad/pallas_call | solution.py:746
  235.7 12.2 %collective-permute-done.26 = f32[8,3840]{1,0:T(8,128)S(1)} collective-permute-done((f32[8,3840]{1,0:T(8,128)S(1)}, f32[8,3840]{1,0:T(8,128)S(1)}, u32[]{:S(2)}, u32[]{:S(2)}) %collective-permute-start.26) | collective-permute-done | bytes 122912 | tf_op jit(solution)/shard_map/ppermute | solution.py:27
  248.0 5.6 collective-permute-start.29
  253.6 10.8 %up_weight_grad.1 = (bf16[2,4,256,1024]{3,2,1,0:T(8,128)(2,1)}, bf16[2,4,256,1024]{3,2,1,0:T(8,128)(2,1)}) custom-call(s32[1]{0:T(128)} %bitcast.row_ref.refs_0_, bf16[512,1024]{1,0:T(8,128)(2,1)} %bitcast.78, bf16[512,4096]{1,0:T(8,128)(2,1)} %get-tuple-element.213.upg), custom_call_target="tpu_custom_call" | custom-call | flops 4294967296 | bytes 14680064 | tf_op jit(solution)/shard_map/up_weight_grad/pallas_call | solution.py:776
  265.3 4.6 collective-permute-start.33
  269.9 7.6 %add_convert_fusion = bf16[2,1024,1024]{2,1,0:T(8,128)(2,1)} fusion(bf16[2,1024,1024]{2,1,0:T(8,128)(2,1)} %collective-permute-done.30, bf16[2,1024,1024]{2,1,0:T(8,128)(2,1)} %get-tuple-element.206), kind=kLoop, calls=%fused_computation | loop fusion | flops 8388608 | bytes 12582912 | tf_op jit(solution)/shard_map/convert_element_type | solution.py:1290
  278.9 15.3 %attend_back_prev.1 = (f32[8,256,256]{2,1,0:T(8,128)}, bf16[2,7,256,256]{3,2,1,0:T(8,128)(2,1)}) custom-call(s32[8]{0:T(128)} %refs_0_.3, bf16[8,256,256]{2,1,0:T(8,128)(2,1)} %copy-done.18, bf16[7,256,256]{2,1,0:T(8,128)(2,1)} %copy-done.76, bf16[7,256,256]{2,1,0:T(8,128)(2,1)} %copy-done.77, bf16[8,64,256]{2,1,0:T(8,128)(2,1)} %copy-done.43, ...), custom_call_target="tpu_custom_call" | custom-call | flops 8053063680 | bytes 12582912 | tf_op jit(solution)/shard_map/attend_back_prev/pallas_call | solution.py:490
  295.3 8.6 %core_sum.1 = bf16[2,1280,1024]{2,1,0:T(8,128)(2,1)} custom-call(bf16[2,4,256,1024]{3,2,1,0:T(8,128)(2,1)} %get-tuple-element.232.ua, bf16[2,4,256,1024]{3,2,1,0:T(8,128)(2,1)} %collective-permute-done.35.ub, bf16[2,256,1024]{2,1,0:T(8,128)(2,1)} %copy-done.28, bf16[2,256,1024]{2,1,0:T(8,128)(2,1)} %copy-done.78), custom_call_target="tpu_custom_call" | custom-call | flops 1000 | bytes 1000 | tf_op jit(solution)/shard_map/core_sum/pallas_call | solution.py:833
  304.1 26.5 %attend_back_own.1 = (bf16[8,256,256]{2,1,0:T(8,128)(2,1)}, f32[8,256,256]{2,1,0:T(8,128)}, f32[8,256,256]{2,1,0:T(8,128)}) custom-call(s32[8]{0:T(128)} %refs_0_.3, bf16[8,256,256]{2,1,0:T(8,128)(2,1)} %copy-done.18, bf16[8,256,256]{2,1,0:T(8,128)(2,1)} %copy-done.19, bf16[8,256,256]{2,1,0:T(8,128)(2,1)} %copy-done.20, bf16[8,64,256]{2,1,0:T(8,128)(2,1)} %copy-done.43, ...), custom_call_target="tpu_custom_call" | custom-call | flops 1000 | bytes 1000 | tf_op jit(solution)/shard_map/attend_back_own/pallas_call | solution.py:490
  330.6 18.5 %collective-permute-done.37.rk.rv = bf16[2,7,256,256]{3,2,1,0:T(8,128)(2,1)S(1)} collective-permute-done((bf16[2,7,256,256]{3,2,1,0:T(8,128)(2,1)}, bf16[2,7,256,256]{3,2,1,0:T(8,128)(2,1)S(1)}, u32[]{:S(2)}, u32[]{:S(2)}) %collective-permute-start.37) | collective-permute-done | bytes 1835040 | tf_op jit(solution)/shard_map/ppermute | solution.py:31
  353.7 8.0 %project_back.1 = (bf16[8,256,768]{2,1,0:T(8,128)(2,1)S(1)}, bf16[8,64,1024]{2,1,0:T(8,128)(2,1)S(1)}, bf16[8,64,1024]{2,1,0:T(8,128)(2,1)S(1)}, bf16[2,8,64,1024]{3,2,1,0:T(8,128)(2,1)}, f32[8,512]{1,0:T(8,128)S(1)}) custom-call(s32[1]{0:T(128)} %bitcast.row_ref.refs_0_, bf16[8,256,256]{2,1,0:T(8,128)(2,1)S(1)} %copy-done.61, ...), custom_call_target="tpu_custom_call" | custom-call | flops 3221225472 | bytes 14680064 | tf_op jit(solution)/shard_map/project_back/pallas_call | solution.py:995
  369.5 7.4 %collective-permute-start.41 = (bf16[8,8,4096]{2,1,0:T(8,128)(2,1)S(1)}, bf16[8,8,4096]{2,1,0:T(8,128)(2,1)S(1)}, u32[]{:S(2)}, u32[]{:S(2)}) collective-permute-start(bf16[8,8,4096]{2,1,0:T(8,128)(2,1)S(1)} %constant_dynamic-update-slice_fusion.refs_2_), channel_id=1, source_target_pairs={{0,8},{1,9},{2,10},{3,11},{4,12},{5,13},{6,14},{7,15},{8,0},{9,1},... | collective-permute-start | bytes 1572872 | tf_op jit(solution)/shard_map/ppermute | solution.py:27
  381.7 4.7 project_weight.1
  388.4 16.3 %collective-permute-done.41.refs_4_ = bf16[8,8,4096]{2,1,0:T(8,128)(2,1)S(1)} collective-permute-done((bf16[8,8,4096]{2,1,0:T(8,128)(2,1)S(1)}, bf16[8,8,4096]{2,1,0:T(8,128)(2,1)S(1)}, u32[]{:S(2)}, u32[]{:S(2)}) %collective-permute-start.41) | collective-permute-done | bytes 524320 | tf_op jit(solution)/shard_map/ppermute | solution.py:27
  416.4 8.2 %collective-permute-done.43 = bf16[4,64,768]{2,1,0:T(8,128)(2,1)} collective-permute-done((bf16[4,64,768]{2,1,0:T(8,128)(2,1)}, bf16[4,64,768]{2,1,0:T(8,128)(2,1)}, u32[]{:S(2)}, u32[]{:S(2)}) %collective-permute-start.43) | collective-permute-done | bytes 393248 | tf_op jit(solution)/shard_map/ppermute | solution.py:27
  424.6 8.7 %collective-permute-done.44 = bf16[4,64,768]{2,1,0:T(8,128)(2,1)} collective-permute-done((bf16[4,64,768]{2,1,0:T(8,128)(2,1)}, bf16[4,64,768]{2,1,0:T(8,128)(2,1)}, u32[]{:S(2)}, u32[]{:S(2)}) %collective-permute-start.44) | collective-permute-done | bytes 393248 | tf_op jit(solution)/shard_map/ppermute | solution.py:27
  456.6 5.3 collective-permute-done.53
  468.2 28.7 %reduce-scatter.5.cloned.1.call-done = bf16[2,80,1024]{2,1,0:T(8,128)(2,1)} async-done(((bf16[2,1280,1024]{2,1,0:T(8,128)(2,1)}), bf16[2,80,1024]{2,1,0:T(8,128)(2,1)}) %reduce-scatter.5.cloned.1.call-update) | async-done | bytes 327696 | tf_op jit(solution)/shard_map/reduce_scatter | solution.py:1301
  518.4 7.5 %collective-permute-done.66 = bf16[4,16,3072]{2,1,0:T(8,128)(2,1)S(1)} collective-permute-done((bf16[4,16,3072]{2,1,0:T(8,128)(2,1)S(1)}, bf16[4,16,3072]{2,1,0:T(8,128)(2,1)S(1)}, u32[]{:S(2)}, u32[]{:S(2)}) %collective-permute-start.66) | collective-permute-done | bytes 393248 | tf_op jit(solution)/shard_map/ppermute | solution.py:27
  535.8 26.6 %collective-permute-done.68 = bf16[80,1024]{1,0:T(8,128)(2,1)S(1)} collective-permute-done((bf16[80,1024]{1,0:T(8,128)(2,1)S(1)}, bf16[80,1024]{1,0:T(8,128)(2,1)S(1)}, u32[]{:S(2)}, u32[]{:S(2)}) %collective-permute-start.68) | collective-permute-done | bytes 163872 | tf_op jit(solution)/shard_map/ppermute | solution.py:27
  573.2 13.7 %collective-permute-done.72.high = bf16[2,4,16,3072]{3,2,1,0:T(8,128)(2,1)} collective-permute-done((bf16[2,4,16,3072]{3,2,1,0:T(8,128)(2,1)S(1)}, bf16[2,4,16,3072]{3,2,1,0:T(8,128)(2,1)}, u32[]{:S(2)}, u32[]{:S(2)}) %collective-permute-start.72) | collective-permute-done | bytes 786464 | tf_op jit(solution)/shard_map/ppermute | solution.py:27
  590.7 6.2 %final_sums.1 = (f32[256,6144]{1,0:T(8,128)}, f32[1,1536]{1,0:T(1,128)S(1)}, f32[1,768]{1,0:T(1,128)S(1)}, f32[1,256]{1,0:T(1,128)}, f32[1,1024]{1,0:T(1,128)}, /*index=5*/f32[1,256]{1,0:T(1,128)}) custom-call(s32[1]{0:T(128)} %bitcast.row_ref.refs_0_, bf16[2,4,16,3584]{3,2,1,0:T(8,128)(2,1)S(1)} %pad_maximum_fusion.refs_0_, ...), custom_call_target="tpu_custom_call" | custom-call | flops 805306368 | bytes 10485760 | tf_op jit(solution)/shard_map/final_sums/pallas_call | solution.py:1144
  602.2 4.8 spread.1
  (402 shorter events, 179.4 us)
Async XLA Ops:
  7.2 401.1 %reduce-scatter.3.cloned.1.call-start = ((), (), s32[]{:S(2)}) async-start(), calls=%async_computation.2 | async-start | bytes 4456448 | tf_op jit(solution)/shard_map/reduce_scatter | solution.py:1295
  7.2 51.9 %collective-permute-start = (bf16[8,64,1024]{2,1,0:T(8,128)(2,1)}, bf16[8,64,1024]{2,1,0:T(8,128)(2,1)}, u32[]{:S(2)}, u32[]{:S(2)}) collective-permute-start(bf16[8,64,1024]{2,1,0:T(8,128)(2,1)} %x.3), channel_id=1, source_target_pairs={{0,2},{1,3},{2,0},{3,1},{4,6},{5,7},{6,4},{7,5},{8,10},{9,11},{10,... | collective-permute-start | bytes 3145736 | tf_op jit(solution)/shard_map/ppermute | solution.py:27
  10.4 48.8 %collective-permute-start.1 = (bf16[7,64,1024]{2,1,0:T(8,128)(2,1)}, bf16[7,64,1024]{2,1,0:T(8,128)(2,1)}, u32[]{:S(2)}, u32[]{:S(2)}) collective-permute-start(bf16[7,64,1024]{2,1,0:T(8,128)(2,1)} %slice.69), channel_id=1, source_target_pairs={{0,4},{1,5},{2,6},{3,7},{4,8},{5,9},{6,10},{7,11},{8,12},{9,13},{1... | collective-permute-start | bytes 2752520 | tf_op jit(solution)/shard_map/ppermute | solution.py:31
  12.6 25.0 %collective-permute-start.5 = (bf16[2,256,768]{2,1,0:T(8,128)(2,1)S(1)}, bf16[2,256,768]{2,1,0:T(8,128)(2,1)S(1)}, u32[]{:S(2)}, u32[]{:S(2)}) collective-permute-start(bf16[2,256,768]{2,1,0:T(8,128)(2,1)S(1)} %get-tuple-element.164), channel_id=1, source_target_pairs={{0,66},{1,67},{2,64},{3,65},{4,70},{5,71},{6,68},{7,69},{8,74},{9,... | collective-permute-start | bytes 2359304 | tf_op jit(solution)/shard_map/ppermute | solution.py:27
  37.5 22.9 %collective-permute-start.7 = (bf16[8,64,1024]{2,1,0:T(8,128)(2,1)S(1)}, bf16[8,64,1024]{2,1,0:T(8,128)(2,1)S(1)}, u32[]{:S(2)}, u32[]{:S(2)}) collective-permute-start(bf16[8,64,1024]{2,1,0:T(8,128)(2,1)S(1)} %copy-done.3), channel_id=1, source_target_pairs={{0,1},{1,0},{2,3},{3,2},{4,5},{5,4},{6,7},{7,6},{8,9},{9,8},{10,11... | collective-permute-start | bytes 3145736 | tf_op jit(solution)/shard_map/ppermute | solution.py:27
  59.2 28.6 %collective-permute-start.6 = (bf16[7,64,1024]{2,1,0:T(8,128)(2,1)}, bf16[7,64,1024]{2,1,0:T(8,128)(2,1)S(1)}, u32[]{:S(2)}, u32[]{:S(2)}) collective-permute-start(bf16[7,64,1024]{2,1,0:T(8,128)(2,1)} %collective-permute-done.1.refs_1_), channel_id=1, source_target_pairs={{0,2},{1,3},{2,0},{3,1},{4,6},{5,7},{6,4},{7,5},{8,10},{9,11},{10,... | collective-permute-start | bytes 2752520 | tf_op jit(solution)/shard_map/ppermute | solution.py:27
  60.4 27.3 %collective-permute-start.10 = (f32[8,2048]{1,0:T(8,128)S(1)}, f32[8,2048]{1,0:T(8,128)S(1)}, u32[]{:S(2)}, u32[]{:S(2)}) collective-permute-start(f32[8,2048]{1,0:T(8,128)S(1)} %slice.72), channel_id=1, source_target_pairs={{0,4},{1,5},{2,6},{3,7},{4,8},{5,9},{6,10},{7,11},{8,12},{9,13},{1... | collective-permute-start | bytes 196616 | tf_op jit(solution)/shard_map/ppermute | solution.py:31
  60.5 67.9 %collective-permute-start.18 = (bf16[256,4096]{1,0:T(8,128)(2,1)}, bf16[256,4096]{1,0:T(8,128)(2,1)}, u32[]{:S(2)}, u32[]{:S(2)}) collective-permute-start(bf16[256,4096]{1,0:T(8,128)(2,1)} %u0.1), channel_id=1, source_target_pairs={{0,66},{1,67},{2,64},{3,65},{4,70},{5,71},{6,68},{7,69},{8,74},{9,... | collective-permute-start | bytes 6291464 | tf_op jit(solution)/shard_map/ppermute | solution.py:27
  87.8 46.7 %collective-permute-start.19 = (bf16[1024,1024]{1,0:T(8,128)(2,1)}, bf16[1024,1024]{1,0:T(8,128)(2,1)}, u32[]{:S(2)}, u32[]{:S(2)}) collective-permute-start(bf16[1024,1024]{1,0:T(8,128)(2,1)} %d0.3), channel_id=1, source_target_pairs={{0,2},{1,3},{2,0},{3,1},{4,6},{5,7},{6,4},{7,5},{8,10},{9,11},{10,... | collective-permute-start | bytes 6291464 | tf_op jit(solution)/shard_map/ppermute | solution.py:27
  89.2 38.9 %collective-permute-start.17 = (bf16[256,1024]{1,0:T(8,128)(2,1)S(1)}, bf16[256,1024]{1,0:T(8,128)(2,1)S(1)}, u32[]{:S(2)}, u32[]{:S(2)}) collective-permute-start(bf16[256,1024]{1,0:T(8,128)(2,1)S(1)} %copy-done.14), channel_id=1, source_target_pairs={{0,66},{1,67},{2,64},{3,65},{4,70},{5,71},{6,68},{7,69},{8,74},{9,... | collective-permute-start | bytes 1572872 | tf_op jit(solution)/shard_map/ppermute | solution.py:27
  92.6 42.8 %collective-permute-start.16 = (bf16[256,1024]{1,0:T(8,128)(2,1)S(1)}, bf16[256,1024]{1,0:T(8,128)(2,1)S(1)}, u32[]{:S(2)}, u32[]{:S(2)}) collective-permute-start(bf16[256,1024]{1,0:T(8,128)(2,1)S(1)} %copy-done.14), channel_id=1, source_target_pairs={{0,1},{1,0},{2,3},{3,2},{4,5},{5,4},{6,7},{7,6},{8,9},{9,8},{10,11... | collective-permute-start | bytes 1572872 | tf_op jit(solution)/shard_map/ppermute | solution.py:27
  92.8 69.3 %collective-permute-start.21 = (bf16[256,4096]{1,0:T(8,128)(2,1)}, bf16[256,4096]{1,0:T(8,128)(2,1)}, u32[]{:S(2)}, u32[]{:S(2)}) collective-permute-start(bf16[256,4096]{1,0:T(8,128)(2,1)} %u0.1), channel_id=1, source_target_pairs={{0,1},{1,0},{2,3},{3,2},{4,5},{5,4},{6,7},{7,6},{8,9},{9,8},{10,11... | collective-permute-start | bytes 6291464 | tf_op jit(solution)/shard_map/ppermute | solution.py:27
  128.1 34.0 %collective-permute-start.23 = (bf16[1024,1024]{1,0:T(8,128)(2,1)}, bf16[1024,1024]{1,0:T(8,128)(2,1)S(1)}, u32[]{:S(2)}, u32[]{:S(2)}) collective-permute-start(bf16[1024,1024]{1,0:T(8,128)(2,1)} %d0.3), channel_id=1, source_target_pairs={{0,1},{1,0},{2,3},{3,2},{4,5},{5,4},{6,7},{7,6},{8,9},{9,8},{10,11... | collective-permute-start | bytes 6291464 | tf_op jit(solution)/shard_map/ppermute | solution.py:27
  134.5 27.6 %collective-permute-start.22 = (bf16[256,4096]{1,0:T(8,128)(2,1)}, bf16[256,4096]{1,0:T(8,128)(2,1)S(1)}, u32[]{:S(2)}, u32[]{:S(2)}) collective-permute-start(bf16[256,4096]{1,0:T(8,128)(2,1)} %collective-permute-done.18.u2), channel_id=1, source_target_pairs={{0,1},{1,0},{2,3},{3,2},{4,5},{5,4},{6,7},{7,6},{8,9},{9,8},{10,11... | collective-permute-start | bytes 6291464 | tf_op jit(solution)/shard_map/ppermute | solution.py:27
  134.9 27.2 %collective-permute-start.24 = (bf16[1024,1024]{1,0:T(8,128)(2,1)}, bf16[1024,1024]{1,0:T(8,128)(2,1)S(1)}, u32[]{:S(2)}, u32[]{:S(2)}) collective-permute-start(bf16[1024,1024]{1,0:T(8,128)(2,1)} %collective-permute-done.19.d2), channel_id=1, source_target_pairs={{0,1},{1,0},{2,3},{3,2},{4,5},{5,4},{6,7},{7,6},{8,9},{9,8},{10,11... | collective-permute-start | bytes 6291464 | tf_op jit(solution)/shard_map/ppermute | solution.py:27
  230.9 34.2 %collective-permute-start.30 = (bf16[2,1024,1024]{2,1,0:T(8,128)(2,1)}, bf16[2,1024,1024]{2,1,0:T(8,128)(2,1)}, u32[]{:S(2)}, u32[]{:S(2)}) collective-permute-start(bf16[2,1024,1024]{2,1,0:T(8,128)(2,1)} %get-tuple-element.217), channel_id=1, source_target_pairs={{0,1},{1,0},{2,3},{3,2},{4,5},{5,4},{6,7},{7,6},{8,9},{9,8},{10,11... | collective-permute-start | bytes 12582920 | tf_op jit(solution)/shard_map/ppermute | solution.py:27
  278.4 218.5 %reduce-scatter.5.cloned.1.call-start = ((), (), s32[]{:S(2)}) async-start(), calls=%async_computation.3 | async-start | bytes 5570560 | tf_op jit(solution)/shard_map/reduce_scatter | solution.py:1301
  303.9 294.2 %all-gather.2.cloned.1.call-start = ((), (), s32[]{:S(2)}) async-start(), calls=%async_computation.4 | async-start | bytes 2228224 | tf_op jit(solution)/shard_map/all_gather | solution.py:1344
  304.1 45.1 %collective-permute-start.37 = (bf16[2,7,256,256]{3,2,1,0:T(8,128)(2,1)}, bf16[2,7,256,256]{3,2,1,0:T(8,128)(2,1)S(1)}, u32[]{:S(2)}, u32[]{:S(2)}) collective-permute-start(bf16[2,7,256,256]{3,2,1,0:T(8,128)(2,1)} %get-tuple-element.240), channel_id=1, source_target_pairs={{0,124},{1,125},{2,126},{3,127},{4,0},{5,1},{6,2},{7,3},{8,4},{9,5... | collective-permute-start | bytes 5505032 | tf_op jit(solution)/shard_map/ppermute | solution.py:31
  369.5 35.2 %collective-permute-start.41 = (bf16[8,8,4096]{2,1,0:T(8,128)(2,1)S(1)}, bf16[8,8,4096]{2,1,0:T(8,128)(2,1)S(1)}, u32[]{:S(2)}, u32[]{:S(2)}) collective-permute-start(bf16[8,8,4096]{2,1,0:T(8,128)(2,1)S(1)} %constant_dynamic-update-slice_fusion.refs_2_), channel_id=1, source_target_pairs={{0,8},{1,9},{2,10},{3,11},{4,12},{5,13},{6,14},{7,15},{8,0},{9,1},... | collective-permute-start | bytes 1572872 | tf_op jit(solution)/shard_map/ppermute | solution.py:27
  376.9 30.6 %collective-permute-start.42 = (bf16[8,8,4096]{2,1,0:T(8,128)(2,1)S(1)}, bf16[8,8,4096]{2,1,0:T(8,128)(2,1)S(1)}, u32[]{:S(2)}, u32[]{:S(2)}) collective-permute-start(bf16[8,8,4096]{2,1,0:T(8,128)(2,1)S(1)} %constant_dynamic-update-slice_fusion.refs_2_), channel_id=1, source_target_pairs={{0,12},{1,13},{2,14},{3,15},{4,8},{5,9},{6,10},{7,11},{8,4},{9,5},... | collective-permute-start | bytes 1572872 | tf_op jit(solution)/shard_map/ppermute | solution.py:27
  379.7 58.3 %collective-permute-start.39 = (bf16[8,64,1024]{2,1,0:T(8,128)(2,1)}, bf16[8,64,1024]{2,1,0:T(8,128)(2,1)}, u32[]{:S(2)}, u32[]{:S(2)}) collective-permute-start(bf16[8,64,1024]{2,1,0:T(8,128)(2,1)} %fusion), channel_id=1, source_target_pairs={{0,2},{1,3},{2,0},{3,1},{4,6},{5,7},{6,4},{7,5},{8,10},{9,11},{10,... | collective-permute-start | bytes 3145736 | tf_op jit(solution)/shard_map/ppermute | solution.py:27
  410.5 22.8 %collective-permute-start.44 = (bf16[4,64,768]{2,1,0:T(8,128)(2,1)}, bf16[4,64,768]{2,1,0:T(8,128)(2,1)}, u32[]{:S(2)}, u32[]{:S(2)}) collective-permute-start(bf16[4,64,768]{2,1,0:T(8,128)(2,1)} %get-tuple-element.307), channel_id=1, source_target_pairs={{0,8},{1,9},{2,10},{3,11},{4,12},{5,13},{6,14},{7,15},{8,0},{9,1},... | collective-permute-start | bytes 1179656 | tf_op jit(solution)/shard_map/ppermute | solution.py:27
  412.3 24.1 %collective-permute-start.45 = (bf16[4,64,768]{2,1,0:T(8,128)(2,1)}, bf16[4,64,768]{2,1,0:T(8,128)(2,1)}, u32[]{:S(2)}, u32[]{:S(2)}) collective-permute-start(bf16[4,64,768]{2,1,0:T(8,128)(2,1)} %get-tuple-element.306), channel_id=1, source_target_pairs={{0,12},{1,13},{2,14},{3,15},{4,8},{5,9},{6,10},{7,11},{8,4},{9,5},... | collective-permute-start | bytes 1179656 | tf_op jit(solution)/shard_map/ppermute | solution.py:27
  528.6 38.3 %collective-permute-start.71 = (bf16[2,4,16,3584]{3,2,1,0:T(8,128)(2,1)S(1)}, bf16[2,4,16,3584]{3,2,1,0:T(8,128)(2,1)S(1)}, u32[]{:S(2)}, u32[]{:S(2)}) collective-permute-start(bf16[2,4,16,3584]{3,2,1,0:T(8,128)(2,1)S(1)} %pad_maximum_fusion.refs_0_), channel_id=1, source_target_pairs={{0,4},{1,5},{2,6},{3,7},{4,0},{5,1},{6,2},{7,3},{8,12},{9,13},{10,... | collective-permute-start | bytes 2752520 | tf_op jit(solution)/shard_map/ppermute | solution.py:27
  529.2 33.2 %collective-permute-start.68 = (bf16[80,1024]{1,0:T(8,128)(2,1)S(1)}, bf16[80,1024]{1,0:T(8,128)(2,1)S(1)}, u32[]{:S(2)}, u32[]{:S(2)}) collective-permute-start(bf16[80,1024]{1,0:T(8,128)(2,1)S(1)} %add_convert_fusion.2), channel_id=1, source_target_pairs={{0,4},{1,5},{2,6},{3,7},{4,0},{5,1},{6,2},{7,3},{8,12},{9,13},{10,... | collective-permute-start | bytes 491528 | tf_op jit(solution)/shard_map/ppermute | solution.py:27
  530.9 34.7 %collective-permute-start.69 = (bf16[80,1024]{1,0:T(8,128)(2,1)S(1)}, bf16[80,1024]{1,0:T(8,128)(2,1)S(1)}, u32[]{:S(2)}, u32[]{:S(2)}) collective-permute-start(bf16[80,1024]{1,0:T(8,128)(2,1)S(1)} %add_convert_fusion.2), channel_id=1, source_target_pairs={{0,8},{1,9},{2,10},{3,11},{4,12},{5,13},{6,14},{7,15},{8,0},{9,1},... | collective-permute-start | bytes 491528 | tf_op jit(solution)/shard_map/ppermute | solution.py:27
  532.2 33.4 %collective-permute-start.70 = (bf16[80,1024]{1,0:T(8,128)(2,1)S(1)}, bf16[80,1024]{1,0:T(8,128)(2,1)S(1)}, u32[]{:S(2)}, u32[]{:S(2)}) collective-permute-start(bf16[80,1024]{1,0:T(8,128)(2,1)S(1)} %add_convert_fusion.2), channel_id=1, source_target_pairs={{0,12},{1,13},{2,14},{3,15},{4,8},{5,9},{6,10},{7,11},{8,4},{9,5},... | collective-permute-start | bytes 491528 | tf_op jit(solution)/shard_map/ppermute | solution.py:27
  535.6 31.5 %collective-permute-start.54 = (f32[8,256]{1,0:T(8,128)}, f32[8,256]{1,0:T(8,128)S(1)}, u32[]{:S(2)}, u32[]{:S(2)}) collective-permute-start(f32[8,256]{1,0:T(8,128)} %fusion.2), channel_id=1, source_target_pairs={{0,3},{1,2},{2,1},{3,0},{4,7},{5,6},{6,5},{7,4},{8,11},{9,10},{10,... | collective-permute-start | bytes 24584 | tf_op jit(solution)/shard_map/ppermute | solution.py:27
  567.0 35.2 %collective-permute-start.73 = (bf16[4,80,1024]{2,1,0:T(8,128)(2,1)S(1)}, bf16[4,80,1024]{2,1,0:T(8,128)(2,1)}, u32[]{:S(2)}, u32[]{:S(2)}) collective-permute-start(bf16[4,80,1024]{2,1,0:T(8,128)(2,1)S(1)} %pad_maximum_fusion.2.refs_0_), channel_id=1, source_target_pairs={{0,16},{1,17},{2,18},{3,19},{4,20},{5,21},{6,22},{7,23},{8,24},{9,... | collective-permute-start | bytes 1966088 | tf_op jit(solution)/shard_map/ppermute | solution.py:27
  567.1 35.1 %collective-permute-start.74 = (bf16[4,80,1024]{2,1,0:T(8,128)(2,1)S(1)}, bf16[4,80,1024]{2,1,0:T(8,128)(2,1)}, u32[]{:S(2)}, u32[]{:S(2)}) collective-permute-start(bf16[4,80,1024]{2,1,0:T(8,128)(2,1)S(1)} %pad_maximum_fusion.2.refs_0_), channel_id=1, source_target_pairs={{0,32},{1,33},{2,34},{3,35},{4,36},{5,37},{6,38},{7,39},{8,40},{9,... | collective-permute-start | bytes 1966088 | tf_op jit(solution)/shard_map/ppermute | solution.py:27
  569.9 32.3 %collective-permute-start.75 = (bf16[4,80,1024]{2,1,0:T(8,128)(2,1)S(1)}, bf16[4,80,1024]{2,1,0:T(8,128)(2,1)}, u32[]{:S(2)}, u32[]{:S(2)}) collective-permute-start(bf16[4,80,1024]{2,1,0:T(8,128)(2,1)S(1)} %pad_maximum_fusion.2.refs_0_), channel_id=1, source_target_pairs={{0,48},{1,49},{2,50},{3,51},{4,52},{5,53},{6,54},{7,55},{8,56},{9,... | collective-permute-start | bytes 1966088 | tf_op jit(solution)/shard_map/ppermute | solution.py:27
  (145 other events, 2234.1 us)
Sparse Core Ops, SparseCore 0:
  277.8 128.3 reduce-scatter.2
  410.4 86.4 reduce-scatter.4
  500.5 49.5 all-gather.1

commit v3 on v1

--- a/solution.py
+++ b/solution.py
@@ -904,30 +904,50 @@
     )(row, *pieces, late, far)
 
 
-def place_kernel(index_ref, a0, a1, a2, a3, out):
-    for m, a in enumerate((a0, a1, a2, a3)):
+def stack_kernel(a0, a1, a2, a3, weights, sums):
+    for k, a in enumerate((a0, a1, a2, a3)):
+        weights[k] = a[:, : 3 * D]
+        sums[k] = a[:, 3 * D :]
+
+
+def stack(pieces):
+    rows, width = pieces[0].shape
+    return pl.pallas_call(
+        stack_kernel,
+        out_shape=[shape((4, rows, 3 * D)), shape((4, rows, LATE))],
+        grid=(1,),
+        in_specs=[whole((rows, width))] * 4,
+        out_specs=[whole((4, rows, 3 * D)), whole((4, rows, LATE))],
+        compiler_params=params(16),
+        cost_estimate=cost(0, 2 * MB),
+        name="stack",
+    )(*pieces)
+
+
+def place_kernel(index_ref, low, high, out):
+    for m, a in enumerate((low.at[0], low.at[1], high.at[1], high.at[0])):
 
         @pl.when(pl.program_id(0) == m)
         def _():
             for k in range(4):
-                out[0, index_ref[1] ^ k] = a[k, :, : 3 * D].astype(F32)
-
-
-def place(index, pieces):
-    rows = pieces[0].shape[1]
+                out[0, index_ref[1] ^ k] = a[k].astype(F32)
+
+
+def place(index, low, high):
+    rows = low.shape[2]
     return pl.pallas_call(
         place_kernel,
         out_shape=shape((4, 4, rows, 3 * D), F32),
         grid_spec=pltpu.PrefetchScalarGridSpec(
             num_scalar_prefetch=1,
             grid=(4,),
-            in_specs=[whole(a.shape) for a in pieces],
+            in_specs=[whole(low.shape)] * 2,
             out_specs=pl.BlockSpec((1, 4, rows, 3 * D), lambda i, index: (index[0] ^ i, 0, 0, 0)),
         ),
         compiler_params=params(24),
         cost_estimate=cost(0, 24 * rows * D),
         name="place",
-    )(index, *pieces).reshape(HC, 3 * D)
+    )(index, low, high).reshape(HC, 3 * D)
 
 
 def project_back_kernel(row_ref, dq, dk, dv, rk, rv, w0, w1, w2, w3, cp, sp, fr, dp, h0, h2, hs, bsum):
@@ -1066,14 +1086,15 @@
 
 def final_kernel(row_ref, *refs):
     row = row_ref[0]
-    late, early = refs[:4], refs[4:8]
-    ada, ab, qb, ob, ub, db, asum = refs[8:]
+    low, high, *early = refs[:6]
+    ada, ab, qb, ob, ub, db, asum = refs[6:]
+    late = [low.at[0], low.at[1], high.at[0], high.at[1]]
+    early = [early[0], early[3], early[1], early[2]]
 
     def rows(ref, cols):
         value = ref[:, :, cols].astype(F32)
         return value.reshape(64, value.shape[-1])
 
-    late = [ref.at[:, :, 3 * D :] for ref in late]
     left = [rows(s, slice(EARLY, EARLY + HC)).astype(BF16) for s in early]
     for segment in range(6):
         source, start = ((late, 0), (late, 1), (early, 0), (early, 1), (early, 2), (late, 2))[segment]
@@ -1120,7 +1141,7 @@
         grid_spec=pltpu.PrefetchScalarGridSpec(
             num_scalar_prefetch=1,
             grid=(1,),
-            in_specs=[whole((4, 16, 3 * D + LATE))] * 4
+            in_specs=[whole((2, 4, 16, LATE))] * 2
             + [whole((8, 8, EARLY + HC))] * 4,
             out_specs=[whole((HC, 6 * D))] + [whole((1, n)) for n in sizes],
             scratch_shapes=[pltpu.VMEM((8, 6 * D), F32)],
@@ -1242,43 +1263,47 @@
 
     early = early_sums(sums, usum, dsum)
     early = early + swap(early, CORE)
+    upg, early, _ = lax.optimization_barrier((upg, early, bg))
+    early_far = swap(early, DIRECT)
+    uk, us = up_weight_grad(row_arg, h2, upg)
+    us = swap(us, CORE)
+    dg_later, early_far, far_back, uk, *back = lax.optimization_barrier(
+        (dg, early_far, *late, uk, *back)
+    )
+    back += [far_back[0], swap(far_back[1], CORE)]
+    early = jnp.concatenate([(early + early_far).astype(BF16), silu_own], axis=1)
+    early_far = swap(early, FAR)
     dk_part, ds_part, layer_output, gate = down_weight_grad(
-        row_arg, after(dg, bg), act, downs, table, middle, cotangent
+        row_arg, dg_later, act, downs, table, middle, cotangent
     )
-    upg, early, gate, far_back, *back = lax.optimization_barrier((upg, early, gate, *late, *back))
-    back += [far_back[0], swap(far_back[1], CORE)]
-    early = early + swap(early, DIRECT)
-    uk, us = up_weight_grad(row_arg, h2, upg)
-    ok, os = out_weight_grad(turned, bg)
-
-    early = jnp.concatenate([early.astype(BF16), silu_own], axis=1)
-    early, uk = lax.optimization_barrier((early, uk))
-    early = jnp.stack([early, swap(early, FAR)])
-    early, uk, ok, *back = lax.optimization_barrier((early, uk, ok, *back))
+    ds_part = swap(ds_part, CORE)
+    dk_part, early, early_far, bg_later, us, *back = lax.optimization_barrier(
+        (dk_part, early, early_far, bg, us, *back)
+    )
+    early = jnp.stack([early, early_far])
     early_parts = [early] + [swap(early, m) for m in (16, 32, 48)]
+    ok, os = out_weight_grad(turned, bg_later)
+    packed = core_sum((uk, us), (dk_part, ds_part), (ok, swap(os, CORE)))
+    packed, early_parts, back = lax.optimization_barrier((packed, early_parts, back))
+    scattered = lax.psum_scatter(packed, ("y", "z"), scatter_dimension=1, tiled=True)
+
     dq_before, both = attend_back(False, frame_position, q, kp, vp, back, mixed, lse)
     returned = shift(both, -1)
-    uk, dq_before = lax.optimization_barrier((uk, dq_before))
-    packed = core_sum(
-        (uk, swap(us, CORE)), (dk_part, swap(ds_part, CORE)), (ok, swap(os, CORE))
-    )
-    dq_before, packed = lax.optimization_barrier((dq_before, packed))
-    scattered = lax.psum_scatter(packed, ("y", "z"), scatter_dimension=1, tiled=True)
     dq, dk, dv = attend_back(
         True, frame_position, q, k, v, back, mixed, lse, tables, dq_before
     )
-    dq, *early_parts = lax.optimization_barrier((dq, *early_parts))
+    early_parts = lax.optimization_barrier((early_parts, dq))[0]
     early = jnp.concatenate(early_parts)
-    early_high = early
+    early_all = [early] + [swap(early, m) for m in (4, 8, 12)]
     early = early[0].astype(F32)
 
     dproj, h0, h2_part, send, bsum = project_back(row_arg, dq, dk, dv, returned, qkv_pieces, tables)
     near = swap(send, CORE)
     qkv_parts = project_weight(row_arg, hidden1, dproj)
     far = swap((h2_part.astype(F32) + near[1].astype(F32)).astype(BF16), DIRECT)
+    qkv_parts, early_all = lax.optimization_barrier((qkv_parts, early_all))
     qkv_parts = exchange_rows(qkv_parts, 4, index, 0)
-    far, qkv_parts, early_high = lax.optimization_barrier((far, qkv_parts, early_high))
-    early_all = [early_high] + [swap(early_high, m) for m in (4, 8, 12)]
+    far, qkv_parts = lax.optimization_barrier((far, qkv_parts))
     quarters = quarter_rows(qkv_parts, 16, index, 1)
     input_grad, late = input_back(x0, h0, near, far, table, mg, bsum, gate)
     late, *quarters = lax.optimization_barrier((late, *quarters))
@@ -1298,17 +1323,23 @@
     turned = turn_heads(qkv_parts[0], qkv_parts[1], qkv_parts[2:])
     last = arrange(row_arg, turned, late_low, late_far)
 
-    scattered, last, *early_all = lax.optimization_barrier((scattered, last, *early_all))
-    last = jnp.stack([last] + [swap(last, m) for m in (16, 32, 48)])
+    scattered, last = lax.optimization_barrier((scattered, last))
+    last = [last] + [swap(last, m) for m in (16, 32, 48)]
     share = scattered[0].astype(F32) + swap(scattered[1], DIRECT).astype(F32)
-    share = (share + swap(share.astype(BF16), FAR).astype(F32)).astype(BF16)
     share, last = lax.optimization_barrier((share, last))
-    last_all = [last] + [swap(last, m) for m in (4, 8, 12)]
+    share_far = swap(share.astype(BF16), FAR)
+    weights, sums_late = stack(last)
+    weights_far, sums_far = swap(weights, 4), swap(sums_late, 12)
+    share, share_far = lax.optimization_barrier((share, share_far))
+    share = (share + share_far.astype(F32)).astype(BF16)
     totals = lax.all_gather(share, ("y", "z"), axis=0, tiled=True)
+    weights = jnp.stack([weights, weights_far])
+    sums_late = jnp.stack([sums_late, sums_far])
+    weights_far, sums_far = swap(weights, 12), swap(sums_late, 4)
     up_total, out_total, down_total = unpack(totals)
-    qkv_total = place(index_arg, last_all)
-
-    ada_total, *bias_sums = final_sums(row_arg, last_all, early_all)
+    qkv_total = place(index_arg, weights, weights_far)
+
+    ada_total, *bias_sums = final_sums(row_arg, (sums_late, sums_far), early_all)
     ada_sum, qkv_sum, out_sum, up_sum, down_sum = [b[0] for b in bias_sums]
     mod_own = jnp.concatenate(
         [late[:, : 2 * D], early[:, : 3 * D], late[:, 2 * D : 3 * D]], axis=1

time: 573 us -> 565 us (0.986)
  waiting for transfers between devices: 220 us -> 206 us
  Pallas kernels: 200 us -> 211 us
  starting transfers between devices: 70.2 us -> 61.7 us
    ppermute x64 -> x65, waiting for transfers between devices: 170 us -> 140 us  [swap(): return lax.ppermute(value, AXES, [(i, i ^ mask) for i in range(128)])]
    ppermute x64 -> x65, starting transfers between devices: 68.5 us -> 57.9 us  [swap(): return lax.ppermute(value, AXES, [(i, i ^ mask) for i in range(128)])]
    all_gather x1, waiting for transfers between devices: 0.01 us -> 9.22 us  [per_device(): totals = lax.all_gather(share, ('y', 'z'), axis=0, tiled=True)]
    pallas_call x2, Pallas kernels: 41.3 us -> 48 us  [attend_back(): pl.pallas_call(lambda *refs: attend_back_kernel(own, *refs), out_shape=[s...]
    ppermute x3, waiting for transfers between devices: 50.2 us -> 56.3 us  [shift(): lax.ppermute(value, AXES, [(i, (i + 4 * steps) % 128) for i in range(128)])]
    unnamed x196 -> x193, local copies, waits for them, and re-layouts: 46 us -> 43.1 us
  transfers between devices with their start and end apart: 69 -> 70, of which waited for: 34 -> 33; matrix products, arithmetic and copies ran while one was open for 2% -> 3% of each run, Pallas kernels for 27% -> 32%
where the time goes in v3:
time: 565 us; the launch traced here: 554 us
  Pallas kernels  211 us (37%)
  waiting for transfers between devices  206 us (36%)
  starting transfers between devices  61.7 us (11%)
  local copies, waits for them, and re-layouts  49.2 us (9%)
  between operations  15.4 us (3%)
  other arithmetic  9.24 us (2%)
    ppermute x65, waiting for transfers between devices, swap(): return lax.ppermute(value, AXES, [(i, i ^ mask) for i in range(128)])  140 us
    ppermute x65, starting transfers between devices, swap(): return lax.ppermute(value, AXES, [(i, i ^ mask) for i in range(128)])  57.9 us
    ppermute x3, waiting for transfers between devices, shift(): lax.ppermute(value, AXES, [(i, (i + 4 * steps) % 128) for i in range(128)])  56.3 us
    pallas_call x2, Pallas kernels, attend_back(): pl.pallas_call(lambda *refs: attend_back_kernel(own, *refs), out_shape=[s...  48 us
    unnamed x193, local copies, waits for them, and re-layouts  43.1 us
    pallas_call x1, Pallas kernels, attend(): pl.pallas_call(attend_kernel, out_shape=[shape((FPD, PR, HC))] * 2 + [sha...  29.6 us
    pallas_call x1, Pallas kernels, feed(): pl.pallas_call(feed_kernel, out_shape=[shape((TOKENS, FF)), shape((TOKENS...  26.8 us
    pallas_call x1, Pallas kernels, down_weight_grad(): pl.pallas_call(down_weight_kernel, out_shape=[shape((2, D, D))] * 2 + [sh...  22 us
  transfers between devices with their start and end apart: 70, of which 33 were waited for; matrix products, arithmetic and copies ran while one was open for 3% of the time, Pallas kernels for 32%

profile of v3, /device:TPU:6, one launch (start us, length us, event | category | flops | bytes accessed | tf_op | source)
XLA Modules:
  0.0 553.6 jit_solution(6808778082567608783)
XLA Ops:
  19.2 18.3 %collective-permute-done.3 = f32[8,7424]{1,0:T(8,128)S(1)} collective-permute-done((f32[8,7424]{1,0:T(8,128)S(1)}, f32[8,7424]{1,0:T(8,128)S(1)}, u32[]{:S(2)}, u32[]{:S(2)}) %collective-permute-start.3) | collective-permute-done | bytes 237600 | tf_op jit(solution)/shard_map/ppermute | solution.py:27
  37.6 21.6 %collective-permute-done.1.refs_1_ = bf16[7,64,1024]{2,1,0:T(8,128)(2,1)} collective-permute-done((bf16[7,64,1024]{2,1,0:T(8,128)(2,1)}, bf16[7,64,1024]{2,1,0:T(8,128)(2,1)}, u32[]{:S(2)}, u32[]{:S(2)}) %collective-permute-start.1) | collective-permute-done | bytes 917536 | tf_op jit(solution)/shard_map/ppermute | solution.py:31
  62.7 11.0 %project_own.1 = (bf16[8,256,1024]{2,1,0:T(8,128)(2,1)S(1)}, bf16[8,256,256]{2,1,0:T(8,128)(2,1)S(1)}, bf16[8,256,256]{2,1,0:T(8,128)(2,1)S(1)}, bf16[8,256,256]{2,1,0:T(8,128)(2,1)S(1)}) custom-call(s32[1]{0:T(128)} %bitcast.row_ref.refs_0_, bf16[8,64,1024]{2,1,0:T(8,128)(2,1)S(1)} %copy-done.3, bf16[8,64,1024]{2,1,0:T(8,128)(2,1)S(1)} %collective-permute-done.7.refs_2_, ...), custom_call_target="tpu_custom_call" | custom-call | flops 3221225472 | bytes 12582912 | tf_op jit(solution)/shard_map/project_own/pallas_call | solution.py:280
  76.7 11.1 %collective-permute-done.10.refs_6_ = f32[8,2048]{1,0:T(8,128)S(1)} collective-permute-done((f32[8,2048]{1,0:T(8,128)S(1)}, f32[8,2048]{1,0:T(8,128)S(1)}, u32[]{:S(2)}, u32[]{:S(2)}) %collective-permute-start.10) | collective-permute-done | bytes 65568 | tf_op jit(solution)/shard_map/ppermute | solution.py:31
  93.2 8.1 %project_prev.1 = (bf16[7,256,256]{2,1,0:T(8,128)(2,1)S(1)}, bf16[7,256,256]{2,1,0:T(8,128)(2,1)S(1)}) custom-call(s32[1]{0:T(128)} %bitcast.row_ref.refs_0_, bf16[7,64,1024]{2,1,0:T(8,128)(2,1)} %collective-permute-done.1.refs_1_, bf16[7,64,1024]{2,1,0:T(8,128)(2,1)S(1)} %collective-permute-done.11.refs_2_, ...), custom_call_target="tpu_custom_call" | custom-call | flops 2818572288 | bytes 11534336 | tf_op jit(solution)/shard_map/project_prev/pallas_call | solution.py:280
  103.2 29.6 %attend.1 = (bf16[8,64,256]{2,1,0:T(8,128)(2,1)}, bf16[8,64,256]{2,1,0:T(8,128)(2,1)}, bf16[2,8,64,256]{3,2,1,0:T(8,128)(2,1)}, f32[8,8,256]{2,1,0:T(8,128)}) custom-call(s32[8]{0:T(128)} %refs_0_.3, bf16[8,256,256]{2,1,0:T(8,128)(2,1)} %copy-done.20, bf16[8,256,256]{2,1,0:T(8,128)(2,1)} %copy-done.21, bf16[8,256,256]{2,1,0:T(8,128)(2,1)} %copy-done.22, ...), custom_call_target="tpu_custom_call" | custom-call | flops 9663676416 | bytes 6291456 | tf_op jit(solution)/shard_map/attend/pallas_call | solution.py:367
  136.2 13.2 %collective-permute-done.14 = bf16[2,8,64,256]{3,2,1,0:T(8,128)(2,1)S(1)} collective-permute-done((bf16[2,8,64,256]{3,2,1,0:T(8,128)(2,1)}, bf16[2,8,64,256]{3,2,1,0:T(8,128)(2,1)S(1)}, u32[]{:S(2)}, u32[]{:S(2)}) %collective-permute-start.14) | collective-permute-done | bytes 524320 | tf_op jit(solution)/shard_map/ppermute | solution.py:27
  164.5 26.8 %feed.1 = (bf16[512,4096]{1,0:T(8,128)(2,1)}, bf16[512,4096]{1,0:T(8,128)(2,1)}, f32[512,1024]{1,0:T(8,128)}, f32[8,512]{1,0:T(8,128)}) custom-call(s32[1]{0:T(128)} %bitcast.row_ref.refs_0_, bf16[512,1024]{1,0:T(8,128)(2,1)} %bitcast.67, bf16[512,1024]{1,0:T(8,128)(2,1)} %bitcast.65, bf16[256,4096]{1,0:T(8,128)(2,1)} %u0.1, ...), custom_call_target="tpu_custom_call" | custom-call | flops 12884901888 | bytes 31457280 | tf_op jit(solution)/shard_map/feed/pallas_call | solution.py:681
  208.6 10.9 %up_weight_grad.1 = (bf16[2,4,256,1024]{3,2,1,0:T(8,128)(2,1)}, bf16[2,4,256,1024]{3,2,1,0:T(8,128)(2,1)}) custom-call(s32[1]{0:T(128)} %bitcast.row_ref.refs_0_, bf16[512,1024]{1,0:T(8,128)(2,1)} %bitcast.68, bf16[512,4096]{1,0:T(8,128)(2,1)} %get-tuple-element.198.upg), custom_call_target="tpu_custom_call" | custom-call | flops 4294967296 | bytes 14680064 | tf_op jit(solution)/shard_map/up_weight_grad/pallas_call | solution.py:776
  221.0 4.4 collective-permute-done.26
  225.5 22.0 %down_weight_grad.1 = (bf16[2,1024,1024]{2,1,0:T(8,128)(2,1)}, bf16[2,1024,1024]{2,1,0:T(8,128)(2,1)}, bf16[8,64,1024]{2,1,0:T(8,128)(2,1)}, f32[8,1024]{1,0:T(8,128)}) custom-call(s32[1]{0:T(128)} %bitcast.row_ref.refs_0_, bf16[512,1024]{1,0:T(8,128)(2,1)} %bitcast.66, bf16[512,4096]{1,0:T(8,128)(2,1)} %get-tuple-element.203.act, bf16[1024,1024]{1,0:T(8,128)(2,1)} %d0.3, ...), custom_call_target="tpu_custom_call" | custom-call | flops 8589934592 | bytes 25165824 | tf_op jit(solution)/shard_map/down_weight_grad/pallas_call | solution.py:746
  249.1 5.7 %collective-permute-start.29 = (bf16[8,4096]{1,0:T(8,128)(2,1)S(1)}, bf16[8,4096]{1,0:T(8,128)(2,1)S(1)}, u32[]{:S(2)}, u32[]{:S(2)}) collective-permute-start(bf16[8,4096]{1,0:T(8,128)(2,1)S(1)} %pad_maximum_fusion.3), channel_id=1, source_target_pairs={{0,64},{1,65},{2,66},{3,67},{4,68},{5,69},{6,70},{7,71},{8,72},{9,... | collective-permute-start | bytes 196616 | tf_op jit(solution)/shard_map/ppermute | solution.py:27
  259.6 4.0 collective-permute-start.34
  266.6 12.0 %core_sum.1 = bf16[2,2304,1024]{2,1,0:T(8,128)(2,1)} custom-call(bf16[2,4,256,1024]{3,2,1,0:T(8,128)(2,1)} %get-tuple-element.205.ua, bf16[2,4,256,1024]{3,2,1,0:T(8,128)(2,1)} %collective-permute-done.30.ub, bf16[2,1024,1024]{2,1,0:T(8,128)(2,1)} %get-tuple-element.214.da, bf16[2,1024,1024]{2,1,0:T(8,128)(2,1)} %copy-done.78, ...), custom_call_target="tpu_custom_call" | custom-call | flops 1000 | bytes 1000 | tf_op jit(solution)/shard_map/core_sum/pallas_call | solution.py:836
  279.3 23.4 %attend_back_prev.1 = (f32[8,256,256]{2,1,0:T(8,128)}, bf16[2,7,256,256]{3,2,1,0:T(8,128)(2,1)}) custom-call(s32[8]{0:T(128)} %refs_0_.3, bf16[8,256,256]{2,1,0:T(8,128)(2,1)} %copy-done.20, bf16[7,256,256]{2,1,0:T(8,128)(2,1)} %copy-done.76, bf16[7,256,256]{2,1,0:T(8,128)(2,1)} %copy-done.77, bf16[8,64,256]{2,1,0:T(8,128)(2,1)} %copy-done.44, ...), custom_call_target="tpu_custom_call" | custom-call | flops 8053063680 | bytes 12582912 | tf_op jit(solution)/shard_map/attend_back_prev/pallas_call | solution.py:490
  304.9 24.6 %attend_back_own.1 = (bf16[8,256,256]{2,1,0:T(8,128)(2,1)}, f32[8,256,256]{2,1,0:T(8,128)}, f32[8,256,256]{2,1,0:T(8,128)}) custom-call(s32[8]{0:T(128)} %refs_0_.3, bf16[8,256,256]{2,1,0:T(8,128)(2,1)} %copy-done.20, bf16[8,256,256]{2,1,0:T(8,128)(2,1)} %copy-done.21, bf16[8,256,256]{2,1,0:T(8,128)(2,1)} %copy-done.22, bf16[8,64,256]{2,1,0:T(8,128)(2,1)} %copy-done.44, ...), custom_call_target="tpu_custom_call" | custom-call | flops 1000 | bytes 1000 | tf_op jit(solution)/shard_map/attend_back_own/pallas_call | solution.py:490
  329.5 23.6 %collective-permute-done.37.rk.rv = bf16[2,7,256,256]{3,2,1,0:T(8,128)(2,1)S(1)} collective-permute-done((bf16[2,7,256,256]{3,2,1,0:T(8,128)(2,1)}, bf16[2,7,256,256]{3,2,1,0:T(8,128)(2,1)S(1)}, u32[]{:S(2)}, u32[]{:S(2)}) %collective-permute-start.37) | collective-permute-done | bytes 1835040 | tf_op jit(solution)/shard_map/ppermute | solution.py:31
  358.7 8.0 %project_back.1 = (bf16[8,256,768]{2,1,0:T(8,128)(2,1)S(1)}, bf16[8,64,1024]{2,1,0:T(8,128)(2,1)S(1)}, bf16[8,64,1024]{2,1,0:T(8,128)(2,1)S(1)}, bf16[2,8,64,1024]{3,2,1,0:T(8,128)(2,1)}, f32[8,512]{1,0:T(8,128)S(1)}) custom-call(s32[1]{0:T(128)} %bitcast.row_ref.refs_0_, bf16[8,256,256]{2,1,0:T(8,128)(2,1)S(1)} %copy-done.62, ...), custom_call_target="tpu_custom_call" | custom-call | flops 3221225472 | bytes 14680064 | tf_op jit(solution)/shard_map/project_back/pallas_call | solution.py:989
  382.2 4.7 project_weight.1
  387.0 15.0 %collective-permute-done.42.refs_5_ = bf16[8,8,4096]{2,1,0:T(8,128)(2,1)S(1)} collective-permute-done((bf16[8,8,4096]{2,1,0:T(8,128)(2,1)S(1)}, bf16[8,8,4096]{2,1,0:T(8,128)(2,1)S(1)}, u32[]{:S(2)}, u32[]{:S(2)}) %collective-permute-start.42) | collective-permute-done | bytes 524320 | tf_op jit(solution)/shard_map/ppermute | solution.py:27
  407.6 16.6 %collective-permute-done.43 = bf16[4,64,768]{2,1,0:T(8,128)(2,1)} collective-permute-done((bf16[4,64,768]{2,1,0:T(8,128)(2,1)}, bf16[4,64,768]{2,1,0:T(8,128)(2,1)}, u32[]{:S(2)}, u32[]{:S(2)}) %collective-permute-start.43) | collective-permute-done | bytes 393248 | tf_op jit(solution)/shard_map/ppermute | solution.py:27
  427.8 5.1 collective-permute-done.44
  440.1 4.1 input_back.1
  449.3 5.3 collective-permute-done.51
  471.3 4.0 collective-permute-done.62.a3
  477.7 7.5 %collective-permute-done.67 = bf16[144,1024]{1,0:T(8,128)(2,1)S(1)} collective-permute-done((bf16[144,1024]{1,0:T(8,128)(2,1)S(1)}, bf16[144,1024]{1,0:T(8,128)(2,1)S(1)}, u32[]{:S(2)}, u32[]{:S(2)}) %collective-permute-start.67) | collective-permute-done | bytes 294944 | tf_op jit(solution)/shard_map/ppermute | solution.py:27
  486.6 8.5 %collective-permute-done.65 = bf16[4,16,3072]{2,1,0:T(8,128)(2,1)S(1)} collective-permute-done((bf16[4,16,3072]{2,1,0:T(8,128)(2,1)S(1)}, bf16[4,16,3072]{2,1,0:T(8,128)(2,1)S(1)}, u32[]{:S(2)}, u32[]{:S(2)}) %collective-permute-start.65) | collective-permute-done | bytes 393248 | tf_op jit(solution)/shard_map/ppermute | solution.py:27
  495.3 5.9 %collective-permute-done.63 = bf16[4,16,3584]{2,1,0:T(8,128)(2,1)S(1)} collective-permute-done((bf16[4,16,3584]{2,1,0:T(8,128)(2,1)S(1)}, bf16[4,16,3584]{2,1,0:T(8,128)(2,1)S(1)}, u32[]{:S(2)}, u32[]{:S(2)}) %collective-permute-start.63) | collective-permute-done | bytes 458784 | tf_op jit(solution)/shard_map/ppermute | solution.py:27
  509.0 10.7 %collective-permute-done.66.high = bf16[2,4,16,3072]{3,2,1,0:T(8,128)(2,1)} collective-permute-done((bf16[2,4,16,3072]{3,2,1,0:T(8,128)(2,1)S(1)}, bf16[2,4,16,3072]{3,2,1,0:T(8,128)(2,1)}, u32[]{:S(2)}, u32[]{:S(2)}) %collective-permute-start.66) | collective-permute-done | bytes 786464 | tf_op jit(solution)/shard_map/ppermute | solution.py:27
  519.6 3.8 place.1
  523.9 6.1 %final_sums.1 = (f32[256,6144]{1,0:T(8,128)}, f32[1,1536]{1,0:T(1,128)S(1)}, f32[1,768]{1,0:T(1,128)S(1)}, f32[1,256]{1,0:T(1,128)}, f32[1,1024]{1,0:T(1,128)}, /*index=5*/f32[1,256]{1,0:T(1,128)}) custom-call(s32[1]{0:T(128)} %bitcast.row_ref.refs_0_, bf16[2,4,16,3584]{3,2,1,0:T(8,128)(2,1)S(1)} %pad_maximum_fusion.refs_0_, ...), custom_call_target="tpu_custom_call" | custom-call | flops 805306368 | bytes 10485760 | tf_op jit(solution)/shard_map/final_sums/pallas_call | solution.py:1138
  531.2 9.2 %all-gather.2.cloned.1.call-done.total = bf16[2304,1024]{1,0:T(8,128)(2,1)} async-done(((bf16[144,1024]{1,0:T(8,128)(2,1)}), bf16[2304,1024]{1,0:T(8,128)(2,1)}) %all-gather.2.cloned.1.call-update) | async-done | bytes 4718608 | tf_op jit(solution)/shard_map/all_gather | solution.py:1335
  (371 shorter events, 153.2 us)
Async XLA Ops:
  7.2 454.2 %reduce-scatter.2.cloned.1.call-start = ((), (), s32[]{:S(2)}) async-start(), calls=%async_computation.1 | async-start | bytes 10027008 | tf_op jit(solution)/shard_map/reduce_scatter | solution.py:1288
  7.2 51.9 %collective-permute-start = (bf16[8,64,1024]{2,1,0:T(8,128)(2,1)}, bf16[8,64,1024]{2,1,0:T(8,128)(2,1)}, u32[]{:S(2)}, u32[]{:S(2)}) collective-permute-start(bf16[8,64,1024]{2,1,0:T(8,128)(2,1)} %x.3), channel_id=1, source_target_pairs={{0,2},{1,3},{2,0},{3,1},{4,6},{5,7},{6,4},{7,5},{8,10},{9,11},{10,... | collective-permute-start | bytes 3145736 | tf_op jit(solution)/shard_map/ppermute | solution.py:27
  10.4 48.8 %collective-permute-start.1 = (bf16[7,64,1024]{2,1,0:T(8,128)(2,1)}, bf16[7,64,1024]{2,1,0:T(8,128)(2,1)}, u32[]{:S(2)}, u32[]{:S(2)}) collective-permute-start(bf16[7,64,1024]{2,1,0:T(8,128)(2,1)} %slice.63), channel_id=1, source_target_pairs={{0,4},{1,5},{2,6},{3,7},{4,8},{5,9},{6,10},{7,11},{8,12},{9,13},{1... | collective-permute-start | bytes 2752520 | tf_op jit(solution)/shard_map/ppermute | solution.py:31
  12.6 25.0 %collective-permute-start.5 = (bf16[2,256,768]{2,1,0:T(8,128)(2,1)S(1)}, bf16[2,256,768]{2,1,0:T(8,128)(2,1)S(1)}, u32[]{:S(2)}, u32[]{:S(2)}) collective-permute-start(bf16[2,256,768]{2,1,0:T(8,128)(2,1)S(1)} %get-tuple-element.158), channel_id=1, source_target_pairs={{0,66},{1,67},{2,64},{3,65},{4,70},{5,71},{6,68},{7,69},{8,74},{9,... | collective-permute-start | bytes 2359304 | tf_op jit(solution)/shard_map/ppermute | solution.py:27
  16.4 21.1 %collective-permute-start.4 = (bf16[256,768]{1,0:T(8,128)(2,1)S(1)}, bf16[256,768]{1,0:T(8,128)(2,1)S(1)}, u32[]{:S(2)}, u32[]{:S(2)}) collective-permute-start(bf16[256,768]{1,0:T(8,128)(2,1)S(1)} %get-tuple-element.157), channel_id=1, source_target_pairs={{0,1},{1,0},{2,3},{3,2},{4,5},{5,4},{6,7},{7,6},{8,9},{9,8},{10,11... | collective-permute-start | bytes 1179656 | tf_op jit(solution)/shard_map/ppermute | solution.py:27
  18.0 19.5 %collective-permute-start.3 = (f32[8,7424]{1,0:T(8,128)S(1)}, f32[8,7424]{1,0:T(8,128)S(1)}, u32[]{:S(2)}, u32[]{:S(2)}) collective-permute-start(f32[8,7424]{1,0:T(8,128)S(1)} %add.88), channel_id=1, source_target_pairs={{0,2},{1,3},{2,0},{3,1},{4,6},{5,7},{6,4},{7,5},{8,10},{9,11},{10,... | collective-permute-start | bytes 712712 | tf_op jit(solution)/shard_map/ppermute | solution.py:27
  37.5 22.9 %collective-permute-start.7 = (bf16[8,64,1024]{2,1,0:T(8,128)(2,1)S(1)}, bf16[8,64,1024]{2,1,0:T(8,128)(2,1)S(1)}, u32[]{:S(2)}, u32[]{:S(2)}) collective-permute-start(bf16[8,64,1024]{2,1,0:T(8,128)(2,1)S(1)} %copy-done.3), channel_id=1, source_target_pairs={{0,1},{1,0},{2,3},{3,2},{4,5},{5,4},{6,7},{7,6},{8,9},{9,8},{10,11... | collective-permute-start | bytes 3145736 | tf_op jit(solution)/shard_map/ppermute | solution.py:27
  59.2 28.6 %collective-permute-start.6 = (bf16[7,64,1024]{2,1,0:T(8,128)(2,1)}, bf16[7,64,1024]{2,1,0:T(8,128)(2,1)S(1)}, u32[]{:S(2)}, u32[]{:S(2)}) collective-permute-start(bf16[7,64,1024]{2,1,0:T(8,128)(2,1)} %collective-permute-done.1.refs_1_), channel_id=1, source_target_pairs={{0,2},{1,3},{2,0},{3,1},{4,6},{5,7},{6,4},{7,5},{8,10},{9,11},{10,... | collective-permute-start | bytes 2752520 | tf_op jit(solution)/shard_map/ppermute | solution.py:27
  60.4 27.3 %collective-permute-start.10 = (f32[8,2048]{1,0:T(8,128)S(1)}, f32[8,2048]{1,0:T(8,128)S(1)}, u32[]{:S(2)}, u32[]{:S(2)}) collective-permute-start(f32[8,2048]{1,0:T(8,128)S(1)} %slice.66), channel_id=1, source_target_pairs={{0,4},{1,5},{2,6},{3,7},{4,8},{5,9},{6,10},{7,11},{8,12},{9,13},{1... | collective-permute-start | bytes 196616 | tf_op jit(solution)/shard_map/ppermute | solution.py:31
  60.5 72.6 %collective-permute-start.18 = (bf16[256,4096]{1,0:T(8,128)(2,1)}, bf16[256,4096]{1,0:T(8,128)(2,1)}, u32[]{:S(2)}, u32[]{:S(2)}) collective-permute-start(bf16[256,4096]{1,0:T(8,128)(2,1)} %u0.1), channel_id=1, source_target_pairs={{0,66},{1,67},{2,64},{3,65},{4,70},{5,71},{6,68},{7,69},{8,74},{9,... | collective-permute-start | bytes 6291464 | tf_op jit(solution)/shard_map/ppermute | solution.py:27
  87.8 46.7 %collective-permute-start.19 = (bf16[1024,1024]{1,0:T(8,128)(2,1)}, bf16[1024,1024]{1,0:T(8,128)(2,1)}, u32[]{:S(2)}, u32[]{:S(2)}) collective-permute-start(bf16[1024,1024]{1,0:T(8,128)(2,1)} %d0.3), channel_id=1, source_target_pairs={{0,2},{1,3},{2,0},{3,1},{4,6},{5,7},{6,4},{7,5},{8,10},{9,11},{10,... | collective-permute-start | bytes 6291464 | tf_op jit(solution)/shard_map/ppermute | solution.py:27
  89.2 43.7 %collective-permute-start.17 = (bf16[256,1024]{1,0:T(8,128)(2,1)S(1)}, bf16[256,1024]{1,0:T(8,128)(2,1)S(1)}, u32[]{:S(2)}, u32[]{:S(2)}) collective-permute-start(bf16[256,1024]{1,0:T(8,128)(2,1)S(1)} %copy-done.15), channel_id=1, source_target_pairs={{0,66},{1,67},{2,64},{3,65},{4,70},{5,71},{6,68},{7,69},{8,74},{9,... | collective-permute-start | bytes 1572872 | tf_op jit(solution)/shard_map/ppermute | solution.py:27
  92.6 42.7 %collective-permute-start.16 = (bf16[256,1024]{1,0:T(8,128)(2,1)S(1)}, bf16[256,1024]{1,0:T(8,128)(2,1)S(1)}, u32[]{:S(2)}, u32[]{:S(2)}) collective-permute-start(bf16[256,1024]{1,0:T(8,128)(2,1)S(1)} %copy-done.15), channel_id=1, source_target_pairs={{0,1},{1,0},{2,3},{3,2},{4,5},{5,4},{6,7},{7,6},{8,9},{9,8},{10,11... | collective-permute-start | bytes 1572872 | tf_op jit(solution)/shard_map/ppermute | solution.py:27
  92.8 69.1 %collective-permute-start.21 = (bf16[256,4096]{1,0:T(8,128)(2,1)}, bf16[256,4096]{1,0:T(8,128)(2,1)}, u32[]{:S(2)}, u32[]{:S(2)}) collective-permute-start(bf16[256,4096]{1,0:T(8,128)(2,1)} %u0.1), channel_id=1, source_target_pairs={{0,1},{1,0},{2,3},{3,2},{4,5},{5,4},{6,7},{7,6},{8,9},{9,8},{10,11... | collective-permute-start | bytes 6291464 | tf_op jit(solution)/shard_map/ppermute | solution.py:27
  132.9 29.0 %collective-permute-start.23 = (bf16[1024,1024]{1,0:T(8,128)(2,1)}, bf16[1024,1024]{1,0:T(8,128)(2,1)S(1)}, u32[]{:S(2)}, u32[]{:S(2)}) collective-permute-start(bf16[1024,1024]{1,0:T(8,128)(2,1)} %d0.3), channel_id=1, source_target_pairs={{0,1},{1,0},{2,3},{3,2},{4,5},{5,4},{6,7},{7,6},{8,9},{9,8},{10,11... | collective-permute-start | bytes 6291464 | tf_op jit(solution)/shard_map/ppermute | solution.py:27
  134.5 27.4 %collective-permute-start.22 = (bf16[256,4096]{1,0:T(8,128)(2,1)}, bf16[256,4096]{1,0:T(8,128)(2,1)S(1)}, u32[]{:S(2)}, u32[]{:S(2)}) collective-permute-start(bf16[256,4096]{1,0:T(8,128)(2,1)} %collective-permute-done.18.u2), channel_id=1, source_target_pairs={{0,1},{1,0},{2,3},{3,2},{4,5},{5,4},{6,7},{7,6},{8,9},{9,8},{10,11... | collective-permute-start | bytes 6291464 | tf_op jit(solution)/shard_map/ppermute | solution.py:27
  134.8 27.1 %collective-permute-start.24 = (bf16[1024,1024]{1,0:T(8,128)(2,1)}, bf16[1024,1024]{1,0:T(8,128)(2,1)S(1)}, u32[]{:S(2)}, u32[]{:S(2)}) collective-permute-start(bf16[1024,1024]{1,0:T(8,128)(2,1)} %collective-permute-done.19.d2), channel_id=1, source_target_pairs={{0,1},{1,0},{2,3},{3,2},{4,5},{5,4},{6,7},{7,6},{8,9},{9,8},{10,11... | collective-permute-start | bytes 6291464 | tf_op jit(solution)/shard_map/ppermute | solution.py:27
  206.3 19.2 %collective-permute-start.27 = (bf16[2,8,64,256]{3,2,1,0:T(8,128)(2,1)}, bf16[2,8,64,256]{3,2,1,0:T(8,128)(2,1)S(1)}, u32[]{:S(2)}, u32[]{:S(2)}) collective-permute-start(bf16[2,8,64,256]{3,2,1,0:T(8,128)(2,1)} %copy-done.63), channel_id=1, source_target_pairs={{0,2},{1,3},{2,0},{3,1},{4,6},{5,7},{6,4},{7,5},{8,10},{9,11},{10,... | collective-permute-start | bytes 1572872 | tf_op jit(solution)/shard_map/ppermute | solution.py:27
  219.5 37.6 %collective-permute-start.30 = (bf16[2,4,256,1024]{3,2,1,0:T(8,128)(2,1)}, bf16[2,4,256,1024]{3,2,1,0:T(8,128)(2,1)}, u32[]{:S(2)}, u32[]{:S(2)}) collective-permute-start(bf16[2,4,256,1024]{3,2,1,0:T(8,128)(2,1)} %get-tuple-element.209), channel_id=1, source_target_pairs={{0,1},{1,0},{2,3},{3,2},{4,5},{5,4},{6,7},{7,6},{8,9},{9,8},{10,11... | collective-permute-start | bytes 12582920 | tf_op jit(solution)/shard_map/ppermute | solution.py:27
  259.4 19.1 %collective-permute-start.36 = (bf16[2,8,4096]{2,1,0:T(8,128)(2,1)S(1)}, bf16[2,8,4096]{2,1,0:T(8,128)(2,1)S(1)}, u32[]{:S(2)}, u32[]{:S(2)}) collective-permute-start(bf16[2,8,4096]{2,1,0:T(8,128)(2,1)S(1)} %pad_maximum_fusion.2), channel_id=1, source_target_pairs={{0,48},{1,49},{2,50},{3,51},{4,52},{5,53},{6,54},{7,55},{8,56},{9,... | collective-permute-start | bytes 393224 | tf_op jit(solution)/shard_map/ppermute | solution.py:27
  259.5 19.1 %collective-permute-start.35 = (bf16[2,8,4096]{2,1,0:T(8,128)(2,1)S(1)}, bf16[2,8,4096]{2,1,0:T(8,128)(2,1)S(1)}, u32[]{:S(2)}, u32[]{:S(2)}) collective-permute-start(bf16[2,8,4096]{2,1,0:T(8,128)(2,1)S(1)} %pad_maximum_fusion.2), channel_id=1, source_target_pairs={{0,32},{1,33},{2,34},{3,35},{4,36},{5,37},{6,38},{7,39},{8,40},{9,... | collective-permute-start | bytes 393224 | tf_op jit(solution)/shard_map/ppermute | solution.py:27
  279.3 261.1 %all-gather.2.cloned.1.call-start = ((), (), s32[]{:S(2)}) async-start(), calls=%async_computation.2 | async-start | bytes 5013504 | tf_op jit(solution)/shard_map/all_gather | solution.py:1335
  302.8 50.3 %collective-permute-start.37 = (bf16[2,7,256,256]{3,2,1,0:T(8,128)(2,1)}, bf16[2,7,256,256]{3,2,1,0:T(8,128)(2,1)S(1)}, u32[]{:S(2)}, u32[]{:S(2)}) collective-permute-start(bf16[2,7,256,256]{3,2,1,0:T(8,128)(2,1)} %get-tuple-element.234), channel_id=1, source_target_pairs={{0,124},{1,125},{2,126},{3,127},{4,0},{5,1},{6,2},{7,3},{8,4},{9,5... | collective-permute-start | bytes 5505032 | tf_op jit(solution)/shard_map/ppermute | solution.py:31
  373.6 28.4 %collective-permute-start.42 = (bf16[8,8,4096]{2,1,0:T(8,128)(2,1)S(1)}, bf16[8,8,4096]{2,1,0:T(8,128)(2,1)S(1)}, u32[]{:S(2)}, u32[]{:S(2)}) collective-permute-start(bf16[8,8,4096]{2,1,0:T(8,128)(2,1)S(1)} %constant_dynamic-update-slice_fusion.refs_2_), channel_id=1, source_target_pairs={{0,12},{1,13},{2,14},{3,15},{4,8},{5,9},{6,10},{7,11},{8,4},{9,5},... | collective-permute-start | bytes 1572872 | tf_op jit(solution)/shard_map/ppermute | solution.py:27
  373.7 28.4 %collective-permute-start.41 = (bf16[8,8,4096]{2,1,0:T(8,128)(2,1)S(1)}, bf16[8,8,4096]{2,1,0:T(8,128)(2,1)S(1)}, u32[]{:S(2)}, u32[]{:S(2)}) collective-permute-start(bf16[8,8,4096]{2,1,0:T(8,128)(2,1)S(1)} %constant_dynamic-update-slice_fusion.refs_2_), channel_id=1, source_target_pairs={{0,8},{1,9},{2,10},{3,11},{4,12},{5,13},{6,14},{7,15},{8,0},{9,1},... | collective-permute-start | bytes 1572872 | tf_op jit(solution)/shard_map/ppermute | solution.py:27
  375.4 27.0 %collective-permute-start.40 = (bf16[8,8,4096]{2,1,0:T(8,128)(2,1)S(1)}, bf16[8,8,4096]{2,1,0:T(8,128)(2,1)S(1)}, u32[]{:S(2)}, u32[]{:S(2)}) collective-permute-start(bf16[8,8,4096]{2,1,0:T(8,128)(2,1)S(1)} %constant_dynamic-update-slice_fusion.refs_2_), channel_id=1, source_target_pairs={{0,4},{1,5},{2,6},{3,7},{4,0},{5,1},{6,2},{7,3},{8,12},{9,13},{10,... | collective-permute-start | bytes 1572872 | tf_op jit(solution)/shard_map/ppermute | solution.py:27
  380.3 54.1 %collective-permute-start.39 = (bf16[8,64,1024]{2,1,0:T(8,128)(2,1)}, bf16[8,64,1024]{2,1,0:T(8,128)(2,1)}, u32[]{:S(2)}, u32[]{:S(2)}) collective-permute-start(bf16[8,64,1024]{2,1,0:T(8,128)(2,1)} %fusion), channel_id=1, source_target_pairs={{0,2},{1,3},{2,0},{3,1},{4,6},{5,7},{6,4},{7,5},{8,10},{9,11},{10,... | collective-permute-start | bytes 3145736 | tf_op jit(solution)/shard_map/ppermute | solution.py:27
  403.5 20.7 %collective-permute-start.43 = (bf16[4,64,768]{2,1,0:T(8,128)(2,1)}, bf16[4,64,768]{2,1,0:T(8,128)(2,1)}, u32[]{:S(2)}, u32[]{:S(2)}) collective-permute-start(bf16[4,64,768]{2,1,0:T(8,128)(2,1)} %get-tuple-element.293), channel_id=1, source_target_pairs={{0,4},{1,5},{2,6},{3,7},{4,0},{5,1},{6,2},{7,3},{8,12},{9,13},{10,... | collective-permute-start | bytes 1179656 | tf_op jit(solution)/shard_map/ppermute | solution.py:27
  403.7 24.1 %collective-permute-start.45 = (bf16[4,64,768]{2,1,0:T(8,128)(2,1)}, bf16[4,64,768]{2,1,0:T(8,128)(2,1)}, u32[]{:S(2)}, u32[]{:S(2)}) collective-permute-start(bf16[4,64,768]{2,1,0:T(8,128)(2,1)} %get-tuple-element.294), channel_id=1, source_target_pairs={{0,12},{1,13},{2,14},{3,15},{4,8},{5,9},{6,10},{7,11},{8,4},{9,5},... | collective-permute-start | bytes 1179656 | tf_op jit(solution)/shard_map/ppermute | solution.py:27
  405.2 27.7 %collective-permute-start.44 = (bf16[4,64,768]{2,1,0:T(8,128)(2,1)}, bf16[4,64,768]{2,1,0:T(8,128)(2,1)}, u32[]{:S(2)}, u32[]{:S(2)}) collective-permute-start(bf16[4,64,768]{2,1,0:T(8,128)(2,1)} %get-tuple-element.295), channel_id=1, source_target_pairs={{0,8},{1,9},{2,10},{3,11},{4,12},{5,13},{6,14},{7,15},{8,0},{9,1},... | collective-permute-start | bytes 1179656 | tf_op jit(solution)/shard_map/ppermute | solution.py:27
  495.2 24.4 %collective-permute-start.66 = (bf16[2,4,16,3072]{3,2,1,0:T(8,128)(2,1)S(1)}, bf16[2,4,16,3072]{3,2,1,0:T(8,128)(2,1)}, u32[]{:S(2)}, u32[]{:S(2)}) collective-permute-start(bf16[2,4,16,3072]{3,2,1,0:T(8,128)(2,1)S(1)} %pad_maximum_fusion.1.low), channel_id=1, source_target_pairs={{0,12},{1,13},{2,14},{3,15},{4,8},{5,9},{6,10},{7,11},{8,4},{9,5},... | collective-permute-start | bytes 2359304 | tf_op jit(solution)/shard_map/ppermute | solution.py:27
  501.3 22.5 %collective-permute-start.64 = (bf16[2,4,16,3584]{3,2,1,0:T(8,128)(2,1)S(1)}, bf16[2,4,16,3584]{3,2,1,0:T(8,128)(2,1)S(1)}, u32[]{:S(2)}, u32[]{:S(2)}) collective-permute-start(bf16[2,4,16,3584]{3,2,1,0:T(8,128)(2,1)S(1)} %pad_maximum_fusion.refs_0_), channel_id=1, source_target_pairs={{0,4},{1,5},{2,6},{3,7},{4,0},{5,1},{6,2},{7,3},{8,12},{9,13},{10,... | collective-permute-start | bytes 2752520 | tf_op jit(solution)/shard_map/ppermute | solution.py:27
  (133 other events, 2000.6 us)
Sparse Core Ops, SparseCore 0:
  278.7 156.0 reduce-scatter.1
  486.2 54.2 all-gather.1
